TPU v7x, 128 devices: a whole 4x4x4 slice. The times are simulated.
128 devices in a mesh: layer: 16 (over y, x), ex: 8 (over z, core).
Axes of the slice: x: 4, y: 4, z: 4, core: 2. Of those that a mesh axis runs over, the one named last changes fastest.
Arguments:
- partials: bfloat16 [16, 8192, 2048], P('layer', None, 'ex'), may hold values from -6 to 6
- scales: float32 [16, 128, 2048], P('layer', None, 'ex'), may hold values from 0.01 to 3.6, as said below
- pairs: int32 [80, 3], replicated, may hold values from 0 to 15, as said below
Outputs:
- gram: float32 [2048, 1280], P('ex')
Inputs may be any that keep to these rules, and one draw needn't show every extreme that they name: Positive scales. `pairs`: each row is (row block, column block, computing index along ex, from 0 to 7). Block x is held by ex index x // 2. Rows s * 8 to (s + 1) * 8 - 1 name every block exactly once, and no row names one block twice. At most 20 rows name one computing index, and one index has exactly 20.
All inputs are finite; a program needn't handle non-finite values.
Results may differ from a plain program's by a relative error of at most 0.0041.
Values may be sent and summed in bfloat16 or wider, within the bound.
No kernel may reach another device: no remote copies, remote signals or barrier semaphores. Data moves between devices by JAX's collectives and lax.ppermute only.
A program may use at most 64 MiB of HBM per device.

v0:
```python
import math

import jax
import jax.numpy as jnp
from jax import lax
from jax.sharding import PartitionSpec as P

K = 8192
TB = 128
QB = 64
SLOTS = 10
BLK_DEV = 2
MAXP = 20


def on_device(partials, scales, pairs):
    slice_rows = partials.shape[1] // lax.axis_size("layer")
    local_cols = partials.shape[2]
    n_ex = lax.axis_size("ex")
    piece_vals = partials[0]
    scale_rows = scales[0]
    dequant = (
        piece_vals.astype(jnp.float32).reshape(
            slice_rows * lax.axis_size("layer") // QB, QB, local_cols
        )
        * scale_rows[:, None, :]
    )
    summed = lax.psum_scatter(
        dequant.reshape(slice_rows * lax.axis_size("layer"), local_cols),
        "layer",
        scatter_dimension=0,
        tiled=True,
    )
    squares = lax.psum(jnp.sum(summed * summed, axis=0), "layer")
    unit_rows = (summed * lax.rsqrt(squares / K + 1e-06)).astype(jnp.bfloat16)
    everyone = lax.all_gather(unit_rows, "ex", axis=1, tiled=True)
    block_count = everyone.shape[1] // TB
    by_block = everyone.reshape(slice_rows, block_count, TB)
    owner_index = lax.axis_index("ex")
    npairs_all = pairs.shape[0]
    computer = pairs[:, 2]
    one_hot = (computer[:, None] == jnp.arange(n_ex, dtype=jnp.int32)[None, :]).astype(jnp.int32)
    positions = jnp.sum((jnp.cumsum(one_hot, axis=0) - 1) * one_hot, axis=1)
    pair_ids = jnp.arange(npairs_all, dtype=jnp.int32)
    is_local = computer == owner_index
    picker = (
        is_local[None, :] & (positions[None, :] == jnp.arange(MAXP, dtype=jnp.int32)[:, None])
    ).astype(jnp.int32)
    chosen = jnp.sum(picker * pair_ids[None, :], axis=1)
    filled = jnp.sum(picker, axis=1).astype(jnp.float32)
    row_block = pairs[chosen, 0]
    col_block = pairs[chosen, 1]
    left_rows = jnp.take(by_block, row_block, axis=1)
    right_rows = jnp.take(by_block, col_block, axis=1)
    tile_sums = jnp.einsum(
        "kmr,kmc->mrc", left_rows, right_rows, preferred_element_type=jnp.float32
    )
    tile_sums = tile_sums * (filled[:, None, None] / math.sqrt(K))
    per_group = block_count // 2
    own_blocks = owner_index * BLK_DEV + jnp.arange(BLK_DEV, dtype=jnp.int32)
    grouped = pairs.reshape(SLOTS, per_group, 3)
    group_ids = jnp.arange(SLOTS * per_group, dtype=jnp.int32).reshape(SLOTS, per_group)
    hit_row = (grouped[None, :, :, 0] == own_blocks[:, None, None]).astype(jnp.int32)
    hit_col = (grouped[None, :, :, 1] == own_blocks[:, None, None]).astype(jnp.int32)
    pair_of = jnp.sum((hit_row + hit_col) * group_ids[None, :, :], axis=2)
    as_col = jnp.sum(hit_col, axis=2)
    source_slot = computer[pair_of] * MAXP + positions[pair_of]
    all_tiles = lax.all_gather(tile_sums, "ex", axis=0, tiled=True)
    picked = all_tiles[source_slot]
    picked = jnp.where(as_col[:, :, None, None] == 1, jnp.swapaxes(picked, 2, 3), picked)
    assembled = jnp.transpose(picked, (0, 2, 1, 3)).reshape(local_cols, SLOTS * TB)
    return lax.psum(assembled, "layer")


def solution(mesh):
    in_specs = (P("layer", None, "ex"), P("layer", None, "ex"), P())
    out_specs = P("ex", None)
    return jax.shard_map(
        on_device, mesh=mesh, in_specs=in_specs, out_specs=out_specs, check_vma=False
    )
```

profile of v0, /device:TPU:0, one launch (start us, length us, event | category | flops | bytes accessed | tf_op | source)
XLA Modules:
  0.0 347.6 jit_solution(5017042965815136866)
XLA Ops:
  6.5 0.0 reduce-scatter.2.cloned.1.call-start
  6.5 6.0 %convert_multiply_fusion = f32[8192,256]{1,0:T(8,128)} fusion(bf16[1,8192,256]{2,1,0:T(8,128)(2,1)} %param.5, f32[128,256]{1,0:T(8,128)} %bitcast.58), kind=kLoop, calls=%fused_computation.7 | loop fusion | flops 4194304 | bytes 12713984 | tf_op jit(solution)/shard_map/mul | solution.py:23
  12.5 0.0 copy-start
  12.5 0.0 reduce-scatter.2.cloned.1.call-update
  12.5 0.0 all-gather.3.cloned.1.call-start
  12.6 87.7 %reduce-scatter.2.cloned.1.call-done = f32[512,256]{1,0:T(8,128)} async-done(((f32[8192,256]{1,0:T(8,128)}), f32[512,256]{1,0:T(8,128)}) %reduce-scatter.2.cloned.1.call-update) | async-done | bytes 524304 | tf_op jit(solution)/shard_map/reduce_scatter | solution.py:28
  100.2 1.1 multiply_reduce_fusion
  101.4 38.2 %psum.14 = f32[256]{0:T(256)S(1)} all-reduce(f32[256]{0:T(256)S(1)} %multiply_reduce_fusion), channel_id=1, replica_groups=mesh['layer'=16,'ex'=8] {'layer'}, use_global_device_ids=true, to_apply=%region_3.0 | all-reduce | flops 256 | bytes 2048 | tf_op jit(solution)/shard_map/psum | solution.py:34
  139.6 1.8 multiply_convert_fusion
  141.4 0.0 all-gather.3.cloned.1.call-update
  141.4 0.0 all-gather.5.cloned.1.call-start
  141.4 0.0 copy-done
  141.5 0.1 fusion.13
  141.5 0.1 reduce_window_sum.11
  141.7 0.2 select_reduce_fusion
  141.8 0.1 convert_reduce_fusion
  142.0 0.9 gather_fusion
  142.8 0.9 gather_fusion.1
  143.8 21.7 %all-gather.3.cloned.1.call-done = bf16[512,2048]{1,0:T(8,128)(2,1)} async-done(((bf16[512,256]{1,0:T(8,128)(2,1)}), bf16[512,2048]{1,0:T(8,128)(2,1)}) %all-gather.3.cloned.1.call-update) | async-done | bytes 2097168 | tf_op jit(solution)/shard_map/all_gather | solution.py:36
  165.4 3.9 %copy.52 = bf16[512,2048]{0,1:T(8,128)(2,1)} copy(bf16[512,2048]{1,0:T(8,128)(2,1)} %all-gather.3.cloned.1.call-done) | data formatting | bytes 4194304 | tf_op jit(solution)/shard_map/all_gather | solution.py:36
  169.3 3.0 copy.53
  172.4 2.6 gather_fusion.5
  174.9 2.5 gather_fusion.6
  177.5 4.7 %fusion.7 = f32[20,128,128]{2,1,0:T(8,128)} fusion(bf16[20,512,128]{2,1,0:T(8,128)(2,1)} %gather_fusion.6, pred[20]{0:T(512)(128)(4,1)S(1)} %get-tuple-element.14, bf16[20,512,128]{2,1,0:T(8,128)(2,1)} %gather_fusion.5, pred[20]{0:T(512)(128)(4,1)S(1)} %get-tuple-element.15, f32[20]{0:T(128)S(1)} %convert_multiply_fusion.1), kind=kOutput, calls=%fused_computation.15 | convolution fusion | flops 338493440 | bytes 6553720 | tf_op jit(solution)/shard_map/kmr,kmc->mrc/dot_general | solution.py:55
  182.2 0.0 all-gather.5.cloned.1.call-update
  182.2 0.0 all-reduce.4.cloned.1.call-start
  182.3 0.1 reshape.106
  182.4 0.1 copy.50
  182.5 0.1 copy.56
  182.5 0.1 convert_reduce_fusion.1
  182.6 0.1 reshape.140
  182.7 0.7 gather_fusion.3
  183.4 0.7 gather_fusion.2
  184.1 0.1 add.92
  184.2 0.1 reshape.156
  184.3 0.1 copy.51
  184.5 57.5 %all-gather.5.cloned.1.call-done = f32[160,128,128]{2,1,0:T(8,128)} async-done(((f32[20,128,128]{2,1,0:T(8,128)}), f32[160,128,128]{2,1,0:T(8,128)}) %all-gather.5.cloned.1.call-update) | async-done | bytes 10485776 | tf_op jit(solution)/shard_map/all_gather | solution.py:68
  242.0 4.6 %gather_fusion.4 = f32[20,128,128]{2,1,0:T(8,128)S(1)} fusion(f32[160,128,128]{2,1,0:T(8,128)} %all-gather.5.cloned.1.call-done, s32[1024]{0:T(1024)S(1)} %pad_clamp_fusion), kind=kCustom, calls=%fused_computation.6 | custom fusion | bytes 2621520 | tf_op jit(solution)/shard_map/gather | solution.py:69
  246.6 1.4 copy.58
  247.9 1.4 bitcast_select_fusion
  249.3 1.1 copy.64
  250.5 0.0 all-reduce.4.cloned.1.call-update
  250.5 87.8 %all-reduce.4.cloned.1.call-done = f32[256,1280]{0,1:T(8,128)} async-done(((f32[256,1280]{0,1:T(8,128)}), f32[256,1280]{0,1:T(8,128)}) %all-reduce.4.cloned.1.call-update) | async-done | bytes 1310736 | tf_op jit(solution)/shard_map/psum | solution.py:72
  338.3 2.8 copy.59
  (19 shorter events, 0.1 us)
Async XLA Ops:
  6.5 93.7 %reduce-scatter.2.cloned.1.call-start = ((), (), s32[]{:S(2)}) async-start(), calls=%async_computation.1 | async-start | bytes 8912896 | tf_op jit(solution)/shard_map/reduce_scatter | solution.py:28
  12.5 128.9 %copy-start = (s32[80,3]{0,1:T(4,128)S(1)}, s32[80,3]{0,1:T(4,128)}, u32[]{:S(2)}) copy-start(s32[80,3]{0,1:T(4,128)} %param.7) | copy-start | bytes 2884
  12.5 152.9 %all-gather.3.cloned.1.call-start = ((), (), s32[]{:S(2)}) async-start(), calls=%async_computation.2 | async-start | bytes 2359296 | tf_op jit(solution)/shard_map/all_gather | solution.py:36
  141.4 100.6 %all-gather.5.cloned.1.call-start = ((), (), s32[]{:S(2)}) async-start(), calls=%async_computation.3 | async-start | bytes 11796480 | tf_op jit(solution)/shard_map/all_gather | solution.py:68
  182.2 156.1 %all-reduce.4.cloned.1.call-start = ((), (), s32[]{:S(2)}) async-start(), calls=%async_computation.4 | async-start | bytes 2621440 | tf_op jit(solution)/shard_map/psum | solution.py:72
Sparse Core Ops, SparseCore 0:
  12.6 87.5 reduce-scatter.1
  141.5 23.8 all-gather.2
  182.4 59.5 all-gather.4
  250.6 87.6 all-reduce.3
where the time goes:
time: 348 us
  waiting for transfers between devices  255 us (73%)
  blocking collectives  38.2 us (11%)
  local copies, waits for them, and re-layouts  25.7 us (7%)
  between operations  13.3 us (4%)
  other arithmetic  10.9 us (3%)
  matrix products  4.73 us (1%)
    psum x1, waiting for transfers between devices, on_device(): return lax.psum(assembled, 'layer')  87.8 us
    reduce_scatter x1, waiting for transfers between devices, on_device(): lax.psum_scatter(dequant.reshape(slice_rows * lax.axis_size('layer'), loc...  87.7 us
    all_gather x1, waiting for transfers between devices, on_device(): all_tiles = lax.all_gather(tile_sums, 'ex', axis=0, tiled=True)  57.5 us
    psum x1, blocking collectives, on_device(): squares = lax.psum(jnp.sum(summed * summed, axis=0), 'layer')  38.2 us
    all_gather x1, waiting for transfers between devices, on_device(): everyone = lax.all_gather(unit_rows, 'ex', axis=1, tiled=True)  21.7 us
  transfers between devices with their start and end apart: 4, of which 4 were waited for; matrix products, arithmetic and copies ran while one was open for 1% of the time, Pallas kernels for 0%

commit v1 on v0

v1 whole, which is shorter than its diff:
```python
import math

import jax
import jax.numpy as jnp
from jax import lax
from jax.experimental import pallas as pl
from jax.experimental.pallas import tpu as pltpu
from jax.sharding import PartitionSpec as P

K = 8192
TB = 128
QB = 64
SLOTS = 10
LAYERS = 16
N_EX = 8
BLK_DEV = 2
COLS = BLK_DEV * TB
SLICE = K // LAYERS
SCALES = SLICE // QB
ROWS = COLS // LAYERS
WIDE = SLOTS * TB
AUX = 2 * TB
OWN = SLOTS
BF, F32 = jnp.bfloat16, jnp.float32


def sum_layers(piece_ref, scale_ref, high_ref, low_ref):
    row = pl.program_id(0)
    total = None
    for layer in range(LAYERS):
        term = piece_ref[layer].astype(F32) * scale_ref[layer, pl.ds(row, 1), :]
        total = term if total is None else total + term
    high = total.astype(BF)
    high_ref[...] = high
    low_ref[...] = (total - high.astype(F32)).astype(BF)


def summed_slice(pieces, scales):
    block = pl.BlockSpec((QB, COLS), lambda i: (i, 0))
    return pl.pallas_call(
        sum_layers,
        grid=(SCALES,),
        in_specs=[
            pl.BlockSpec((LAYERS, QB, COLS), lambda i: (0, i, 0)),
            pl.BlockSpec((LAYERS, SCALES, COLS), lambda i: (0, 0, 0)),
        ],
        out_specs=[block, block],
        out_shape=[jax.ShapeDtypeStruct((SLICE, COLS), BF)] * 2,
        cost_estimate=pl.CostEstimate(
            flops=2 * LAYERS * SLICE * COLS,
            bytes_accessed=2 * LAYERS * SLICE * COLS,
            transcendentals=0,
        ),
    )(pieces, scales)


def tiles(where_ref, high_ref, low_ref, *refs):
    parts, (out_ref, dots, squares) = refs[:7], refs[7:]
    contract = (((0,), (0,)), ((), ()))
    high, low = high_ref[...], low_ref[...]
    for n, ref in enumerate((high_ref, *parts)):
        part = ref[...]
        dot = lax.dot_general(high, part, contract, preferred_element_type=F32)
        dot += lax.dot_general(low, part, contract, preferred_element_type=F32)
        wide = part.astype(F32)
        square = jnp.sum(wide * wide, axis=0, keepdims=True)
        for half in range(BLK_DEV):
            cut = slice(half * TB, (half + 1) * TB)
            dots[n * BLK_DEV + half] = dot[:, cut]
            squares[n * BLK_DEV + half] = jnp.broadcast_to(square[:, cut], (8, TB))
    exact = high.astype(F32) + low.astype(F32)
    own = jnp.sum(exact * exact, axis=0, keepdims=True)
    for b in range(BLK_DEV):
        rows = slice(b * TB, (b + 1) * TB)
        aux = []
        for s in range(SLOTS):
            at = where_ref[b * SLOTS + s]
            out_ref[rows, s * TB : (s + 1) * TB] = dots[at, rows, :].astype(BF)
            aux.append(squares[at][:1])
        aux.append(own[:, rows])
        aux.append(jnp.zeros((ROWS - SLOTS - 1, TB), F32))
        aux = jnp.concatenate(aux, axis=0)
        first = aux.astype(BF)
        second = (aux - first.astype(F32)).astype(BF)
        both = jnp.concatenate([first, second], axis=1)
        for i in range(TB // ROWS):
            out_ref[b * TB + i * ROWS : b * TB + (i + 1) * ROWS, WIDE:] = both


def partial_tiles(where, high, low, parts):
    return pl.pallas_call(
        tiles,
        in_specs=[pl.BlockSpec(memory_space=pltpu.SMEM)]
        + [pl.BlockSpec(memory_space=pltpu.VMEM)] * 9,
        out_specs=pl.BlockSpec(memory_space=pltpu.VMEM),
        out_shape=jax.ShapeDtypeStruct((COLS, WIDE + AUX), BF),
        scratch_shapes=[
            pltpu.VMEM((N_EX * BLK_DEV, COLS, TB), F32),
            pltpu.VMEM((N_EX * BLK_DEV, 8, TB), F32),
        ],
        compiler_params=pltpu.CompilerParams(vmem_limit_bytes=32 * 2**20),
        cost_estimate=pl.CostEstimate(
            flops=4 * SLICE * COLS * COLS * N_EX,
            bytes_accessed=2 * SLICE * COLS * 9 + 2 * COLS * (WIDE + AUX),
            transcendentals=0,
        ),
    )(where, high, low, *parts)


def finish(me_ref, sums_ref, out_ref):
    total = sums_ref[0].astype(F32)
    for layer in range(1, LAYERS):
        total += sums_ref[layer].astype(F32)
    squares = total[:, WIDE : WIDE + TB] + total[:, WIDE + TB :]
    inverse = lax.rsqrt(squares / K + 1e-06)
    first = lax.rem(me_ref[0], TB // ROWS) * ROWS
    lane = lax.broadcasted_iota(jnp.int32, (ROWS, TB), 1)
    row = lax.broadcasted_iota(jnp.int32, (ROWS, TB), 0)
    own = jnp.broadcast_to(inverse[OWN : OWN + 1], (ROWS, TB))
    left = jnp.sum(jnp.where(lane == first + row, own, 0.0), axis=1, keepdims=True)
    left = left / math.sqrt(K)
    for s in range(SLOTS):
        cut = slice(s * TB, (s + 1) * TB)
        value = (total[:, cut] * left * inverse[s : s + 1]).astype(BF)
        for layer in range(LAYERS):
            out_ref[layer, :, cut] = value


def finished_rows(me, sums):
    return pl.pallas_call(
        finish,
        in_specs=[
            pl.BlockSpec(memory_space=pltpu.SMEM),
            pl.BlockSpec(memory_space=pltpu.VMEM),
        ],
        out_specs=pl.BlockSpec(memory_space=pltpu.VMEM),
        out_shape=jax.ShapeDtypeStruct((LAYERS, ROWS, WIDE), BF),
        compiler_params=pltpu.CompilerParams(vmem_limit_bytes=32 * 2**20),
        cost_estimate=pl.CostEstimate(
            flops=LAYERS * ROWS * WIDE,
            bytes_accessed=4 * LAYERS * ROWS * WIDE,
            transcendentals=ROWS * TB,
        ),
    )(me, sums)


def partner_places(pairs, ex):
    own = ex * BLK_DEV + jnp.arange(BLK_DEV, dtype=jnp.int32)[:, None, None]
    grouped = pairs.reshape(1, SLOTS, -1, 3)
    row, col = grouped[..., 0], grouped[..., 1]
    partner = jnp.sum(
        jnp.where(row == own, col, 0) + jnp.where(col == own, row, 0), axis=2
    )
    holder, half = partner // BLK_DEV, partner % BLK_DEV
    turn = (ex // 2 - holder // 2) % (N_EX // 2)
    other = (holder % 2) != (ex % 2)
    part = turn + jnp.where(other, N_EX // 2, 0)
    return (part * BLK_DEV + half).reshape(-1).astype(jnp.int32)


def on_device(partials, scales, pairs):
    ex = lax.axis_index("ex")
    here = lax.axis_index("layer").astype(jnp.int32).reshape(1)
    where = partner_places(pairs, ex)
    across = lambda a: lax.all_to_all(a, "layer", 0, 0, tiled=True)
    slice_scales = across(scales.reshape(LAYERS, SCALES, COLS))
    pieces = across(partials.reshape(LAYERS, SLICE, COLS))
    high, low = summed_slice(pieces, slice_scales)

    around = lambda a, d: lax.ppermute(
        a, "ex", [(e, (e + 2 * d) % N_EX) for e in range(N_EX)]
    )
    swap = lambda a: lax.ppermute(a, "ex", [(e, e ^ 1) for e in range(N_EX)])
    same = [around(high, d) for d in (1, 2, 3)]
    other = [swap(a) for a in (high, *same)]
    sums = partial_tiles(where, high, low, (*same, *other))

    sums = across(sums.reshape(LAYERS, ROWS, WIDE + AUX))
    rows = across(finished_rows(here, sums))
    return rows.reshape(COLS, WIDE).astype(F32)


def solution(mesh):
    in_specs = (P("layer", None, "ex"), P("layer", None, "ex"), P())
    out_specs = P("ex", None)
    return jax.shard_map(
        on_device, mesh=mesh, in_specs=in_specs, out_specs=out_specs, check_vma=False
    )
```

time: 348 us -> 144 us (0.41)
  waiting for transfers between devices: 255 us -> 84.2 us
  local copies, waits for them, and re-layouts: 25.7 us -> 2.23 us
  starting transfers between devices: 0.13 us -> 15.6 us
  between operations: 13.3 us -> 0.08 us
  other arithmetic: 10.9 us -> 1.31 us
  Pallas kernels: 0 us -> 9.05 us
  blocking collectives: 38.2 us -> 30.8 us
  matrix products: 4.73 us -> 0 us
    psum x1 -> x0, waiting for transfers between devices: 87.8 us -> none  [on_device(): return lax.psum(assembled, 'layer')]
    reduce_scatter x1 -> x0, waiting for transfers between devices: 87.7 us -> none  [on_device(): lax.psum_scatter(dequant.reshape(slice_rows * lax.axis_size('layer'), loc...]
    all_gather x2 -> x0, waiting for transfers between devices: 79.2 us -> none  [the longest x1 57.5 us: on_device(): all_tiles = lax.all_gather(tile_sums, 'ex', axis=0, tiled=True)]
    all_to_all x0 -> x2, waiting for transfers between devices: none -> 74.6 us  [on_device(): across = lambda a: lax.all_to_all(a, 'layer', 0, 0, tiled=True)]
    psum x1 -> x0, blocking collectives: 38.2 us -> none  [on_device(): squares = lax.psum(jnp.sum(summed * summed, axis=0), 'layer')]
    all_to_all x0 -> x2, blocking collectives: none -> 30.8 us  [on_device(): across = lambda a: lax.all_to_all(a, 'layer', 0, 0, tiled=True)]
    gather x8 -> x0, local copies, waits for them, and re-layouts: 14.2 us -> none  [the longest x2 5.96 us: on_device(): picked = all_tiles[source_slot]]
    ppermute x0 -> x7, waiting for transfers between devices: none -> 9.55 us  [the longest x3 8.38 us: on_device(): lax.ppermute(a, 'ex', [(e, (e + 2 * d) % N_EX) for e in range(N_EX)])]
  transfers between devices with their start and end apart: 4 -> 9, of which waited for: 4 -> 6; matrix products, arithmetic and copies ran while one was open for 1% -> 0% of each run, Pallas kernels for 0% -> 0%
where the time goes in v1:
time: 144 us; the launch traced here: 143 us
  waiting for transfers between devices  84.2 us (58%)
  blocking collectives  30.8 us (21%)
  starting transfers between devices  15.6 us (11%)
  Pallas kernels  9.05 us (6%)
  local copies, waits for them, and re-layouts  2.23 us (2%)
    all_to_all x2, waiting for transfers between devices, on_device(): across = lambda a: lax.all_to_all(a, 'layer', 0, 0, tiled=True)  74.6 us
    all_to_all x2, blocking collectives, on_device(): across = lambda a: lax.all_to_all(a, 'layer', 0, 0, tiled=True)  30.8 us
    all_to_all x2, starting transfers between devices, on_device(): across = lambda a: lax.all_to_all(a, 'layer', 0, 0, tiled=True)  8.57 us
    ppermute x3, waiting for transfers between devices, on_device(): lax.ppermute(a, 'ex', [(e, (e + 2 * d) % N_EX) for e in range(N_EX)])  8.38 us
    ppermute x3, starting transfers between devices, on_device(): lax.ppermute(a, 'ex', [(e, (e + 2 * d) % N_EX) for e in range(N_EX)])  6.51 us
    pallas_call x1, Pallas kernels, summed_slice(): pl.pallas_call(sum_layers, grid=(SCALES,), in_specs=[pl.BlockSpec((LAYERS...  6.06 us
  transfers between devices with their start and end apart: 9, of which 6 were waited for; matrix products, arithmetic and copies ran while one was open for 0% of the time, Pallas kernels for 0%

profile of v1, /device:TPU:0, one launch (start us, length us, event | category | flops | bytes accessed | tf_op | source)
XLA Modules:
  0.0 143.2 jit_solution(16714368734178913987)
XLA Ops:
  0.0 15.2 %all_to_all.20.scale_ref = f32[16,8,256]{2,1,0:T(8,128)} all-to-all(f32[16,8,256]{2,1,0:T(8,128)} %bitcast.12), channel_id=1, replica_groups=mesh['layer'=16,'ex'=8] {'layer'}, dimensions={0} | all-to-all | bytes 262144 | tf_op jit(solution)/shard_map/all_to_all | solution.py:165
  15.2 0.0 copy-start.2
  15.2 4.7 %all-to-all-start = ((bf16[16,512,256]{2,1,0:T(8,128)(2,1)}), bf16[16,512,256]{2,1,0:T(8,128)(2,1)}, u32[]{:S(2)}, u32[]{:S(2)}) async-start(bf16[16,512,256]{2,1,0:T(8,128)(2,1)} %bitcast.11), calls=%async_computation | async-start | bytes 8388608 | tf_op jit(solution)/shard_map/all_to_all | solution.py:165
  19.9 0.0 copy-done.2
  19.9 0.1 reshape.28
  20.0 60.0 %all-to-all-done.piece_ref = bf16[16,512,256]{2,1,0:T(8,128)(2,1)} async-done(((bf16[16,512,256]{2,1,0:T(8,128)(2,1)}), bf16[16,512,256]{2,1,0:T(8,128)(2,1)}, u32[]{:S(2)}, u32[]{:S(2)}) %all-to-all-start) | async-done | bytes 4194336 | tf_op jit(solution)/shard_map/all_to_all | solution.py:165
  80.0 6.1 %shard_map.37 = (bf16[512,256]{1,0:T(8,128)(2,1)}, bf16[512,256]{1,0:T(8,128)(2,1)}) custom-call(bf16[16,512,256]{2,1,0:T(8,128)(2,1)} %all-to-all-done.piece_ref, f32[16,8,256]{2,1,0:T(8,128)} %all_to_all.20.scale_ref), custom_call_target="tpu_custom_call" | custom-call | flops 4194304 | bytes 4194304 | tf_op jit(solution)/shard_map/pallas_call | solution.py:40
  86.1 1.9 %collective-permute-start = (bf16[512,256]{1,0:T(8,128)(2,1)}, bf16[512,256]{1,0:T(8,128)(2,1)S(1)}, u32[]{:S(2)}, u32[]{:S(2)}) collective-permute-start(bf16[512,256]{1,0:T(8,128)(2,1)} %get-tuple-element.7.high_ref), channel_id=1, source_target_pairs={{0,2},{1,3},{2,4},{3,5},{4,6},{5,7},{6,0},{7,1},{8,10},{9,11},{10,... | collective-permute-start | bytes 786440 | tf_op jit(solution)/shard_map/ppermute | solution.py:170
  88.0 3.6 %collective-permute-start.1 = (bf16[512,256]{1,0:T(8,128)(2,1)}, bf16[512,256]{1,0:T(8,128)(2,1)S(1)}, u32[]{:S(2)}, u32[]{:S(2)}) collective-permute-start(bf16[512,256]{1,0:T(8,128)(2,1)} %get-tuple-element.7.high_ref), channel_id=1, source_target_pairs={{0,4},{1,5},{2,6},{3,7},{4,0},{5,1},{6,2},{7,3},{8,12},{9,13},{10,... | collective-permute-start | bytes 786440 | tf_op jit(solution)/shard_map/ppermute | solution.py:170
  91.6 1.0 collective-permute-start.2
  92.6 0.1 copy.10
  92.7 0.1 copy.11
  92.7 0.0 collective-permute-start.3
  92.8 4.5 %collective-permute-done.refs_0_ = bf16[512,256]{1,0:T(8,128)(2,1)S(1)} collective-permute-done((bf16[512,256]{1,0:T(8,128)(2,1)}, bf16[512,256]{1,0:T(8,128)(2,1)S(1)}, u32[]{:S(2)}, u32[]{:S(2)}) %collective-permute-start) | collective-permute-done | bytes 262176 | tf_op jit(solution)/shard_map/ppermute | solution.py:170
  97.3 0.0 collective-permute-start.4
  97.3 3.8 %collective-permute-done.1.refs_1_ = bf16[512,256]{1,0:T(8,128)(2,1)S(1)} collective-permute-done((bf16[512,256]{1,0:T(8,128)(2,1)}, bf16[512,256]{1,0:T(8,128)(2,1)S(1)}, u32[]{:S(2)}, u32[]{:S(2)}) %collective-permute-start.1) | collective-permute-done | bytes 262176 | tf_op jit(solution)/shard_map/ppermute | solution.py:170
  101.1 0.0 collective-permute-start.5
  101.1 0.0 collective-permute-done.2.refs_2_
  101.1 0.5 collective-permute-start.6
  101.6 0.1 add_reduce_fusion
  101.7 0.1 reduce_sum.12
  101.9 0.0 collective-permute-done.3.refs_3_
  101.9 0.0 collective-permute-done.4.refs_4_
  101.9 0.8 collective-permute-done.5.refs_5_
  102.7 0.4 collective-permute-done.6.refs_6_
  103.0 0.0 copy-start
  103.0 0.9 copy-done
  104.0 0.0 copy-start.1
  104.0 0.9 copy-done.1
  104.9 2.8 %shard_map.38 = bf16[256,1536]{1,0:T(8,128)(2,1)} custom-call(s32[20]{0:T(128)S(1)} %fusion.1.where_ref, bf16[512,256]{1,0:T(8,128)(2,1)S(1)} %copy-done, bf16[512,256]{1,0:T(8,128)(2,1)S(1)} %copy-done.1, bf16[512,256]{1,0:T(8,128)(2,1)S(1)} %collective-permute-done.refs_0_, bf16[512,256]{1,0:T(8,128)(2,1)S(1)} %collective-permute-done.1.refs_1_, ...), custom_call_target="tpu_custom_call" | custom-call | flops 1073741824 | bytes 3145728 | tf_op jit(solution)/shard_map/pallas_call | solution.py:91
  107.7 3.9 %all-to-all-start.2 = ((bf16[16,16,1536]{2,1,0:T(8,128)(2,1)}), bf16[16,16,1536]{2,1,0:T(8,128)(2,1)S(1)}, u32[]{:S(2)}, u32[]{:S(2)}) async-start(bf16[16,16,1536]{2,1,0:T(8,128)(2,1)} %bitcast.5), calls=%async_computation.2 | async-start | bytes 1572864 | tf_op jit(solution)/shard_map/all_to_all | solution.py:165
  111.7 14.6 %all-to-all-done.2.sums_ref = bf16[16,16,1536]{2,1,0:T(8,128)(2,1)S(1)} async-done(((bf16[16,16,1536]{2,1,0:T(8,128)(2,1)}), bf16[16,16,1536]{2,1,0:T(8,128)(2,1)S(1)}, u32[]{:S(2)}, u32[]{:S(2)}) %all-to-all-start.2) | async-done | bytes 786464 | tf_op jit(solution)/shard_map/all_to_all | solution.py:165
  126.3 0.2 shard_map.39
  126.5 15.6 %all_to_all.21 = bf16[16,16,1280]{2,1,0:T(8,128)(2,1)S(1)} all-to-all(bf16[16,16,1280]{2,1,0:T(8,128)(2,1)S(1)} %shard_map.39), channel_id=1, replica_groups=mesh['layer'=16,'ex'=8] {'layer'}, dimensions={0} | all-to-all | bytes 1310720 | tf_op jit(solution)/shard_map/all_to_all | solution.py:165
  142.1 1.2 bitcast_convert_fusion
  (3 shorter events, 0.0 us)
Async XLA Ops:
  15.2 4.7 %copy-start.2 = (s32[80,3]{0,1:T(4,128)S(1)}, s32[80,3]{0,1:T(4,128)}, u32[]{:S(2)}) copy-start(s32[80,3]{0,1:T(4,128)} %param.5) | copy-start | bytes 2884
  15.2 64.8 %all-to-all-start = ((bf16[16,512,256]{2,1,0:T(8,128)(2,1)}), bf16[16,512,256]{2,1,0:T(8,128)(2,1)}, u32[]{:S(2)}, u32[]{:S(2)}) async-start(bf16[16,512,256]{2,1,0:T(8,128)(2,1)} %bitcast.11), calls=%async_computation | async-start | bytes 8388608 | tf_op jit(solution)/shard_map/all_to_all | solution.py:165
  86.1 11.2 %collective-permute-start = (bf16[512,256]{1,0:T(8,128)(2,1)}, bf16[512,256]{1,0:T(8,128)(2,1)S(1)}, u32[]{:S(2)}, u32[]{:S(2)}) collective-permute-start(bf16[512,256]{1,0:T(8,128)(2,1)} %get-tuple-element.7.high_ref), channel_id=1, source_target_pairs={{0,2},{1,3},{2,4},{3,5},{4,6},{5,7},{6,0},{7,1},{8,10},{9,11},{10,... | collective-permute-start | bytes 786440 | tf_op jit(solution)/shard_map/ppermute | solution.py:170
  88.0 13.1 %collective-permute-start.1 = (bf16[512,256]{1,0:T(8,128)(2,1)}, bf16[512,256]{1,0:T(8,128)(2,1)S(1)}, u32[]{:S(2)}, u32[]{:S(2)}) collective-permute-start(bf16[512,256]{1,0:T(8,128)(2,1)} %get-tuple-element.7.high_ref), channel_id=1, source_target_pairs={{0,4},{1,5},{2,6},{3,7},{4,0},{5,1},{6,2},{7,3},{8,12},{9,13},{10,... | collective-permute-start | bytes 786440 | tf_op jit(solution)/shard_map/ppermute | solution.py:170
  91.6 9.6 %collective-permute-start.2 = (bf16[512,256]{1,0:T(8,128)(2,1)}, bf16[512,256]{1,0:T(8,128)(2,1)S(1)}, u32[]{:S(2)}, u32[]{:S(2)}) collective-permute-start(bf16[512,256]{1,0:T(8,128)(2,1)} %get-tuple-element.7.high_ref), channel_id=1, source_target_pairs={{0,6},{1,7},{2,0},{3,1},{4,2},{5,3},{6,4},{7,5},{8,14},{9,15},{10,... | collective-permute-start | bytes 786440 | tf_op jit(solution)/shard_map/ppermute | solution.py:170
  92.7 9.1 %collective-permute-start.3 = (bf16[512,256]{1,0:T(8,128)(2,1)}, bf16[512,256]{1,0:T(8,128)(2,1)S(1)}, u32[]{:S(2)}, u32[]{:S(2)}) collective-permute-start(bf16[512,256]{1,0:T(8,128)(2,1)} %get-tuple-element.7.high_ref), channel_id=1, source_target_pairs={{0,1},{1,0},{2,3},{3,2},{4,5},{5,4},{6,7},{7,6},{8,9},{9,8},{10,11... | collective-permute-start | bytes 786440 | tf_op jit(solution)/shard_map/ppermute | solution.py:173
  97.3 4.6 %collective-permute-start.4 = (bf16[512,256]{1,0:T(8,128)(2,1)S(1)}, bf16[512,256]{1,0:T(8,128)(2,1)S(1)}, u32[]{:S(2)}, u32[]{:S(2)}) collective-permute-start(bf16[512,256]{1,0:T(8,128)(2,1)S(1)} %collective-permute-done.refs_0_), channel_id=1, source_target_pairs={{0,1},{1,0},{2,3},{3,2},{4,5},{5,4},{6,7},{7,6},{8,9},{9,8},{10,11... | collective-permute-start | bytes 786440 | tf_op jit(solution)/shard_map/ppermute | solution.py:173
  101.1 1.5 %collective-permute-start.5 = (bf16[512,256]{1,0:T(8,128)(2,1)S(1)}, bf16[512,256]{1,0:T(8,128)(2,1)S(1)}, u32[]{:S(2)}, u32[]{:S(2)}) collective-permute-start(bf16[512,256]{1,0:T(8,128)(2,1)S(1)} %collective-permute-done.1.refs_1_), channel_id=1, source_target_pairs={{0,1},{1,0},{2,3},{3,2},{4,5},{5,4},{6,7},{7,6},{8,9},{9,8},{10,11... | collective-permute-start | bytes 786440 | tf_op jit(solution)/shard_map/ppermute | solution.py:173
  101.1 1.9 %collective-permute-start.6 = (bf16[512,256]{1,0:T(8,128)(2,1)S(1)}, bf16[512,256]{1,0:T(8,128)(2,1)S(1)}, u32[]{:S(2)}, u32[]{:S(2)}) collective-permute-start(bf16[512,256]{1,0:T(8,128)(2,1)S(1)} %collective-permute-done.2.refs_2_), channel_id=1, source_target_pairs={{0,1},{1,0},{2,3},{3,2},{4,5},{5,4},{6,7},{7,6},{8,9},{9,8},{10,11... | collective-permute-start | bytes 786440 | tf_op jit(solution)/shard_map/ppermute | solution.py:173
  103.0 1.0 copy-start
  104.0 0.9 copy-start.1
  107.7 18.6 %all-to-all-start.2 = ((bf16[16,16,1536]{2,1,0:T(8,128)(2,1)}), bf16[16,16,1536]{2,1,0:T(8,128)(2,1)S(1)}, u32[]{:S(2)}, u32[]{:S(2)}) async-start(bf16[16,16,1536]{2,1,0:T(8,128)(2,1)} %bitcast.5), calls=%async_computation.2 | async-start | bytes 1572864 | tf_op jit(solution)/shard_map/all_to_all | solution.py:165

commit v2 on v1

--- a/solution.py
+++ b/solution.py
@@ -16,7 +16,10 @@
 BLK_DEV = 2
 COLS = BLK_DEV * TB
 SLICE = K // LAYERS
-SCALES = SLICE // QB
+SIDE = 4
+PART = K // 2 // SIDE
+PART_SCALES = PART // QB
+QUARTER = PART // SIDE
 ROWS = COLS // LAYERS
 WIDE = SLOTS * TB
 AUX = 2 * TB
@@ -24,34 +27,110 @@
 BF, F32 = jnp.bfloat16, jnp.float32
 
 
-def sum_layers(piece_ref, scale_ref, high_ref, low_ref):
-    row = pl.program_id(0)
-    total = None
-    for layer in range(LAYERS):
-        term = piece_ref[layer].astype(F32) * scale_ref[layer, pl.ds(row, 1), :]
-        total = term if total is None else total + term
-    high = total.astype(BF)
-    high_ref[...] = high
-    low_ref[...] = (total - high.astype(F32)).astype(BF)
-
-
-def summed_slice(pieces, scales):
-    block = pl.BlockSpec((QB, COLS), lambda i: (i, 0))
-    return pl.pallas_call(
-        sum_layers,
-        grid=(SCALES,),
+def lay_out(place_ref, piece_ref, scale_ref, *refs):
+    outs, sem = refs[:-1], refs[-1]
+    copies = []
+    for half in range(2):
+        for turn in range(SIDE):
+            n = half * SIDE + turn
+            part = lax.rem(place_ref[1 - half] + turn, SIDE)
+            first = pl.multiple_of(half * (K // 2) + part * PART, PART)
+            copy = pltpu.make_async_copy(
+                piece_ref.at[pl.ds(first, PART)], outs[n].at[:PART], sem.at[n]
+            )
+            copy.start()
+            copies.append(copy)
+    for half in range(2):
+        for turn in range(SIDE):
+            part = lax.rem(place_ref[1 - half] + turn, SIDE)
+            first = half * (K // 2 // QB) + part * PART_SCALES
+            first = pl.multiple_of(first, PART_SCALES)
+            scale = scale_ref[pl.ds(first, PART_SCALES), :]
+            high = scale.astype(BF)
+            outs[half * SIDE + turn][PART:, :] = jnp.concatenate(
+                [high, (scale - high.astype(F32)).astype(BF)], axis=0
+            )
+    for copy in copies:
+        copy.wait()
+
+
+def laid_out(place, pieces, scales):
+    shape = jax.ShapeDtypeStruct((PART + 2 * PART_SCALES, COLS), BF)
+    return pl.pallas_call(
+        lay_out,
         in_specs=[
-            pl.BlockSpec((LAYERS, QB, COLS), lambda i: (0, i, 0)),
-            pl.BlockSpec((LAYERS, SCALES, COLS), lambda i: (0, 0, 0)),
+            pl.BlockSpec(memory_space=pltpu.SMEM),
+            pl.BlockSpec(memory_space=pltpu.HBM),
+            pl.BlockSpec(memory_space=pltpu.VMEM),
         ],
-        out_specs=[block, block],
+        out_specs=[pl.BlockSpec(memory_space=pltpu.VMEM)] * (2 * SIDE),
+        out_shape=[shape] * (2 * SIDE),
+        scratch_shapes=[pltpu.SemaphoreType.DMA((2 * SIDE,))],
+        compiler_params=pltpu.CompilerParams(vmem_limit_bytes=32 * 2**20),
+        cost_estimate=pl.CostEstimate(
+            flops=0, bytes_accessed=4 * K * COLS, transcendentals=0
+        ),
+    )(place, pieces, scales)
+
+
+def sum_first(place_ref, *refs):
+    pieces, outs, scales = refs[: 2 * SIDE], refs[2 * SIDE : -1], refs[-1]
+    for n, ref in enumerate(pieces):
+        both = ref[PART:, :].astype(F32)
+        scales[n] = both[:PART_SCALES] + both[PART_SCALES:]
+    for half in range(2):
+        for turn in range(SIDE):
+            part = lax.rem(place_ref[half] + turn, SIDE)
+            for block in range(QUARTER // QB):
+                row = part * (QUARTER // QB) + block
+                first = pl.multiple_of(row * QB, QB)
+                total = None
+                for n in range(half * SIDE, (half + 1) * SIDE):
+                    term = pieces[n][pl.ds(first, QB), :].astype(F32)
+                    term = term * scales[n, pl.ds(row, 1), :]
+                    total = term if total is None else total + term
+                out = outs[half * SIDE + turn]
+                out[block * QB : (block + 1) * QB, :] = total
+
+
+def summed_first(place, pieces):
+    return pl.pallas_call(
+        sum_first,
+        in_specs=[pl.BlockSpec(memory_space=pltpu.SMEM)]
+        + [pl.BlockSpec(memory_space=pltpu.VMEM)] * (2 * SIDE),
+        out_specs=[pl.BlockSpec(memory_space=pltpu.VMEM)] * (2 * SIDE),
+        out_shape=[jax.ShapeDtypeStruct((QUARTER, COLS), F32)] * (2 * SIDE),
+        scratch_shapes=[pltpu.VMEM((2 * SIDE, PART_SCALES, COLS), F32)],
+        compiler_params=pltpu.CompilerParams(vmem_limit_bytes=32 * 2**20),
+        cost_estimate=pl.CostEstimate(
+            flops=2 * K * COLS, bytes_accessed=4 * K * COLS, transcendentals=0
+        ),
+    )(place, *pieces)
+
+
+def sum_second(*refs):
+    pieces, (high_ref, low_ref) = refs[: 2 * SIDE], refs[2 * SIDE :]
+    for half in range(2):
+        total = pieces[half * SIDE][...]
+        for n in range(half * SIDE + 1, (half + 1) * SIDE):
+            total += pieces[n][...]
+        high = total.astype(BF)
+        rows = slice(half * QUARTER, (half + 1) * QUARTER)
+        high_ref[rows, :] = high
+        low_ref[rows, :] = (total - high.astype(F32)).astype(BF)
+
+
+def summed_second(pieces):
+    return pl.pallas_call(
+        sum_second,
+        in_specs=[pl.BlockSpec(memory_space=pltpu.VMEM)] * (2 * SIDE),
+        out_specs=[pl.BlockSpec(memory_space=pltpu.VMEM)] * 2,
         out_shape=[jax.ShapeDtypeStruct((SLICE, COLS), BF)] * 2,
-        cost_estimate=pl.CostEstimate(
-            flops=2 * LAYERS * SLICE * COLS,
-            bytes_accessed=2 * LAYERS * SLICE * COLS,
-            transcendentals=0,
-        ),
-    )(pieces, scales)
+        compiler_params=pltpu.CompilerParams(vmem_limit_bytes=32 * 2**20),
+        cost_estimate=pl.CostEstimate(
+            flops=8 * SLICE * COLS, bytes_accessed=20 * SLICE * COLS, transcendentals=0
+        ),
+    )(*pieces)
 
 
 def tiles(where_ref, high_ref, low_ref, *refs):
@@ -160,12 +239,25 @@
 
 def on_device(partials, scales, pairs):
     ex = lax.axis_index("ex")
-    here = lax.axis_index("layer").astype(jnp.int32).reshape(1)
+    layer = lax.axis_index("layer").astype(jnp.int32)
+    here = layer.reshape(1)
+    place = jnp.stack([layer // SIDE, layer % SIDE])
     where = partner_places(pairs, ex)
-    across = lambda a: lax.all_to_all(a, "layer", 0, 0, tiled=True)
-    slice_scales = across(scales.reshape(LAYERS, SCALES, COLS))
-    pieces = across(partials.reshape(LAYERS, SLICE, COLS))
-    high, low = summed_slice(pieces, slice_scales)
+
+    def along(axis, a, turn):
+        go = lambda y, x: ((y + turn) % SIDE, x) if axis == 0 else (y, (x + turn) % SIDE)
+        to = [go(n // SIDE, n % SIDE) for n in range(LAYERS)]
+        return lax.ppermute(a, "layer", [(n, y * SIDE + x) for n, (y, x) in enumerate(to)])
+
+    def exchanged(parts, axes):
+        return [
+            a if n % SIDE == 0 else along(axes[n // SIDE], a, n % SIDE)
+            for n, a in enumerate(parts)
+        ]
+
+    parts = laid_out(place, partials[0], scales[0])
+    parts = summed_first(place, exchanged(parts, (1, 0)))
+    high, low = summed_second(exchanged(parts, (0, 1)))
 
     around = lambda a, d: lax.ppermute(
         a, "ex", [(e, (e + 2 * d) % N_EX) for e in range(N_EX)]
@@ -175,6 +267,7 @@
     other = [swap(a) for a in (high, *same)]
     sums = partial_tiles(where, high, low, (*same, *other))
 
+    across = lambda a: lax.all_to_all(a, "layer", 0, 0, tiled=True)
     sums = across(sums.reshape(LAYERS, ROWS, WIDE + AUX))
     rows = across(finished_rows(here, sums))
     return rows.reshape(COLS, WIDE).astype(F32)

time: 144 us -> 116 us (0.81)
  waiting for transfers between devices: 84.2 us -> 43.9 us
  starting transfers between devices: 15.6 us -> 27.2 us
  blocking collectives: 30.8 us -> 35.5 us
  Pallas kernels: 9.05 us -> 4.53 us
    all_to_all x2 -> x0, waiting for transfers between devices: 74.6 us -> none  [on_device(): across = lambda a: lax.all_to_all(a, 'layer', 0, 0, tiled=True)]
    ppermute x0 -> x12, waiting for transfers between devices: none -> 31 us  [along(): lax.ppermute(a, 'layer', [(n, y * SIDE + x) for n, (y, x) in enumerate(to)])]
    ppermute x0 -> x12, starting transfers between devices: none -> 21.9 us  [along(): lax.ppermute(a, 'layer', [(n, y * SIDE + x) for n, (y, x) in enumerate(to)])]
    all_to_all x2 -> x0, starting transfers between devices: 8.57 us -> none  [on_device(): across = lambda a: lax.all_to_all(a, 'layer', 0, 0, tiled=True)]
    all_to_all x2, blocking collectives: 30.8 us -> 35.5 us  [on_device(): across = lambda a: lax.all_to_all(a, 'layer', 0, 0, tiled=True)]
    pallas_call x1 -> x3, Pallas kernels: 6.06 us -> 2.43 us  [the longest x1 1.3 us: summed_first(): pl.pallas_call(sum_first, in_specs=[pl.BlockSpec(memory_space=pltpu.SMEM)...]
    ppermute x3, waiting for transfers between devices: 8.38 us -> 11.6 us  [on_device(): lax.ppermute(a, 'ex', [(e, (e + 2 * d) % N_EX) for e in range(N_EX)])]
  transfers between devices with their start and end apart: 9 -> 19, of which waited for: 6 -> 11; matrix products, arithmetic and copies ran while one was open for 0% -> 0% of each run, Pallas kernels for 0% -> 0%
where the time goes in v2:
time: 116 us
  waiting for transfers between devices  43.9 us (38%)
  blocking collectives  35.5 us (31%)
  starting transfers between devices  27.2 us (23%)
  Pallas kernels  4.53 us (4%)
  local copies, waits for them, and re-layouts  3.42 us (3%)
  other arithmetic  1.38 us (1%)
    all_to_all x2, blocking collectives, on_device(): across = lambda a: lax.all_to_all(a, 'layer', 0, 0, tiled=True)  35.5 us
    ppermute x12, waiting for transfers between devices, along(): lax.ppermute(a, 'layer', [(n, y * SIDE + x) for n, (y, x) in enumerate(to)])  31 us
    ppermute x12, starting transfers between devices, along(): lax.ppermute(a, 'layer', [(n, y * SIDE + x) for n, (y, x) in enumerate(to)])  21.9 us
    ppermute x3, waiting for transfers between devices, on_device(): lax.ppermute(a, 'ex', [(e, (e + 2 * d) % N_EX) for e in range(N_EX)])  11.6 us
    ppermute x3, starting transfers between devices, on_device(): lax.ppermute(a, 'ex', [(e, (e + 2 * d) % N_EX) for e in range(N_EX)])  5.37 us
    unnamed x6, local copies, waits for them, and re-layouts  3.09 us
  transfers between devices with their start and end apart: 19, of which 11 were waited for; matrix products, arithmetic and copies ran while one was open for 0% of the time, Pallas kernels for 0%

profile of v2, /device:TPU:0, one launch (start us, length us, event | category | flops | bytes accessed | tf_op | source)
XLA Modules:
  0.0 116.1 jit_solution(506127673466640096)
XLA Ops:
  0.0 0.1 pad_add_fusion.place_ref
  0.1 0.0 copy-start
  0.1 2.2 %copy-done = bf16[1,8192,256]{2,1,0:T(8,128)(2,1)S(1)} copy-done((bf16[1,8192,256]{2,1,0:T(8,128)(2,1)S(1)}, bf16[1,8192,256]{2,1,0:T(8,128)(2,1)}, u32[]{:S(2)}) %copy-start) | copy-done | bytes 4194328
  2.3 0.0 copy-start.1
  2.3 0.9 copy-done.1
  3.2 1.0 shard_map.37
  4.2 1.6 %collective-permute-start = (bf16[1056,256]{1,0:T(8,128)(2,1)S(1)}, bf16[1056,256]{1,0:T(8,128)(2,1)S(1)}, u32[]{:S(2)}, u32[]{:S(2)}) collective-permute-start(bf16[1056,256]{1,0:T(8,128)(2,1)S(1)} %get-tuple-element.24), channel_id=1, source_target_pairs={{0,8},{8,16},{16,24},{24,0},{32,40},{40,48},{48,56},{56,32},{64,72... | collective-permute-start | bytes 1622024 | tf_op jit(solution)/shard_map/ppermute | solution.py:250
  5.8 2.7 %collective-permute-start.1 = (bf16[1056,256]{1,0:T(8,128)(2,1)S(1)}, bf16[1056,256]{1,0:T(8,128)(2,1)S(1)}, u32[]{:S(2)}, u32[]{:S(2)}) collective-permute-start(bf16[1056,256]{1,0:T(8,128)(2,1)S(1)} %get-tuple-element.25), channel_id=1, source_target_pairs={{0,16},{8,24},{16,0},{24,8},{32,48},{40,56},{48,32},{56,40},{64,80... | collective-permute-start | bytes 1622024 | tf_op jit(solution)/shard_map/ppermute | solution.py:250
  8.6 1.4 %collective-permute-start.2 = (bf16[1056,256]{1,0:T(8,128)(2,1)S(1)}, bf16[1056,256]{1,0:T(8,128)(2,1)S(1)}, u32[]{:S(2)}, u32[]{:S(2)}) collective-permute-start(bf16[1056,256]{1,0:T(8,128)(2,1)S(1)} %get-tuple-element.26), channel_id=1, source_target_pairs={{0,24},{8,0},{16,8},{24,16},{32,56},{40,32},{48,40},{56,48},{64,88... | collective-permute-start | bytes 1622024 | tf_op jit(solution)/shard_map/ppermute | solution.py:250
  10.0 1.6 %collective-permute-start.3 = (bf16[1056,256]{1,0:T(8,128)(2,1)S(1)}, bf16[1056,256]{1,0:T(8,128)(2,1)S(1)}, u32[]{:S(2)}, u32[]{:S(2)}) collective-permute-start(bf16[1056,256]{1,0:T(8,128)(2,1)S(1)} %get-tuple-element.28), channel_id=1, source_target_pairs={{0,32},{8,40},{16,48},{24,56},{32,64},{40,72},{48,80},{56,88},{64,... | collective-permute-start | bytes 1622024 | tf_op jit(solution)/shard_map/ppermute | solution.py:250
  11.6 2.9 %collective-permute-start.4 = (bf16[1056,256]{1,0:T(8,128)(2,1)S(1)}, bf16[1056,256]{1,0:T(8,128)(2,1)S(1)}, u32[]{:S(2)}, u32[]{:S(2)}) collective-permute-start(bf16[1056,256]{1,0:T(8,128)(2,1)S(1)} %get-tuple-element.29), channel_id=1, source_target_pairs={{0,64},{8,72},{16,80},{24,88},{32,96},{40,104},{48,112},{56,120},{... | collective-permute-start | bytes 1622024 | tf_op jit(solution)/shard_map/ppermute | solution.py:250
  14.5 4.9 %collective-permute-done.refs_1_ = bf16[1056,256]{1,0:T(8,128)(2,1)S(1)} collective-permute-done((bf16[1056,256]{1,0:T(8,128)(2,1)S(1)}, bf16[1056,256]{1,0:T(8,128)(2,1)S(1)}, u32[]{:S(2)}, u32[]{:S(2)}) %collective-permute-start) | collective-permute-done | bytes 540704 | tf_op jit(solution)/shard_map/ppermute | solution.py:250
  19.4 3.4 %collective-permute-start.5 = (bf16[1056,256]{1,0:T(8,128)(2,1)S(1)}, bf16[1056,256]{1,0:T(8,128)(2,1)S(1)}, u32[]{:S(2)}, u32[]{:S(2)}) collective-permute-start(bf16[1056,256]{1,0:T(8,128)(2,1)S(1)} %get-tuple-element.30), channel_id=1, source_target_pairs={{0,96},{8,104},{16,112},{24,120},{32,0},{40,8},{48,16},{56,24},{64... | collective-permute-start | bytes 1622024 | tf_op jit(solution)/shard_map/ppermute | solution.py:250
  22.7 9.4 %collective-permute-done.1.refs_2_ = bf16[1056,256]{1,0:T(8,128)(2,1)S(1)} collective-permute-done((bf16[1056,256]{1,0:T(8,128)(2,1)S(1)}, bf16[1056,256]{1,0:T(8,128)(2,1)S(1)}, u32[]{:S(2)}, u32[]{:S(2)}) %collective-permute-start.1) | collective-permute-done | bytes 540704 | tf_op jit(solution)/shard_map/ppermute | solution.py:250
  32.1 0.0 collective-permute-done.2.refs_3_
  32.1 0.0 collective-permute-done.3.refs_5_
  32.1 5.1 %collective-permute-done.4.refs_6_ = bf16[1056,256]{1,0:T(8,128)(2,1)S(1)} collective-permute-done((bf16[1056,256]{1,0:T(8,128)(2,1)S(1)}, bf16[1056,256]{1,0:T(8,128)(2,1)S(1)}, u32[]{:S(2)}, u32[]{:S(2)}) %collective-permute-start.4) | collective-permute-done | bytes 540704 | tf_op jit(solution)/shard_map/ppermute | solution.py:250
  37.2 0.0 collective-permute-done.5.refs_7_
  37.2 0.0 copy-start.2
  37.2 1.3 %shard_map.38 = (f32[256,256]{1,0:T(8,128)S(1)}, f32[256,256]{1,0:T(8,128)S(1)}, f32[256,256]{1,0:T(8,128)S(1)}, f32[256,256]{1,0:T(8,128)S(1)}, f32[256,256]{1,...) custom-call(s32[2]{0:T(128)S(1)} %pad_add_fusion.place_ref, ...), custom_call_target="tpu_custom_call" | custom-call | flops 4194304 | bytes 8388608 | tf_op jit(solution)/shard_map/pallas_call | solution.py:97
  38.5 2.0 %collective-permute-start.6 = (f32[256,256]{1,0:T(8,128)S(1)}, f32[256,256]{1,0:T(8,128)S(1)}, u32[]{:S(2)}, u32[]{:S(2)}) collective-permute-start(f32[256,256]{1,0:T(8,128)S(1)} %get-tuple-element.32), channel_id=1, source_target_pairs={{0,32},{8,40},{16,48},{24,56},{32,64},{40,72},{48,80},{56,88},{64,... | collective-permute-start | bytes 786440 | tf_op jit(solution)/shard_map/ppermute | solution.py:250
  40.5 1.6 %collective-permute-start.7 = (f32[256,256]{1,0:T(8,128)S(1)}, f32[256,256]{1,0:T(8,128)S(1)}, u32[]{:S(2)}, u32[]{:S(2)}) collective-permute-start(f32[256,256]{1,0:T(8,128)S(1)} %get-tuple-element.33), channel_id=1, source_target_pairs={{0,64},{8,72},{16,80},{24,88},{32,96},{40,104},{48,112},{56,120},{... | collective-permute-start | bytes 786440 | tf_op jit(solution)/shard_map/ppermute | solution.py:250
  42.1 1.7 %collective-permute-start.8 = (f32[256,256]{1,0:T(8,128)S(1)}, f32[256,256]{1,0:T(8,128)S(1)}, u32[]{:S(2)}, u32[]{:S(2)}) collective-permute-start(f32[256,256]{1,0:T(8,128)S(1)} %get-tuple-element.34), channel_id=1, source_target_pairs={{0,96},{8,104},{16,112},{24,120},{32,0},{40,8},{48,16},{56,24},{64... | collective-permute-start | bytes 786440 | tf_op jit(solution)/shard_map/ppermute | solution.py:250
  43.8 0.6 collective-permute-start.9
  44.4 1.1 collective-permute-start.10
  45.5 1.7 %collective-permute-done.6.refs_1_ = f32[256,256]{1,0:T(8,128)S(1)} collective-permute-done((f32[256,256]{1,0:T(8,128)S(1)}, f32[256,256]{1,0:T(8,128)S(1)}, u32[]{:S(2)}, u32[]{:S(2)}) %collective-permute-start.6) | collective-permute-done | bytes 262176 | tf_op jit(solution)/shard_map/ppermute | solution.py:250
  47.2 1.2 %collective-permute-start.11 = (f32[256,256]{1,0:T(8,128)S(1)}, f32[256,256]{1,0:T(8,128)S(1)}, u32[]{:S(2)}, u32[]{:S(2)}) collective-permute-start(f32[256,256]{1,0:T(8,128)S(1)} %get-tuple-element.38), channel_id=1, source_target_pairs={{0,24},{8,0},{16,8},{24,16},{32,56},{40,32},{48,40},{56,48},{64,88... | collective-permute-start | bytes 786440 | tf_op jit(solution)/shard_map/ppermute | solution.py:250
  48.4 0.0 copy-done.2
  48.4 0.1 reshape.22
  48.5 4.4 %collective-permute-done.7.refs_2_ = f32[256,256]{1,0:T(8,128)S(1)} collective-permute-done((f32[256,256]{1,0:T(8,128)S(1)}, f32[256,256]{1,0:T(8,128)S(1)}, u32[]{:S(2)}, u32[]{:S(2)}) %collective-permute-start.7) | collective-permute-done | bytes 262176 | tf_op jit(solution)/shard_map/ppermute | solution.py:250
  52.9 0.0 collective-permute-done.8.refs_3_
  52.9 4.8 %collective-permute-done.9.refs_5_ = f32[256,256]{1,0:T(8,128)S(1)} collective-permute-done((f32[256,256]{1,0:T(8,128)S(1)}, f32[256,256]{1,0:T(8,128)S(1)}, u32[]{:S(2)}, u32[]{:S(2)}) %collective-permute-start.9) | collective-permute-done | bytes 262176 | tf_op jit(solution)/shard_map/ppermute | solution.py:250
  57.8 0.0 collective-permute-done.10.refs_6_
  57.8 0.6 collective-permute-done.11.refs_7_
  58.4 0.1 shard_map.39
  58.5 4.1 %collective-permute-start.14 = (bf16[512,256]{1,0:T(8,128)(2,1)S(1)}, bf16[512,256]{1,0:T(8,128)(2,1)S(1)}, u32[]{:S(2)}, u32[]{:S(2)}) collective-permute-start(bf16[512,256]{1,0:T(8,128)(2,1)S(1)} %get-tuple-element.39.high_ref), channel_id=1, source_target_pairs={{0,6},{1,7},{2,0},{3,1},{4,2},{5,3},{6,4},{7,5},{8,14},{9,15},{10,... | collective-permute-start | bytes 786440 | tf_op jit(solution)/shard_map/ppermute | solution.py:262
  62.6 0.0 collective-permute-start.13
  62.6 1.3 %collective-permute-start.12 = (bf16[512,256]{1,0:T(8,128)(2,1)S(1)}, bf16[512,256]{1,0:T(8,128)(2,1)S(1)}, u32[]{:S(2)}, u32[]{:S(2)}) collective-permute-start(bf16[512,256]{1,0:T(8,128)(2,1)S(1)} %get-tuple-element.39.high_ref), channel_id=1, source_target_pairs={{0,2},{1,3},{2,4},{3,5},{4,6},{5,7},{6,0},{7,1},{8,10},{9,11},{10,... | collective-permute-start | bytes 786440 | tf_op jit(solution)/shard_map/ppermute | solution.py:262
  63.9 0.1 copy.10
  64.0 0.1 copy.11
  64.1 0.0 collective-permute-start.15
  64.1 8.2 %collective-permute-done.14.refs_2_ = bf16[512,256]{1,0:T(8,128)(2,1)S(1)} collective-permute-done((bf16[512,256]{1,0:T(8,128)(2,1)S(1)}, bf16[512,256]{1,0:T(8,128)(2,1)S(1)}, u32[]{:S(2)}, u32[]{:S(2)}) %collective-permute-start.14) | collective-permute-done | bytes 262176 | tf_op jit(solution)/shard_map/ppermute | solution.py:262
  72.3 0.0 collective-permute-start.18
  72.3 0.9 collective-permute-done.13.refs_1_
  73.3 0.0 collective-permute-start.17
  73.3 2.5 %collective-permute-done.12.refs_0_ = bf16[512,256]{1,0:T(8,128)(2,1)S(1)} collective-permute-done((bf16[512,256]{1,0:T(8,128)(2,1)S(1)}, bf16[512,256]{1,0:T(8,128)(2,1)S(1)}, u32[]{:S(2)}, u32[]{:S(2)}) %collective-permute-start.12) | collective-permute-done | bytes 262176 | tf_op jit(solution)/shard_map/ppermute | solution.py:262
  75.7 0.0 collective-permute-start.16
  75.7 0.1 add_reduce_fusion
  75.8 0.1 reduce_sum.12
  75.9 0.0 collective-permute-done.15.refs_3_
  76.0 0.0 collective-permute-done.18.refs_6_
  76.0 0.0 collective-permute-done.17.refs_5_
  76.0 1.3 %collective-permute-done.16.refs_4_ = bf16[512,256]{1,0:T(8,128)(2,1)S(1)} collective-permute-done((bf16[512,256]{1,0:T(8,128)(2,1)S(1)}, bf16[512,256]{1,0:T(8,128)(2,1)S(1)}, u32[]{:S(2)}, u32[]{:S(2)}) %collective-permute-start.16) | collective-permute-done | bytes 262176 | tf_op jit(solution)/shard_map/ppermute | solution.py:265
  77.3 1.9 %shard_map.40 = bf16[256,1536]{1,0:T(8,128)(2,1)S(1)} custom-call(s32[20]{0:T(128)S(1)} %fusion.1.where_ref, bf16[512,256]{1,0:T(8,128)(2,1)S(1)} %get-tuple-element.39.high_ref, bf16[512,256]{1,0:T(8,128)(2,1)S(1)} %get-tuple-element.40.low_ref, bf16[512,256]{1,0:T(8,128)(2,1)S(1)} %collective-permute-done.12.refs_0_, ...), custom_call_target="tpu_custom_call" | custom-call | flops 1073741824 | bytes 3145728 | tf_op jit(solution)/shard_map/pallas_call | solution.py:170
  79.2 20.0 %all_to_all.10.sums_ref = bf16[16,16,1536]{2,1,0:T(8,128)(2,1)S(1)} all-to-all(bf16[16,16,1536]{2,1,0:T(8,128)(2,1)S(1)} %bitcast.14), channel_id=1, replica_groups=mesh['layer'=16,'ex'=8] {'layer'}, dimensions={0} | all-to-all | bytes 1572864 | tf_op jit(solution)/shard_map/all_to_all | solution.py:270
  99.1 0.2 shard_map.41
  99.3 15.5 %all_to_all.11 = bf16[16,16,1280]{2,1,0:T(8,128)(2,1)S(1)} all-to-all(bf16[16,16,1280]{2,1,0:T(8,128)(2,1)S(1)} %shard_map.41), channel_id=1, replica_groups=mesh['layer'=16,'ex'=8] {'layer'}, dimensions={0} | all-to-all | bytes 1310720 | tf_op jit(solution)/shard_map/all_to_all | solution.py:270
  114.9 1.2 %bitcast_convert_fusion = f32[256,1280]{1,0:T(8,128)} fusion(bf16[16,16,1280]{2,1,0:T(8,128)(2,1)S(1)} %all_to_all.11), kind=kLoop, calls=%fused_computation | loop fusion | flops 327680 | bytes 1966080 | tf_op jit(solution)/shard_map/convert_element_type | solution.py:273
  (3 shorter events, 0.0 us)
Async XLA Ops:
  0.1 2.2 %copy-start = (bf16[1,8192,256]{2,1,0:T(8,128)(2,1)S(1)}, bf16[1,8192,256]{2,1,0:T(8,128)(2,1)}, u32[]{:S(2)}) copy-start(bf16[1,8192,256]{2,1,0:T(8,128)(2,1)} %param.3) | copy-start | bytes 12582916
  2.3 0.9 copy-start.1
  4.2 15.2 %collective-permute-start = (bf16[1056,256]{1,0:T(8,128)(2,1)S(1)}, bf16[1056,256]{1,0:T(8,128)(2,1)S(1)}, u32[]{:S(2)}, u32[]{:S(2)}) collective-permute-start(bf16[1056,256]{1,0:T(8,128)(2,1)S(1)} %get-tuple-element.24), channel_id=1, source_target_pairs={{0,8},{8,16},{16,24},{24,0},{32,40},{40,48},{48,56},{56,32},{64,72... | collective-permute-start | bytes 1622024 | tf_op jit(solution)/shard_map/ppermute | solution.py:250
  5.8 26.3 %collective-permute-start.1 = (bf16[1056,256]{1,0:T(8,128)(2,1)S(1)}, bf16[1056,256]{1,0:T(8,128)(2,1)S(1)}, u32[]{:S(2)}, u32[]{:S(2)}) collective-permute-start(bf16[1056,256]{1,0:T(8,128)(2,1)S(1)} %get-tuple-element.25), channel_id=1, source_target_pairs={{0,16},{8,24},{16,0},{24,8},{32,48},{40,56},{48,32},{56,40},{64,80... | collective-permute-start | bytes 1622024 | tf_op jit(solution)/shard_map/ppermute | solution.py:250
  8.6 23.6 %collective-permute-start.2 = (bf16[1056,256]{1,0:T(8,128)(2,1)S(1)}, bf16[1056,256]{1,0:T(8,128)(2,1)S(1)}, u32[]{:S(2)}, u32[]{:S(2)}) collective-permute-start(bf16[1056,256]{1,0:T(8,128)(2,1)S(1)} %get-tuple-element.26), channel_id=1, source_target_pairs={{0,24},{8,0},{16,8},{24,16},{32,56},{40,32},{48,40},{56,48},{64,88... | collective-permute-start | bytes 1622024 | tf_op jit(solution)/shard_map/ppermute | solution.py:250
  10.0 22.1 %collective-permute-start.3 = (bf16[1056,256]{1,0:T(8,128)(2,1)S(1)}, bf16[1056,256]{1,0:T(8,128)(2,1)S(1)}, u32[]{:S(2)}, u32[]{:S(2)}) collective-permute-start(bf16[1056,256]{1,0:T(8,128)(2,1)S(1)} %get-tuple-element.28), channel_id=1, source_target_pairs={{0,32},{8,40},{16,48},{24,56},{32,64},{40,72},{48,80},{56,88},{64,... | collective-permute-start | bytes 1622024 | tf_op jit(solution)/shard_map/ppermute | solution.py:250
  11.6 25.6 %collective-permute-start.4 = (bf16[1056,256]{1,0:T(8,128)(2,1)S(1)}, bf16[1056,256]{1,0:T(8,128)(2,1)S(1)}, u32[]{:S(2)}, u32[]{:S(2)}) collective-permute-start(bf16[1056,256]{1,0:T(8,128)(2,1)S(1)} %get-tuple-element.29), channel_id=1, source_target_pairs={{0,64},{8,72},{16,80},{24,88},{32,96},{40,104},{48,112},{56,120},{... | collective-permute-start | bytes 1622024 | tf_op jit(solution)/shard_map/ppermute | solution.py:250
  19.4 17.8 %collective-permute-start.5 = (bf16[1056,256]{1,0:T(8,128)(2,1)S(1)}, bf16[1056,256]{1,0:T(8,128)(2,1)S(1)}, u32[]{:S(2)}, u32[]{:S(2)}) collective-permute-start(bf16[1056,256]{1,0:T(8,128)(2,1)S(1)} %get-tuple-element.30), channel_id=1, source_target_pairs={{0,96},{8,104},{16,112},{24,120},{32,0},{40,8},{48,16},{56,24},{64... | collective-permute-start | bytes 1622024 | tf_op jit(solution)/shard_map/ppermute | solution.py:250
  37.2 11.2 %copy-start.2 = (s32[80,3]{0,1:T(4,128)S(1)}, s32[80,3]{0,1:T(4,128)}, u32[]{:S(2)}) copy-start(s32[80,3]{0,1:T(4,128)} %param.5) | copy-start | bytes 2884
  38.5 8.7 %collective-permute-start.6 = (f32[256,256]{1,0:T(8,128)S(1)}, f32[256,256]{1,0:T(8,128)S(1)}, u32[]{:S(2)}, u32[]{:S(2)}) collective-permute-start(f32[256,256]{1,0:T(8,128)S(1)} %get-tuple-element.32), channel_id=1, source_target_pairs={{0,32},{8,40},{16,48},{24,56},{32,64},{40,72},{48,80},{56,88},{64,... | collective-permute-start | bytes 786440 | tf_op jit(solution)/shard_map/ppermute | solution.py:250
  40.5 12.4 %collective-permute-start.7 = (f32[256,256]{1,0:T(8,128)S(1)}, f32[256,256]{1,0:T(8,128)S(1)}, u32[]{:S(2)}, u32[]{:S(2)}) collective-permute-start(f32[256,256]{1,0:T(8,128)S(1)} %get-tuple-element.33), channel_id=1, source_target_pairs={{0,64},{8,72},{16,80},{24,88},{32,96},{40,104},{48,112},{56,120},{... | collective-permute-start | bytes 786440 | tf_op jit(solution)/shard_map/ppermute | solution.py:250
  42.1 10.8 %collective-permute-start.8 = (f32[256,256]{1,0:T(8,128)S(1)}, f32[256,256]{1,0:T(8,128)S(1)}, u32[]{:S(2)}, u32[]{:S(2)}) collective-permute-start(f32[256,256]{1,0:T(8,128)S(1)} %get-tuple-element.34), channel_id=1, source_target_pairs={{0,96},{8,104},{16,112},{24,120},{32,0},{40,8},{48,16},{56,24},{64... | collective-permute-start | bytes 786440 | tf_op jit(solution)/shard_map/ppermute | solution.py:250
  43.8 14.0 %collective-permute-start.9 = (f32[256,256]{1,0:T(8,128)S(1)}, f32[256,256]{1,0:T(8,128)S(1)}, u32[]{:S(2)}, u32[]{:S(2)}) collective-permute-start(f32[256,256]{1,0:T(8,128)S(1)} %get-tuple-element.36), channel_id=1, source_target_pairs={{0,8},{8,16},{16,24},{24,0},{32,40},{40,48},{48,56},{56,32},{64,72... | collective-permute-start | bytes 786440 | tf_op jit(solution)/shard_map/ppermute | solution.py:250
  44.4 13.4 %collective-permute-start.10 = (f32[256,256]{1,0:T(8,128)S(1)}, f32[256,256]{1,0:T(8,128)S(1)}, u32[]{:S(2)}, u32[]{:S(2)}) collective-permute-start(f32[256,256]{1,0:T(8,128)S(1)} %get-tuple-element.37), channel_id=1, source_target_pairs={{0,16},{8,24},{16,0},{24,8},{32,48},{40,56},{48,32},{56,40},{64,80... | collective-permute-start | bytes 786440 | tf_op jit(solution)/shard_map/ppermute | solution.py:250
  47.2 11.2 %collective-permute-start.11 = (f32[256,256]{1,0:T(8,128)S(1)}, f32[256,256]{1,0:T(8,128)S(1)}, u32[]{:S(2)}, u32[]{:S(2)}) collective-permute-start(f32[256,256]{1,0:T(8,128)S(1)} %get-tuple-element.38), channel_id=1, source_target_pairs={{0,24},{8,0},{16,8},{24,16},{32,56},{40,32},{48,40},{56,48},{64,88... | collective-permute-start | bytes 786440 | tf_op jit(solution)/shard_map/ppermute | solution.py:250
  58.5 13.8 %collective-permute-start.14 = (bf16[512,256]{1,0:T(8,128)(2,1)S(1)}, bf16[512,256]{1,0:T(8,128)(2,1)S(1)}, u32[]{:S(2)}, u32[]{:S(2)}) collective-permute-start(bf16[512,256]{1,0:T(8,128)(2,1)S(1)} %get-tuple-element.39.high_ref), channel_id=1, source_target_pairs={{0,6},{1,7},{2,0},{3,1},{4,2},{5,3},{6,4},{7,5},{8,14},{9,15},{10,... | collective-permute-start | bytes 786440 | tf_op jit(solution)/shard_map/ppermute | solution.py:262
  62.6 10.6 %collective-permute-start.13 = (bf16[512,256]{1,0:T(8,128)(2,1)S(1)}, bf16[512,256]{1,0:T(8,128)(2,1)S(1)}, u32[]{:S(2)}, u32[]{:S(2)}) collective-permute-start(bf16[512,256]{1,0:T(8,128)(2,1)S(1)} %get-tuple-element.39.high_ref), channel_id=1, source_target_pairs={{0,4},{1,5},{2,6},{3,7},{4,0},{5,1},{6,2},{7,3},{8,12},{9,13},{10,... | collective-permute-start | bytes 786440 | tf_op jit(solution)/shard_map/ppermute | solution.py:262
  62.6 13.1 %collective-permute-start.12 = (bf16[512,256]{1,0:T(8,128)(2,1)S(1)}, bf16[512,256]{1,0:T(8,128)(2,1)S(1)}, u32[]{:S(2)}, u32[]{:S(2)}) collective-permute-start(bf16[512,256]{1,0:T(8,128)(2,1)S(1)} %get-tuple-element.39.high_ref), channel_id=1, source_target_pairs={{0,2},{1,3},{2,4},{3,5},{4,6},{5,7},{6,0},{7,1},{8,10},{9,11},{10,... | collective-permute-start | bytes 786440 | tf_op jit(solution)/shard_map/ppermute | solution.py:262
  64.1 11.9 %collective-permute-start.15 = (bf16[512,256]{1,0:T(8,128)(2,1)S(1)}, bf16[512,256]{1,0:T(8,128)(2,1)S(1)}, u32[]{:S(2)}, u32[]{:S(2)}) collective-permute-start(bf16[512,256]{1,0:T(8,128)(2,1)S(1)} %get-tuple-element.39.high_ref), channel_id=1, source_target_pairs={{0,1},{1,0},{2,3},{3,2},{4,5},{5,4},{6,7},{7,6},{8,9},{9,8},{10,11... | collective-permute-start | bytes 786440 | tf_op jit(solution)/shard_map/ppermute | solution.py:265
  72.3 3.6 %collective-permute-start.18 = (bf16[512,256]{1,0:T(8,128)(2,1)S(1)}, bf16[512,256]{1,0:T(8,128)(2,1)S(1)}, u32[]{:S(2)}, u32[]{:S(2)}) collective-permute-start(bf16[512,256]{1,0:T(8,128)(2,1)S(1)} %collective-permute-done.14.refs_2_), channel_id=1, source_target_pairs={{0,1},{1,0},{2,3},{3,2},{4,5},{5,4},{6,7},{7,6},{8,9},{9,8},{10,11... | collective-permute-start | bytes 786440 | tf_op jit(solution)/shard_map/ppermute | solution.py:265
  73.3 2.7 %collective-permute-start.17 = (bf16[512,256]{1,0:T(8,128)(2,1)S(1)}, bf16[512,256]{1,0:T(8,128)(2,1)S(1)}, u32[]{:S(2)}, u32[]{:S(2)}) collective-permute-start(bf16[512,256]{1,0:T(8,128)(2,1)S(1)} %collective-permute-done.13.refs_1_), channel_id=1, source_target_pairs={{0,1},{1,0},{2,3},{3,2},{4,5},{5,4},{6,7},{7,6},{8,9},{9,8},{10,11... | collective-permute-start | bytes 786440 | tf_op jit(solution)/shard_map/ppermute | solution.py:265
  75.7 1.5 %collective-permute-start.16 = (bf16[512,256]{1,0:T(8,128)(2,1)S(1)}, bf16[512,256]{1,0:T(8,128)(2,1)S(1)}, u32[]{:S(2)}, u32[]{:S(2)}) collective-permute-start(bf16[512,256]{1,0:T(8,128)(2,1)S(1)} %collective-permute-done.12.refs_0_), channel_id=1, source_target_pairs={{0,1},{1,0},{2,3},{3,2},{4,5},{5,4},{6,7},{7,6},{8,9},{9,8},{10,11... | collective-permute-start | bytes 786440 | tf_op jit(solution)/shard_map/ppermute | solution.py:265

commit v3 on v1

--- a/solution.py
+++ b/solution.py
@@ -1,3 +1,4 @@
+import functools
 import math
 
 import jax
@@ -16,7 +17,10 @@
 BLK_DEV = 2
 COLS = BLK_DEV * TB
 SLICE = K // LAYERS
-SCALES = SLICE // QB
+SIDE = 4
+PART = K // 2 // SIDE
+PART_SCALES = PART // QB
+QUARTER = PART // SIDE
 ROWS = COLS // LAYERS
 WIDE = SLOTS * TB
 AUX = 2 * TB
@@ -24,52 +28,127 @@
 BF, F32 = jnp.bfloat16, jnp.float32
 
 
-def sum_layers(piece_ref, scale_ref, high_ref, low_ref):
-    row = pl.program_id(0)
-    total = None
-    for layer in range(LAYERS):
-        term = piece_ref[layer].astype(F32) * scale_ref[layer, pl.ds(row, 1), :]
-        total = term if total is None else total + term
+def lay_out(half, place_ref, piece_ref, scale_ref, *refs):
+    outs, sem = refs[:-1], refs[-1]
+    copies = []
+    for turn in range(SIDE):
+        part = lax.rem(place_ref[1 - half] + turn, SIDE)
+        first = pl.multiple_of(half * (K // 2) + part * PART, PART)
+        copy = pltpu.make_async_copy(
+            piece_ref.at[pl.ds(first, PART)], outs[turn].at[:PART], sem.at[turn]
+        )
+        copy.start()
+        copies.append(copy)
+    for turn in range(SIDE):
+        part = lax.rem(place_ref[1 - half] + turn, SIDE)
+        first = half * (K // 2 // QB) + part * PART_SCALES
+        first = pl.multiple_of(first, PART_SCALES)
+        scale = scale_ref[pl.ds(first, PART_SCALES), :]
+        high = scale.astype(BF)
+        outs[turn][PART:, :] = jnp.concatenate(
+            [high, (scale - high.astype(F32)).astype(BF)], axis=0
+        )
+    for copy in copies:
+        copy.wait()
+
+
+def laid_out(half, place, pieces, scales):
+    shape = jax.ShapeDtypeStruct((PART + 2 * PART_SCALES, COLS), BF)
+    return pl.pallas_call(
+        functools.partial(lay_out, half),
+        in_specs=[
+            pl.BlockSpec(memory_space=pltpu.SMEM),
+            pl.BlockSpec(memory_space=pltpu.HBM),
+            pl.BlockSpec(memory_space=pltpu.VMEM),
+        ],
+        out_specs=[pl.BlockSpec(memory_space=pltpu.VMEM)] * SIDE,
+        out_shape=[shape] * SIDE,
+        scratch_shapes=[pltpu.SemaphoreType.DMA((SIDE,))],
+        compiler_params=pltpu.CompilerParams(vmem_limit_bytes=32 * 2**20),
+        cost_estimate=pl.CostEstimate(
+            flops=0, bytes_accessed=2 * K * COLS, transcendentals=0
+        ),
+    )(place, pieces, scales)
+
+
+def sum_first(half, place_ref, *refs):
+    pieces, outs, scales = refs[:SIDE], refs[SIDE:-1], refs[-1]
+    for n, ref in enumerate(pieces):
+        both = ref[PART:, :].astype(F32)
+        scales[n] = both[:PART_SCALES] + both[PART_SCALES:]
+    for turn in range(SIDE):
+        part = lax.rem(place_ref[half] + turn, SIDE)
+        for block in range(QUARTER // QB):
+            row = part * (QUARTER // QB) + block
+            first = pl.multiple_of(row * QB, QB)
+            total = None
+            for n in range(SIDE):
+                term = pieces[n][pl.ds(first, QB), :].astype(F32)
+                term = term * scales[n, pl.ds(row, 1), :]
+                total = term if total is None else total + term
+            outs[turn][block * QB : (block + 1) * QB, :] = total
+
+
+def summed_first(half, place, pieces):
+    return pl.pallas_call(
+        functools.partial(sum_first, half),
+        in_specs=[pl.BlockSpec(memory_space=pltpu.SMEM)]
+        + [pl.BlockSpec(memory_space=pltpu.VMEM)] * SIDE,
+        out_specs=[pl.BlockSpec(memory_space=pltpu.VMEM)] * SIDE,
+        out_shape=[jax.ShapeDtypeStruct((QUARTER, COLS), F32)] * SIDE,
+        scratch_shapes=[pltpu.VMEM((SIDE, PART_SCALES, COLS), F32)],
+        compiler_params=pltpu.CompilerParams(vmem_limit_bytes=32 * 2**20),
+        cost_estimate=pl.CostEstimate(
+            flops=K * COLS, bytes_accessed=2 * K * COLS, transcendentals=0
+        ),
+    )(place, *pieces)
+
+
+def sum_second(*refs):
+    pieces, (high_ref, low_ref) = refs[:SIDE], refs[SIDE:]
+    total = pieces[0][...]
+    for ref in pieces[1:]:
+        total += ref[...]
     high = total.astype(BF)
     high_ref[...] = high
     low_ref[...] = (total - high.astype(F32)).astype(BF)
 
 
-def summed_slice(pieces, scales):
-    block = pl.BlockSpec((QB, COLS), lambda i: (i, 0))
-    return pl.pallas_call(
-        sum_layers,
-        grid=(SCALES,),
-        in_specs=[
-            pl.BlockSpec((LAYERS, QB, COLS), lambda i: (0, i, 0)),
-            pl.BlockSpec((LAYERS, SCALES, COLS), lambda i: (0, 0, 0)),
-        ],
-        out_specs=[block, block],
-        out_shape=[jax.ShapeDtypeStruct((SLICE, COLS), BF)] * 2,
-        cost_estimate=pl.CostEstimate(
-            flops=2 * LAYERS * SLICE * COLS,
-            bytes_accessed=2 * LAYERS * SLICE * COLS,
-            transcendentals=0,
-        ),
-    )(pieces, scales)
-
-
-def tiles(where_ref, high_ref, low_ref, *refs):
-    parts, (out_ref, dots, squares) = refs[:7], refs[7:]
+def summed_second(pieces):
+    return pl.pallas_call(
+        sum_second,
+        in_specs=[pl.BlockSpec(memory_space=pltpu.VMEM)] * SIDE,
+        out_specs=[pl.BlockSpec(memory_space=pltpu.VMEM)] * 2,
+        out_shape=[jax.ShapeDtypeStruct((QUARTER, COLS), BF)] * 2,
+        compiler_params=pltpu.CompilerParams(vmem_limit_bytes=32 * 2**20),
+        cost_estimate=pl.CostEstimate(
+            flops=4 * SLICE * COLS, bytes_accessed=10 * SLICE * COLS, transcendentals=0
+        ),
+    )(*pieces)
+
+
+def tiles(where_ref, *refs):
+    (out_ref, dots, squares), refs = refs[-3:], refs[:-3]
     contract = (((0,), (0,)), ((), ()))
-    high, low = high_ref[...], low_ref[...]
-    for n, ref in enumerate((high_ref, *parts)):
-        part = ref[...]
-        dot = lax.dot_general(high, part, contract, preferred_element_type=F32)
-        dot += lax.dot_general(low, part, contract, preferred_element_type=F32)
-        wide = part.astype(F32)
-        square = jnp.sum(wide * wide, axis=0, keepdims=True)
+    highs, lows, parts = refs[:2], refs[2:4], refs[4:]
+    high = [ref[...] for ref in highs]
+    low = [ref[...] for ref in lows]
+    for n in range(N_EX):
+        dot, square = 0.0, 0.0
+        for half in range(2):
+            part = high[half] if n == 0 else parts[half * (N_EX - 1) + n - 1][...]
+            for own in (high[half], low[half]):
+                dot += lax.dot_general(own, part, contract, preferred_element_type=F32)
+            wide = part.astype(F32)
+            square += jnp.sum(wide * wide, axis=0, keepdims=True)
         for half in range(BLK_DEV):
             cut = slice(half * TB, (half + 1) * TB)
             dots[n * BLK_DEV + half] = dot[:, cut]
             squares[n * BLK_DEV + half] = jnp.broadcast_to(square[:, cut], (8, TB))
-    exact = high.astype(F32) + low.astype(F32)
-    own = jnp.sum(exact * exact, axis=0, keepdims=True)
+    own = 0.0
+    for half in range(2):
+        exact = high[half].astype(F32) + low[half].astype(F32)
+        own += jnp.sum(exact * exact, axis=0, keepdims=True)
     for b in range(BLK_DEV):
         rows = slice(b * TB, (b + 1) * TB)
         aux = []
@@ -87,11 +166,11 @@
             out_ref[b * TB + i * ROWS : b * TB + (i + 1) * ROWS, WIDE:] = both
 
 
-def partial_tiles(where, high, low, parts):
+def partial_tiles(where, highs, lows, parts):
     return pl.pallas_call(
         tiles,
         in_specs=[pl.BlockSpec(memory_space=pltpu.SMEM)]
-        + [pl.BlockSpec(memory_space=pltpu.VMEM)] * 9,
+        + [pl.BlockSpec(memory_space=pltpu.VMEM)] * (4 + len(parts)),
         out_specs=pl.BlockSpec(memory_space=pltpu.VMEM),
         out_shape=jax.ShapeDtypeStruct((COLS, WIDE + AUX), BF),
         scratch_shapes=[
@@ -104,7 +183,7 @@
             bytes_accessed=2 * SLICE * COLS * 9 + 2 * COLS * (WIDE + AUX),
             transcendentals=0,
         ),
-    )(where, high, low, *parts)
+    )(where, *highs, *lows, *parts)
 
 
 def finish(me_ref, sums_ref, out_ref):
@@ -160,21 +239,36 @@
 
 def on_device(partials, scales, pairs):
     ex = lax.axis_index("ex")
-    here = lax.axis_index("layer").astype(jnp.int32).reshape(1)
+    layer = lax.axis_index("layer").astype(jnp.int32)
+    here = layer.reshape(1)
+    place = jnp.stack([layer // SIDE, layer % SIDE])
     where = partner_places(pairs, ex)
-    across = lambda a: lax.all_to_all(a, "layer", 0, 0, tiled=True)
-    slice_scales = across(scales.reshape(LAYERS, SCALES, COLS))
-    pieces = across(partials.reshape(LAYERS, SLICE, COLS))
-    high, low = summed_slice(pieces, slice_scales)
+
+    def along(axis, a, turn):
+        go = lambda y, x: ((y + turn) % SIDE, x) if axis == 0 else (y, (x + turn) % SIDE)
+        to = [go(n // SIDE, n % SIDE) for n in range(LAYERS)]
+        return lax.ppermute(a, "layer", [(n, y * SIDE + x) for n, (y, x) in enumerate(to)])
+
+    def exchanged(parts, axis):
+        return [parts[0]] + [along(axis, parts[turn], turn) for turn in range(1, SIDE)]
 
     around = lambda a, d: lax.ppermute(
         a, "ex", [(e, (e + 2 * d) % N_EX) for e in range(N_EX)]
     )
     swap = lambda a: lax.ppermute(a, "ex", [(e, e ^ 1) for e in range(N_EX)])
-    same = [around(high, d) for d in (1, 2, 3)]
-    other = [swap(a) for a in (high, *same)]
-    sums = partial_tiles(where, high, low, (*same, *other))
-
+
+    highs, lows, others = [], [], []
+    for half in range(2):
+        parts = laid_out(half, place, partials[0], scales[0])
+        parts = summed_first(half, place, exchanged(parts, 1 - half))
+        high, low = summed_second(exchanged(parts, half))
+        same = [around(high, d) for d in (1, 2, 3)]
+        highs.append(high)
+        lows.append(low)
+        others += [*same, *(swap(a) for a in (high, *same))]
+    sums = partial_tiles(where, highs, lows, others)
+
+    across = lambda a: lax.all_to_all(a, "layer", 0, 0, tiled=True)
     sums = across(sums.reshape(LAYERS, ROWS, WIDE + AUX))
     rows = across(finished_rows(here, sums))
     return rows.reshape(COLS, WIDE).astype(F32)

time: 144 us -> 108 us (0.75)
  waiting for transfers between devices: 84.2 us -> 24.7 us
  starting transfers between devices: 15.6 us -> 36.9 us
  blocking collectives: 30.8 us -> 35.7 us
  Pallas kernels: 9.05 us -> 5.65 us
    all_to_all x2 -> x0, waiting for transfers between devices: 74.6 us -> none  [on_device(): across = lambda a: lax.all_to_all(a, 'layer', 0, 0, tiled=True)]
    ppermute x0 -> x12, starting transfers between devices: none -> 23.8 us  [along(): lax.ppermute(a, 'layer', [(n, y * SIDE + x) for n, (y, x) in enumerate(to)])]
    ppermute x0 -> x12, waiting for transfers between devices: none -> 18.5 us  [along(): lax.ppermute(a, 'layer', [(n, y * SIDE + x) for n, (y, x) in enumerate(to)])]
    all_to_all x2 -> x0, starting transfers between devices: 8.57 us -> none  [on_device(): across = lambda a: lax.all_to_all(a, 'layer', 0, 0, tiled=True)]
    ppermute x3 -> x6, starting transfers between devices: 6.51 us -> 11.5 us  [on_device(): lax.ppermute(a, 'ex', [(e, (e + 2 * d) % N_EX) for e in range(N_EX)])]
    all_to_all x2, blocking collectives: 30.8 us -> 35.7 us  [on_device(): across = lambda a: lax.all_to_all(a, 'layer', 0, 0, tiled=True)]
    ppermute x3 -> x6, waiting for transfers between devices: 8.38 us -> 5.21 us  [on_device(): lax.ppermute(a, 'ex', [(e, (e + 2 * d) % N_EX) for e in range(N_EX)])]
    pallas_call x1 -> x6, Pallas kernels: 6.06 us -> 3.53 us  [the longest x2 1.85 us: summed_first(): pl.pallas_call(functools.partial(sum_first, half), in_specs=[pl.BlockSpec...]
  transfers between devices with their start and end apart: 9 -> 26, of which waited for: 6 -> 11; matrix products, arithmetic and copies ran while one was open for 0% -> 0% of each run, Pallas kernels for 0% -> 3%
where the time goes in v3:
time: 108 us
  starting transfers between devices  36.9 us (34%)
  blocking collectives  35.7 us (33%)
  waiting for transfers between devices  24.7 us (23%)
  Pallas kernels  5.65 us (5%)
  local copies, waits for them, and re-layouts  3.42 us (3%)
  other arithmetic  1.38 us (1%)
    all_to_all x2, blocking collectives, on_device(): across = lambda a: lax.all_to_all(a, 'layer', 0, 0, tiled=True)  35.7 us
    ppermute x12, starting transfers between devices, along(): lax.ppermute(a, 'layer', [(n, y * SIDE + x) for n, (y, x) in enumerate(to)])  23.8 us
    ppermute x12, waiting for transfers between devices, along(): lax.ppermute(a, 'layer', [(n, y * SIDE + x) for n, (y, x) in enumerate(to)])  18.5 us
    ppermute x6, starting transfers between devices, on_device(): lax.ppermute(a, 'ex', [(e, (e + 2 * d) % N_EX) for e in range(N_EX)])  11.5 us
    ppermute x6, waiting for transfers between devices, on_device(): lax.ppermute(a, 'ex', [(e, (e + 2 * d) % N_EX) for e in range(N_EX)])  5.21 us
    unnamed x6, local copies, waits for them, and re-layouts  3.1 us
  transfers between devices with their start and end apart: 26, of which 11 were waited for; matrix products, arithmetic and copies ran while one was open for 0% of the time, Pallas kernels for 3%

profile of v3, /device:TPU:0, one launch (start us, length us, event | category | flops | bytes accessed | tf_op | source)
XLA Modules:
  0.0 107.9 jit_solution(11187139489136463892)
XLA Ops:
  0.0 0.1 pad_add_fusion.place_ref
  0.1 2.2 %copy-done = bf16[1,8192,256]{2,1,0:T(8,128)(2,1)S(1)} copy-done((bf16[1,8192,256]{2,1,0:T(8,128)(2,1)S(1)}, bf16[1,8192,256]{2,1,0:T(8,128)(2,1)}, u32[]{:S(2)}) %copy-start) | copy-done | bytes 4194328
  2.3 0.9 copy-done.1
  3.2 0.8 shard_map.37
  3.9 1.6 %collective-permute-start = (bf16[1056,256]{1,0:T(8,128)(2,1)S(1)}, bf16[1056,256]{1,0:T(8,128)(2,1)S(1)}, u32[]{:S(2)}, u32[]{:S(2)}) collective-permute-start(bf16[1056,256]{1,0:T(8,128)(2,1)S(1)} %get-tuple-element.26), channel_id=1, source_target_pairs={{0,8},{8,16},{16,24},{24,0},{32,40},{40,48},{48,56},{56,32},{64,72... | collective-permute-start | bytes 1622024 | tf_op jit(solution)/shard_map/ppermute | solution.py:250
  5.6 2.7 %collective-permute-start.1 = (bf16[1056,256]{1,0:T(8,128)(2,1)S(1)}, bf16[1056,256]{1,0:T(8,128)(2,1)S(1)}, u32[]{:S(2)}, u32[]{:S(2)}) collective-permute-start(bf16[1056,256]{1,0:T(8,128)(2,1)S(1)} %get-tuple-element.27), channel_id=1, source_target_pairs={{0,16},{8,24},{16,0},{24,8},{32,48},{40,56},{48,32},{56,40},{64,80... | collective-permute-start | bytes 1622024 | tf_op jit(solution)/shard_map/ppermute | solution.py:250
  8.3 1.4 %collective-permute-start.2 = (bf16[1056,256]{1,0:T(8,128)(2,1)S(1)}, bf16[1056,256]{1,0:T(8,128)(2,1)S(1)}, u32[]{:S(2)}, u32[]{:S(2)}) collective-permute-start(bf16[1056,256]{1,0:T(8,128)(2,1)S(1)} %get-tuple-element.28), channel_id=1, source_target_pairs={{0,24},{8,0},{16,8},{24,16},{32,56},{40,32},{48,40},{56,48},{64,88... | collective-permute-start | bytes 1622024 | tf_op jit(solution)/shard_map/ppermute | solution.py:250
  9.8 0.8 shard_map.40
  10.5 1.6 %collective-permute-start.6 = (bf16[1056,256]{1,0:T(8,128)(2,1)S(1)}, bf16[1056,256]{1,0:T(8,128)(2,1)S(1)}, u32[]{:S(2)}, u32[]{:S(2)}) collective-permute-start(bf16[1056,256]{1,0:T(8,128)(2,1)S(1)} %get-tuple-element.35), channel_id=1, source_target_pairs={{0,32},{8,40},{16,48},{24,56},{32,64},{40,72},{48,80},{56,88},{64,... | collective-permute-start | bytes 1622024 | tf_op jit(solution)/shard_map/ppermute | solution.py:250
  12.2 2.9 %collective-permute-start.7 = (bf16[1056,256]{1,0:T(8,128)(2,1)S(1)}, bf16[1056,256]{1,0:T(8,128)(2,1)S(1)}, u32[]{:S(2)}, u32[]{:S(2)}) collective-permute-start(bf16[1056,256]{1,0:T(8,128)(2,1)S(1)} %get-tuple-element.36), channel_id=1, source_target_pairs={{0,64},{8,72},{16,80},{24,88},{32,96},{40,104},{48,112},{56,120},{... | collective-permute-start | bytes 1622024 | tf_op jit(solution)/shard_map/ppermute | solution.py:250
  15.1 4.0 %collective-permute-done.refs_1_ = bf16[1056,256]{1,0:T(8,128)(2,1)S(1)} collective-permute-done((bf16[1056,256]{1,0:T(8,128)(2,1)S(1)}, bf16[1056,256]{1,0:T(8,128)(2,1)S(1)}, u32[]{:S(2)}, u32[]{:S(2)}) %collective-permute-start) | collective-permute-done | bytes 540704 | tf_op jit(solution)/shard_map/ppermute | solution.py:250
  19.1 3.4 %collective-permute-start.8 = (bf16[1056,256]{1,0:T(8,128)(2,1)S(1)}, bf16[1056,256]{1,0:T(8,128)(2,1)S(1)}, u32[]{:S(2)}, u32[]{:S(2)}) collective-permute-start(bf16[1056,256]{1,0:T(8,128)(2,1)S(1)} %get-tuple-element.37), channel_id=1, source_target_pairs={{0,96},{8,104},{16,112},{24,120},{32,0},{40,8},{48,16},{56,24},{64... | collective-permute-start | bytes 1622024 | tf_op jit(solution)/shard_map/ppermute | solution.py:250
  22.5 9.4 %collective-permute-done.1.refs_2_ = bf16[1056,256]{1,0:T(8,128)(2,1)S(1)} collective-permute-done((bf16[1056,256]{1,0:T(8,128)(2,1)S(1)}, bf16[1056,256]{1,0:T(8,128)(2,1)S(1)}, u32[]{:S(2)}, u32[]{:S(2)}) %collective-permute-start.1) | collective-permute-done | bytes 540704 | tf_op jit(solution)/shard_map/ppermute | solution.py:250
  31.9 0.9 shard_map.38
  32.8 0.0 copy-start.2
  32.8 1.6 %collective-permute-start.3 = (f32[256,256]{1,0:T(8,128)S(1)}, f32[256,256]{1,0:T(8,128)S(1)}, u32[]{:S(2)}, u32[]{:S(2)}) collective-permute-start(f32[256,256]{1,0:T(8,128)S(1)} %get-tuple-element.30), channel_id=1, source_target_pairs={{0,32},{8,40},{16,48},{24,56},{32,64},{40,72},{48,80},{56,88},{64,... | collective-permute-start | bytes 786440 | tf_op jit(solution)/shard_map/ppermute | solution.py:250
  34.5 2.9 %collective-permute-start.4 = (f32[256,256]{1,0:T(8,128)S(1)}, f32[256,256]{1,0:T(8,128)S(1)}, u32[]{:S(2)}, u32[]{:S(2)}) collective-permute-start(f32[256,256]{1,0:T(8,128)S(1)} %get-tuple-element.31), channel_id=1, source_target_pairs={{0,64},{8,72},{16,80},{24,88},{32,96},{40,104},{48,112},{56,120},{... | collective-permute-start | bytes 786440 | tf_op jit(solution)/shard_map/ppermute | solution.py:250
  37.4 1.3 %collective-permute-start.5 = (f32[256,256]{1,0:T(8,128)S(1)}, f32[256,256]{1,0:T(8,128)S(1)}, u32[]{:S(2)}, u32[]{:S(2)}) collective-permute-start(f32[256,256]{1,0:T(8,128)S(1)} %get-tuple-element.32), channel_id=1, source_target_pairs={{0,96},{8,104},{16,112},{24,120},{32,0},{40,8},{48,16},{56,24},{64... | collective-permute-start | bytes 786440 | tf_op jit(solution)/shard_map/ppermute | solution.py:250
  38.7 0.0 collective-permute-done.7.refs_2_
  38.7 0.0 collective-permute-done.8.refs_3_
  38.8 0.9 shard_map.41
  39.7 1.4 %collective-permute-start.9 = (f32[256,256]{1,0:T(8,128)S(1)}, f32[256,256]{1,0:T(8,128)S(1)}, u32[]{:S(2)}, u32[]{:S(2)}) collective-permute-start(f32[256,256]{1,0:T(8,128)S(1)} %get-tuple-element.39), channel_id=1, source_target_pairs={{0,8},{8,16},{16,24},{24,0},{32,40},{40,48},{48,56},{56,32},{64,72... | collective-permute-start | bytes 786440 | tf_op jit(solution)/shard_map/ppermute | solution.py:250
  41.1 2.4 %collective-permute-start.10 = (f32[256,256]{1,0:T(8,128)S(1)}, f32[256,256]{1,0:T(8,128)S(1)}, u32[]{:S(2)}, u32[]{:S(2)}) collective-permute-start(f32[256,256]{1,0:T(8,128)S(1)} %get-tuple-element.40), channel_id=1, source_target_pairs={{0,16},{8,24},{16,0},{24,8},{32,48},{40,56},{48,32},{56,40},{64,80... | collective-permute-start | bytes 786440 | tf_op jit(solution)/shard_map/ppermute | solution.py:250
  43.5 1.1 %collective-permute-done.3.refs_1_ = f32[256,256]{1,0:T(8,128)S(1)} collective-permute-done((f32[256,256]{1,0:T(8,128)S(1)}, f32[256,256]{1,0:T(8,128)S(1)}, u32[]{:S(2)}, u32[]{:S(2)}) %collective-permute-start.3) | collective-permute-done | bytes 262176 | tf_op jit(solution)/shard_map/ppermute | solution.py:250
  44.6 0.4 collective-permute-start.11
  45.0 0.1 reshape.22
  45.1 3.9 %collective-permute-done.4.refs_2_ = f32[256,256]{1,0:T(8,128)S(1)} collective-permute-done((f32[256,256]{1,0:T(8,128)S(1)}, f32[256,256]{1,0:T(8,128)S(1)}, u32[]{:S(2)}, u32[]{:S(2)}) %collective-permute-start.4) | collective-permute-done | bytes 262176 | tf_op jit(solution)/shard_map/ppermute | solution.py:250
  49.1 0.0 collective-permute-done.5.refs_3_
  49.1 0.1 shard_map.39
  49.1 2.0 %collective-permute-start.12 = (bf16[256,256]{1,0:T(8,128)(2,1)S(1)}, bf16[256,256]{1,0:T(8,128)(2,1)S(1)}, u32[]{:S(2)}, u32[]{:S(2)}) collective-permute-start(bf16[256,256]{1,0:T(8,128)(2,1)S(1)} %get-tuple-element.33.refs_0_), channel_id=1, source_target_pairs={{0,2},{1,3},{2,4},{3,5},{4,6},{5,7},{6,0},{7,1},{8,10},{9,11},{10,... | collective-permute-start | bytes 393224 | tf_op jit(solution)/shard_map/ppermute | solution.py:255
  51.1 3.6 %collective-permute-start.13 = (bf16[256,256]{1,0:T(8,128)(2,1)S(1)}, bf16[256,256]{1,0:T(8,128)(2,1)S(1)}, u32[]{:S(2)}, u32[]{:S(2)}) collective-permute-start(bf16[256,256]{1,0:T(8,128)(2,1)S(1)} %get-tuple-element.33.refs_0_), channel_id=1, source_target_pairs={{0,4},{1,5},{2,6},{3,7},{4,0},{5,1},{6,2},{7,3},{8,12},{9,13},{10,... | collective-permute-start | bytes 393224 | tf_op jit(solution)/shard_map/ppermute | solution.py:255
  54.7 0.0 collective-permute-done.9.refs_1_
  54.7 1.0 collective-permute-start.14
  55.7 0.0 collective-permute-done.10.refs_2_
  55.7 0.0 collective-permute-start.15
  55.7 0.0 collective-permute-done.11.refs_3_
  55.7 0.1 shard_map.42
  55.8 1.1 %collective-permute-start.19 = (bf16[256,256]{1,0:T(8,128)(2,1)S(1)}, bf16[256,256]{1,0:T(8,128)(2,1)S(1)}, u32[]{:S(2)}, u32[]{:S(2)}) collective-permute-start(bf16[256,256]{1,0:T(8,128)(2,1)S(1)} %get-tuple-element.42.refs_1_), channel_id=1, source_target_pairs={{0,2},{1,3},{2,4},{3,5},{4,6},{5,7},{6,0},{7,1},{8,10},{9,11},{10,... | collective-permute-start | bytes 393224 | tf_op jit(solution)/shard_map/ppermute | solution.py:255
  56.9 0.5 collective-permute-done.12.refs_4_
  57.4 2.7 %collective-permute-start.20 = (bf16[256,256]{1,0:T(8,128)(2,1)S(1)}, bf16[256,256]{1,0:T(8,128)(2,1)S(1)}, u32[]{:S(2)}, u32[]{:S(2)}) collective-permute-start(bf16[256,256]{1,0:T(8,128)(2,1)S(1)} %get-tuple-element.42.refs_1_), channel_id=1, source_target_pairs={{0,4},{1,5},{2,6},{3,7},{4,0},{5,1},{6,2},{7,3},{8,12},{9,13},{10,... | collective-permute-start | bytes 393224 | tf_op jit(solution)/shard_map/ppermute | solution.py:255
  60.1 1.2 %collective-permute-start.21 = (bf16[256,256]{1,0:T(8,128)(2,1)S(1)}, bf16[256,256]{1,0:T(8,128)(2,1)S(1)}, u32[]{:S(2)}, u32[]{:S(2)}) collective-permute-start(bf16[256,256]{1,0:T(8,128)(2,1)S(1)} %get-tuple-element.42.refs_1_), channel_id=1, source_target_pairs={{0,6},{1,7},{2,0},{3,1},{4,2},{5,3},{6,4},{7,5},{8,14},{9,15},{10,... | collective-permute-start | bytes 393224 | tf_op jit(solution)/shard_map/ppermute | solution.py:255
  61.3 0.0 collective-permute-done.14.refs_6_
  61.3 0.0 collective-permute-start.22
  61.3 0.0 collective-permute-done.15.refs_7_
  61.3 0.5 collective-permute-start.16
  61.8 0.1 copy.11
  61.9 0.1 copy.10
  61.9 0.1 add_reduce_fusion
  62.0 0.1 reduce_sum.12
  62.1 0.9 collective-permute-done.19.refs_11_
  63.0 3.8 %collective-permute-done.20.refs_12_ = bf16[256,256]{1,0:T(8,128)(2,1)S(1)} collective-permute-done((bf16[256,256]{1,0:T(8,128)(2,1)S(1)}, bf16[256,256]{1,0:T(8,128)(2,1)S(1)}, u32[]{:S(2)}, u32[]{:S(2)}) %collective-permute-start.20) | collective-permute-done | bytes 131104 | tf_op jit(solution)/shard_map/ppermute | solution.py:255
  66.8 0.0 collective-permute-done.21.refs_13_
  66.8 0.5 collective-permute-start.23
  67.3 0.1 collective-permute-start.24
  67.4 0.4 collective-permute-start.25
  67.9 0.3 collective-permute-done.18.refs_10_
  68.1 0.2 collective-permute-done.23.refs_15_
  68.3 0.3 collective-permute-done.24.refs_16_
  68.7 0.2 collective-permute-done.25.refs_17_
  68.8 1.9 %shard_map.43 = bf16[256,1536]{1,0:T(8,128)(2,1)S(1)} custom-call(s32[20]{0:T(128)S(1)} %fusion.1.where_ref, bf16[256,256]{1,0:T(8,128)(2,1)S(1)} %get-tuple-element.33.refs_0_, bf16[256,256]{1,0:T(8,128)(2,1)S(1)} %get-tuple-element.42.refs_1_, bf16[256,256]{1,0:T(8,128)(2,1)S(1)} %get-tuple-element.43.refs_2_, ...), custom_call_target="tpu_custom_call" | custom-call | flops 1073741824 | bytes 3145728 | tf_op jit(solution)/shard_map/pallas_call | solution.py:170
  70.8 20.2 %all_to_all.10.sums_ref = bf16[16,16,1536]{2,1,0:T(8,128)(2,1)S(1)} all-to-all(bf16[16,16,1536]{2,1,0:T(8,128)(2,1)S(1)} %bitcast.15), channel_id=1, replica_groups=mesh['layer'=16,'ex'=8] {'layer'}, dimensions={0} | all-to-all | bytes 1572864 | tf_op jit(solution)/shard_map/all_to_all | solution.py:271
  91.0 0.2 shard_map.44
  91.1 15.5 %all_to_all.11 = bf16[16,16,1280]{2,1,0:T(8,128)(2,1)S(1)} all-to-all(bf16[16,16,1280]{2,1,0:T(8,128)(2,1)S(1)} %shard_map.44), channel_id=1, replica_groups=mesh['layer'=16,'ex'=8] {'layer'}, dimensions={0} | all-to-all | bytes 1310720 | tf_op jit(solution)/shard_map/all_to_all | solution.py:271
  106.7 1.2 %bitcast_convert_fusion = f32[256,1280]{1,0:T(8,128)} fusion(bf16[16,16,1280]{2,1,0:T(8,128)(2,1)S(1)} %all_to_all.11), kind=kLoop, calls=%fused_computation | loop fusion | flops 327680 | bytes 1966080 | tf_op jit(solution)/shard_map/convert_element_type | solution.py:274
  (14 shorter events, 0.1 us)
Async XLA Ops:
  0.1 2.2 %copy-start = (bf16[1,8192,256]{2,1,0:T(8,128)(2,1)S(1)}, bf16[1,8192,256]{2,1,0:T(8,128)(2,1)}, u32[]{:S(2)}) copy-start(bf16[1,8192,256]{2,1,0:T(8,128)(2,1)} %param.3) | copy-start | bytes 12582916
  2.3 0.9 copy-start.1
  3.9 15.2 %collective-permute-start = (bf16[1056,256]{1,0:T(8,128)(2,1)S(1)}, bf16[1056,256]{1,0:T(8,128)(2,1)S(1)}, u32[]{:S(2)}, u32[]{:S(2)}) collective-permute-start(bf16[1056,256]{1,0:T(8,128)(2,1)S(1)} %get-tuple-element.26), channel_id=1, source_target_pairs={{0,8},{8,16},{16,24},{24,0},{32,40},{40,48},{48,56},{56,32},{64,72... | collective-permute-start | bytes 1622024 | tf_op jit(solution)/shard_map/ppermute | solution.py:250
  5.6 26.3 %collective-permute-start.1 = (bf16[1056,256]{1,0:T(8,128)(2,1)S(1)}, bf16[1056,256]{1,0:T(8,128)(2,1)S(1)}, u32[]{:S(2)}, u32[]{:S(2)}) collective-permute-start(bf16[1056,256]{1,0:T(8,128)(2,1)S(1)} %get-tuple-element.27), channel_id=1, source_target_pairs={{0,16},{8,24},{16,0},{24,8},{32,48},{40,56},{48,32},{56,40},{64,80... | collective-permute-start | bytes 1622024 | tf_op jit(solution)/shard_map/ppermute | solution.py:250
  8.3 23.6 %collective-permute-start.2 = (bf16[1056,256]{1,0:T(8,128)(2,1)S(1)}, bf16[1056,256]{1,0:T(8,128)(2,1)S(1)}, u32[]{:S(2)}, u32[]{:S(2)}) collective-permute-start(bf16[1056,256]{1,0:T(8,128)(2,1)S(1)} %get-tuple-element.28), channel_id=1, source_target_pairs={{0,24},{8,0},{16,8},{24,16},{32,56},{40,32},{48,40},{56,48},{64,88... | collective-permute-start | bytes 1622024 | tf_op jit(solution)/shard_map/ppermute | solution.py:250
  10.5 26.8 %collective-permute-start.6 = (bf16[1056,256]{1,0:T(8,128)(2,1)S(1)}, bf16[1056,256]{1,0:T(8,128)(2,1)S(1)}, u32[]{:S(2)}, u32[]{:S(2)}) collective-permute-start(bf16[1056,256]{1,0:T(8,128)(2,1)S(1)} %get-tuple-element.35), channel_id=1, source_target_pairs={{0,32},{8,40},{16,48},{24,56},{32,64},{40,72},{48,80},{56,88},{64,... | collective-permute-start | bytes 1622024 | tf_op jit(solution)/shard_map/ppermute | solution.py:250
  12.2 26.6 %collective-permute-start.7 = (bf16[1056,256]{1,0:T(8,128)(2,1)S(1)}, bf16[1056,256]{1,0:T(8,128)(2,1)S(1)}, u32[]{:S(2)}, u32[]{:S(2)}) collective-permute-start(bf16[1056,256]{1,0:T(8,128)(2,1)S(1)} %get-tuple-element.36), channel_id=1, source_target_pairs={{0,64},{8,72},{16,80},{24,88},{32,96},{40,104},{48,112},{56,120},{... | collective-permute-start | bytes 1622024 | tf_op jit(solution)/shard_map/ppermute | solution.py:250
  19.1 19.6 %collective-permute-start.8 = (bf16[1056,256]{1,0:T(8,128)(2,1)S(1)}, bf16[1056,256]{1,0:T(8,128)(2,1)S(1)}, u32[]{:S(2)}, u32[]{:S(2)}) collective-permute-start(bf16[1056,256]{1,0:T(8,128)(2,1)S(1)} %get-tuple-element.37), channel_id=1, source_target_pairs={{0,96},{8,104},{16,112},{24,120},{32,0},{40,8},{48,16},{56,24},{64... | collective-permute-start | bytes 1622024 | tf_op jit(solution)/shard_map/ppermute | solution.py:250
  32.8 12.2 %copy-start.2 = (s32[80,3]{0,1:T(4,128)S(1)}, s32[80,3]{0,1:T(4,128)}, u32[]{:S(2)}) copy-start(s32[80,3]{0,1:T(4,128)} %param.5) | copy-start | bytes 2884
  32.8 11.8 %collective-permute-start.3 = (f32[256,256]{1,0:T(8,128)S(1)}, f32[256,256]{1,0:T(8,128)S(1)}, u32[]{:S(2)}, u32[]{:S(2)}) collective-permute-start(f32[256,256]{1,0:T(8,128)S(1)} %get-tuple-element.30), channel_id=1, source_target_pairs={{0,32},{8,40},{16,48},{24,56},{32,64},{40,72},{48,80},{56,88},{64,... | collective-permute-start | bytes 786440 | tf_op jit(solution)/shard_map/ppermute | solution.py:250
  34.5 14.6 %collective-permute-start.4 = (f32[256,256]{1,0:T(8,128)S(1)}, f32[256,256]{1,0:T(8,128)S(1)}, u32[]{:S(2)}, u32[]{:S(2)}) collective-permute-start(f32[256,256]{1,0:T(8,128)S(1)} %get-tuple-element.31), channel_id=1, source_target_pairs={{0,64},{8,72},{16,80},{24,88},{32,96},{40,104},{48,112},{56,120},{... | collective-permute-start | bytes 786440 | tf_op jit(solution)/shard_map/ppermute | solution.py:250
  37.4 11.7 %collective-permute-start.5 = (f32[256,256]{1,0:T(8,128)S(1)}, f32[256,256]{1,0:T(8,128)S(1)}, u32[]{:S(2)}, u32[]{:S(2)}) collective-permute-start(f32[256,256]{1,0:T(8,128)S(1)} %get-tuple-element.32), channel_id=1, source_target_pairs={{0,96},{8,104},{16,112},{24,120},{32,0},{40,8},{48,16},{56,24},{64... | collective-permute-start | bytes 786440 | tf_op jit(solution)/shard_map/ppermute | solution.py:250
  39.7 15.0 %collective-permute-start.9 = (f32[256,256]{1,0:T(8,128)S(1)}, f32[256,256]{1,0:T(8,128)S(1)}, u32[]{:S(2)}, u32[]{:S(2)}) collective-permute-start(f32[256,256]{1,0:T(8,128)S(1)} %get-tuple-element.39), channel_id=1, source_target_pairs={{0,8},{8,16},{16,24},{24,0},{32,40},{40,48},{48,56},{56,32},{64,72... | collective-permute-start | bytes 786440 | tf_op jit(solution)/shard_map/ppermute | solution.py:250
  41.1 14.6 %collective-permute-start.10 = (f32[256,256]{1,0:T(8,128)S(1)}, f32[256,256]{1,0:T(8,128)S(1)}, u32[]{:S(2)}, u32[]{:S(2)}) collective-permute-start(f32[256,256]{1,0:T(8,128)S(1)} %get-tuple-element.40), channel_id=1, source_target_pairs={{0,16},{8,24},{16,0},{24,8},{32,48},{40,56},{48,32},{56,40},{64,80... | collective-permute-start | bytes 786440 | tf_op jit(solution)/shard_map/ppermute | solution.py:250
  44.6 11.1 %collective-permute-start.11 = (f32[256,256]{1,0:T(8,128)S(1)}, f32[256,256]{1,0:T(8,128)S(1)}, u32[]{:S(2)}, u32[]{:S(2)}) collective-permute-start(f32[256,256]{1,0:T(8,128)S(1)} %get-tuple-element.41), channel_id=1, source_target_pairs={{0,24},{8,0},{16,8},{24,16},{32,56},{40,32},{48,40},{56,48},{64,88... | collective-permute-start | bytes 786440 | tf_op jit(solution)/shard_map/ppermute | solution.py:250
  49.1 8.3 %collective-permute-start.12 = (bf16[256,256]{1,0:T(8,128)(2,1)S(1)}, bf16[256,256]{1,0:T(8,128)(2,1)S(1)}, u32[]{:S(2)}, u32[]{:S(2)}) collective-permute-start(bf16[256,256]{1,0:T(8,128)(2,1)S(1)} %get-tuple-element.33.refs_0_), channel_id=1, source_target_pairs={{0,2},{1,3},{2,4},{3,5},{4,6},{5,7},{6,0},{7,1},{8,10},{9,11},{10,... | collective-permute-start | bytes 393224 | tf_op jit(solution)/shard_map/ppermute | solution.py:255
  51.1 9.0 %collective-permute-start.13 = (bf16[256,256]{1,0:T(8,128)(2,1)S(1)}, bf16[256,256]{1,0:T(8,128)(2,1)S(1)}, u32[]{:S(2)}, u32[]{:S(2)}) collective-permute-start(bf16[256,256]{1,0:T(8,128)(2,1)S(1)} %get-tuple-element.33.refs_0_), channel_id=1, source_target_pairs={{0,4},{1,5},{2,6},{3,7},{4,0},{5,1},{6,2},{7,3},{8,12},{9,13},{10,... | collective-permute-start | bytes 393224 | tf_op jit(solution)/shard_map/ppermute | solution.py:255
  54.7 6.6 %collective-permute-start.14 = (bf16[256,256]{1,0:T(8,128)(2,1)S(1)}, bf16[256,256]{1,0:T(8,128)(2,1)S(1)}, u32[]{:S(2)}, u32[]{:S(2)}) collective-permute-start(bf16[256,256]{1,0:T(8,128)(2,1)S(1)} %get-tuple-element.33.refs_0_), channel_id=1, source_target_pairs={{0,6},{1,7},{2,0},{3,1},{4,2},{5,3},{6,4},{7,5},{8,14},{9,15},{10,... | collective-permute-start | bytes 393224 | tf_op jit(solution)/shard_map/ppermute | solution.py:255
  55.7 5.6 %collective-permute-start.15 = (bf16[256,256]{1,0:T(8,128)(2,1)S(1)}, bf16[256,256]{1,0:T(8,128)(2,1)S(1)}, u32[]{:S(2)}, u32[]{:S(2)}) collective-permute-start(bf16[256,256]{1,0:T(8,128)(2,1)S(1)} %get-tuple-element.33.refs_0_), channel_id=1, source_target_pairs={{0,1},{1,0},{2,3},{3,2},{4,5},{5,4},{6,7},{7,6},{8,9},{9,8},{10,11... | collective-permute-start | bytes 393224 | tf_op jit(solution)/shard_map/ppermute | solution.py:258
  55.8 7.2 %collective-permute-start.19 = (bf16[256,256]{1,0:T(8,128)(2,1)S(1)}, bf16[256,256]{1,0:T(8,128)(2,1)S(1)}, u32[]{:S(2)}, u32[]{:S(2)}) collective-permute-start(bf16[256,256]{1,0:T(8,128)(2,1)S(1)} %get-tuple-element.42.refs_1_), channel_id=1, source_target_pairs={{0,2},{1,3},{2,4},{3,5},{4,6},{5,7},{6,0},{7,1},{8,10},{9,11},{10,... | collective-permute-start | bytes 393224 | tf_op jit(solution)/shard_map/ppermute | solution.py:255
  57.4 9.4 %collective-permute-start.20 = (bf16[256,256]{1,0:T(8,128)(2,1)S(1)}, bf16[256,256]{1,0:T(8,128)(2,1)S(1)}, u32[]{:S(2)}, u32[]{:S(2)}) collective-permute-start(bf16[256,256]{1,0:T(8,128)(2,1)S(1)} %get-tuple-element.42.refs_1_), channel_id=1, source_target_pairs={{0,4},{1,5},{2,6},{3,7},{4,0},{5,1},{6,2},{7,3},{8,12},{9,13},{10,... | collective-permute-start | bytes 393224 | tf_op jit(solution)/shard_map/ppermute | solution.py:255
  60.1 6.7 %collective-permute-start.21 = (bf16[256,256]{1,0:T(8,128)(2,1)S(1)}, bf16[256,256]{1,0:T(8,128)(2,1)S(1)}, u32[]{:S(2)}, u32[]{:S(2)}) collective-permute-start(bf16[256,256]{1,0:T(8,128)(2,1)S(1)} %get-tuple-element.42.refs_1_), channel_id=1, source_target_pairs={{0,6},{1,7},{2,0},{3,1},{4,2},{5,3},{6,4},{7,5},{8,14},{9,15},{10,... | collective-permute-start | bytes 393224 | tf_op jit(solution)/shard_map/ppermute | solution.py:255
  61.3 6.0 %collective-permute-start.22 = (bf16[256,256]{1,0:T(8,128)(2,1)S(1)}, bf16[256,256]{1,0:T(8,128)(2,1)S(1)}, u32[]{:S(2)}, u32[]{:S(2)}) collective-permute-start(bf16[256,256]{1,0:T(8,128)(2,1)S(1)} %get-tuple-element.42.refs_1_), channel_id=1, source_target_pairs={{0,1},{1,0},{2,3},{3,2},{4,5},{5,4},{6,7},{7,6},{8,9},{9,8},{10,11... | collective-permute-start | bytes 393224 | tf_op jit(solution)/shard_map/ppermute | solution.py:258
  61.3 6.1 %collective-permute-start.16 = (bf16[256,256]{1,0:T(8,128)(2,1)S(1)}, bf16[256,256]{1,0:T(8,128)(2,1)S(1)}, u32[]{:S(2)}, u32[]{:S(2)}) collective-permute-start(bf16[256,256]{1,0:T(8,128)(2,1)S(1)} %collective-permute-done.12.refs_4_), channel_id=1, source_target_pairs={{0,1},{1,0},{2,3},{3,2},{4,5},{5,4},{6,7},{7,6},{8,9},{9,8},{10,11... | collective-permute-start | bytes 393224 | tf_op jit(solution)/shard_map/ppermute | solution.py:258
  63.0 4.9 %collective-permute-start.17 = (bf16[256,256]{1,0:T(8,128)(2,1)S(1)}, bf16[256,256]{1,0:T(8,128)(2,1)S(1)}, u32[]{:S(2)}, u32[]{:S(2)}) collective-permute-start(bf16[256,256]{1,0:T(8,128)(2,1)S(1)} %collective-permute-done.13.refs_5_), channel_id=1, source_target_pairs={{0,1},{1,0},{2,3},{3,2},{4,5},{5,4},{6,7},{7,6},{8,9},{9,8},{10,11... | collective-permute-start | bytes 393224 | tf_op jit(solution)/shard_map/ppermute | solution.py:258
  66.8 1.3 %collective-permute-start.18 = (bf16[256,256]{1,0:T(8,128)(2,1)S(1)}, bf16[256,256]{1,0:T(8,128)(2,1)S(1)}, u32[]{:S(2)}, u32[]{:S(2)}) collective-permute-start(bf16[256,256]{1,0:T(8,128)(2,1)S(1)} %collective-permute-done.14.refs_6_), channel_id=1, source_target_pairs={{0,1},{1,0},{2,3},{3,2},{4,5},{5,4},{6,7},{7,6},{8,9},{9,8},{10,11... | collective-permute-start | bytes 393224 | tf_op jit(solution)/shard_map/ppermute | solution.py:258
  66.8 1.5 %collective-permute-start.23 = (bf16[256,256]{1,0:T(8,128)(2,1)S(1)}, bf16[256,256]{1,0:T(8,128)(2,1)S(1)}, u32[]{:S(2)}, u32[]{:S(2)}) collective-permute-start(bf16[256,256]{1,0:T(8,128)(2,1)S(1)} %collective-permute-done.19.refs_11_), channel_id=1, source_target_pairs={{0,1},{1,0},{2,3},{3,2},{4,5},{5,4},{6,7},{7,6},{8,9},{9,8},{10,11... | collective-permute-start | bytes 393224 | tf_op jit(solution)/shard_map/ppermute | solution.py:258
  67.3 1.3 %collective-permute-start.24 = (bf16[256,256]{1,0:T(8,128)(2,1)S(1)}, bf16[256,256]{1,0:T(8,128)(2,1)S(1)}, u32[]{:S(2)}, u32[]{:S(2)}) collective-permute-start(bf16[256,256]{1,0:T(8,128)(2,1)S(1)} %collective-permute-done.20.refs_12_), channel_id=1, source_target_pairs={{0,1},{1,0},{2,3},{3,2},{4,5},{5,4},{6,7},{7,6},{8,9},{9,8},{10,11... | collective-permute-start | bytes 393224 | tf_op jit(solution)/shard_map/ppermute | solution.py:258
  67.4 1.4 %collective-permute-start.25 = (bf16[256,256]{1,0:T(8,128)(2,1)S(1)}, bf16[256,256]{1,0:T(8,128)(2,1)S(1)}, u32[]{:S(2)}, u32[]{:S(2)}) collective-permute-start(bf16[256,256]{1,0:T(8,128)(2,1)S(1)} %collective-permute-done.21.refs_13_), channel_id=1, source_target_pairs={{0,1},{1,0},{2,3},{3,2},{4,5},{5,4},{6,7},{7,6},{8,9},{9,8},{10,11... | collective-permute-start | bytes 393224 | tf_op jit(solution)/shard_map/ppermute | solution.py:258

commit v4 on v3

--- a/solution.py
+++ b/solution.py
@@ -29,8 +29,17 @@
 
 
 def lay_out(half, place_ref, piece_ref, scale_ref, *refs):
-    outs, sem = refs[:-1], refs[-1]
-    copies = []
+    outs, (scales, sem, scale_sem) = refs[:-3], refs[-3:]
+    copies, scale_copies = [], []
+    for turn in range(SIDE):
+        part = lax.rem(place_ref[1 - half] + turn, SIDE)
+        first = half * (K // 2 // QB) + part * PART_SCALES
+        first = pl.multiple_of(first, PART_SCALES)
+        copy = pltpu.make_async_copy(
+            scale_ref.at[pl.ds(first, PART_SCALES)], scales.at[turn], scale_sem.at[turn]
+        )
+        copy.start()
+        scale_copies.append(copy)
     for turn in range(SIDE):
         part = lax.rem(place_ref[1 - half] + turn, SIDE)
         first = pl.multiple_of(half * (K // 2) + part * PART, PART)
@@ -40,10 +49,8 @@
         copy.start()
         copies.append(copy)
     for turn in range(SIDE):
-        part = lax.rem(place_ref[1 - half] + turn, SIDE)
-        first = half * (K // 2 // QB) + part * PART_SCALES
-        first = pl.multiple_of(first, PART_SCALES)
-        scale = scale_ref[pl.ds(first, PART_SCALES), :]
+        scale_copies[turn].wait()
+        scale = scales[turn]
         high = scale.astype(BF)
         outs[turn][PART:, :] = jnp.concatenate(
             [high, (scale - high.astype(F32)).astype(BF)], axis=0
@@ -59,12 +66,16 @@
         in_specs=[
             pl.BlockSpec(memory_space=pltpu.SMEM),
             pl.BlockSpec(memory_space=pltpu.HBM),
-            pl.BlockSpec(memory_space=pltpu.VMEM),
+            pl.BlockSpec(memory_space=pltpu.HBM),
         ],
         out_specs=[pl.BlockSpec(memory_space=pltpu.VMEM)] * SIDE,
         out_shape=[shape] * SIDE,
-        scratch_shapes=[pltpu.SemaphoreType.DMA((SIDE,))],
-        compiler_params=pltpu.CompilerParams(vmem_limit_bytes=32 * 2**20),
+        scratch_shapes=[
+            pltpu.VMEM((SIDE, PART_SCALES, COLS), F32),
+            pltpu.SemaphoreType.DMA((SIDE,)),
+            pltpu.SemaphoreType.DMA((SIDE,)),
+        ],
+        compiler_params=pltpu.CompilerParams(vmem_limit_bytes=48 * 2**20),
         cost_estimate=pl.CostEstimate(
             flops=0, bytes_accessed=2 * K * COLS, transcendentals=0
         ),
@@ -127,28 +138,82 @@
     )(*pieces)
 
 
-def tiles(where_ref, *refs):
-    (out_ref, dots, squares), refs = refs[-3:], refs[:-3]
+def stacked(parts):
+    rows = parts[0].shape[0]
+
+    def stack(*refs):
+        for n, ref in enumerate(refs[:-1]):
+            refs[-1][n * rows : (n + 1) * rows, :] = ref[...]
+
+    return pl.pallas_call(
+        stack,
+        in_specs=[pl.BlockSpec(memory_space=pltpu.VMEM)] * len(parts),
+        out_specs=pl.BlockSpec(memory_space=pltpu.VMEM),
+        out_shape=jax.ShapeDtypeStruct((len(parts) * rows, COLS), BF),
+        compiler_params=pltpu.CompilerParams(vmem_limit_bytes=32 * 2**20),
+        cost_estimate=pl.CostEstimate(
+            flops=0, bytes_accessed=4 * len(parts) * rows * COLS, transcendentals=0
+        ),
+    )(*parts)
+
+
+def half_dots(refs, keep):
+    high, low = refs[0][...], refs[1][...]
     contract = (((0,), (0,)), ((), ()))
-    highs, lows, parts = refs[:2], refs[2:4], refs[4:]
-    high = [ref[...] for ref in highs]
-    low = [ref[...] for ref in lows]
-    for n in range(N_EX):
-        dot, square = 0.0, 0.0
-        for half in range(2):
-            part = high[half] if n == 0 else parts[half * (N_EX - 1) + n - 1][...]
-            for own in (high[half], low[half]):
-                dot += lax.dot_general(own, part, contract, preferred_element_type=F32)
+    n = 0
+    for ref in (refs[0], *refs[2:]):
+        for first in range(0, ref.shape[0], QUARTER):
+            part = ref[first : first + QUARTER, :]
+            dot = lax.dot_general(high, part, contract, preferred_element_type=F32)
+            dot += lax.dot_general(low, part, contract, preferred_element_type=F32)
             wide = part.astype(F32)
-            square += jnp.sum(wide * wide, axis=0, keepdims=True)
-        for half in range(BLK_DEV):
-            cut = slice(half * TB, (half + 1) * TB)
-            dots[n * BLK_DEV + half] = dot[:, cut]
-            squares[n * BLK_DEV + half] = jnp.broadcast_to(square[:, cut], (8, TB))
-    own = 0.0
-    for half in range(2):
-        exact = high[half].astype(F32) + low[half].astype(F32)
-        own += jnp.sum(exact * exact, axis=0, keepdims=True)
+            keep(n, dot, jnp.sum(wide * wide, axis=0, keepdims=True))
+            n += 1
+    exact = high.astype(F32) + low.astype(F32)
+    return jnp.sum(exact * exact, axis=0, keepdims=True)
+
+
+def first_tiles(*refs):
+    refs, (dots, squares) = refs[:-2], refs[-2:]
+
+    def keep(n, dot, square):
+        for b in range(BLK_DEV):
+            dots[n * BLK_DEV + b] = dot[:, b * TB : (b + 1) * TB]
+        squares[n : n + 1, :] = square
+
+    own = half_dots(refs, keep)
+    squares[N_EX:, :] = jnp.broadcast_to(own, (N_EX, COLS))
+
+
+def first_dots(parts):
+    return pl.pallas_call(
+        first_tiles,
+        in_specs=[pl.BlockSpec(memory_space=pltpu.VMEM)] * len(parts),
+        out_specs=[pl.BlockSpec(memory_space=pltpu.VMEM)] * 2,
+        out_shape=[
+            jax.ShapeDtypeStruct((N_EX * BLK_DEV, COLS, TB), F32),
+            jax.ShapeDtypeStruct((2 * N_EX, COLS), F32),
+        ],
+        compiler_params=pltpu.CompilerParams(vmem_limit_bytes=32 * 2**20),
+        cost_estimate=pl.CostEstimate(
+            flops=2 * SLICE * COLS * COLS * N_EX,
+            bytes_accessed=SLICE * COLS * 9 + 4 * N_EX * COLS * COLS,
+            transcendentals=0,
+        ),
+    )(*parts)
+
+
+def tiles(where_ref, dots_ref, squares_ref, *refs):
+    refs, (out_ref, dots, squares) = refs[:-3], refs[-3:]
+
+    def keep(n, dot, square):
+        square += squares_ref[n : n + 1, :]
+        for b in range(BLK_DEV):
+            cut = slice(b * TB, (b + 1) * TB)
+            dots[n * BLK_DEV + b] = dot[:, cut] + dots_ref[n * BLK_DEV + b]
+            squares[n * BLK_DEV + b] = jnp.broadcast_to(square[:, cut], (8, TB))
+
+    own = half_dots(refs, keep) + squares_ref[N_EX : N_EX + 1, :]
     for b in range(BLK_DEV):
         rows = slice(b * TB, (b + 1) * TB)
         aux = []
@@ -166,11 +231,11 @@
             out_ref[b * TB + i * ROWS : b * TB + (i + 1) * ROWS, WIDE:] = both
 
 
-def partial_tiles(where, highs, lows, parts):
+def partial_tiles(where, dots, squares, parts):
     return pl.pallas_call(
         tiles,
         in_specs=[pl.BlockSpec(memory_space=pltpu.SMEM)]
-        + [pl.BlockSpec(memory_space=pltpu.VMEM)] * (4 + len(parts)),
+        + [pl.BlockSpec(memory_space=pltpu.VMEM)] * (2 + len(parts)),
         out_specs=pl.BlockSpec(memory_space=pltpu.VMEM),
         out_shape=jax.ShapeDtypeStruct((COLS, WIDE + AUX), BF),
         scratch_shapes=[
@@ -179,11 +244,11 @@
         ],
         compiler_params=pltpu.CompilerParams(vmem_limit_bytes=32 * 2**20),
         cost_estimate=pl.CostEstimate(
-            flops=4 * SLICE * COLS * COLS * N_EX,
-            bytes_accessed=2 * SLICE * COLS * 9 + 2 * COLS * (WIDE + AUX),
+            flops=2 * SLICE * COLS * COLS * N_EX,
+            bytes_accessed=SLICE * COLS * 9 + 4 * N_EX * COLS * COLS,
             transcendentals=0,
         ),
-    )(where, *highs, *lows, *parts)
+    )(where, dots, squares, *parts)
 
 
 def finish(me_ref, sums_ref, out_ref):
@@ -233,7 +298,8 @@
     holder, half = partner // BLK_DEV, partner % BLK_DEV
     turn = (ex // 2 - holder // 2) % (N_EX // 2)
     other = (holder % 2) != (ex % 2)
-    part = turn + jnp.where(other, N_EX // 2, 0)
+    part = turn ^ (turn >> 1)
+    part = part + jnp.where(other, N_EX // 2, 0)
     return (part * BLK_DEV + half).reshape(-1).astype(jnp.int32)
 
 
@@ -257,16 +323,22 @@
     )
     swap = lambda a: lax.ppermute(a, "ex", [(e, e ^ 1) for e in range(N_EX)])
 
-    highs, lows, others = [], [], []
+    parts = []
     for half in range(2):
-        parts = laid_out(half, place, partials[0], scales[0])
-        parts = summed_first(half, place, exchanged(parts, 1 - half))
-        high, low = summed_second(exchanged(parts, half))
-        same = [around(high, d) for d in (1, 2, 3)]
-        highs.append(high)
-        lows.append(low)
-        others += [*same, *(swap(a) for a in (high, *same))]
-    sums = partial_tiles(where, highs, lows, others)
+        pieces = laid_out(half, place, partials[0], scales[0])
+        pieces = summed_first(half, place, exchanged(pieces, 1 - half))
+        high, low = summed_second(exchanged(pieces, half))
+        right, left = around(high, 1), around(high, -1)
+        if half == 0:
+            far = around(right, 1)
+            swapped = [swap(stacked([high, right, left, far]))]
+        else:
+            near = swap(stacked([high, right, left]))
+            far = around(left, -1)
+            swapped = [near, swap(far)]
+        parts.append([high, low, right, left, far, *swapped])
+    dots, squares = first_dots(parts[0])
+    sums = partial_tiles(where, dots, squares, parts[1])
 
     across = lambda a: lax.all_to_all(a, "layer", 0, 0, tiled=True)
     sums = across(sums.reshape(LAYERS, ROWS, WIDE + AUX))

time: 108 us -> 113 us (1.046)
  waiting for transfers between devices: 24.7 us -> 36.5 us
  starting transfers between devices: 36.9 us -> 28.5 us
  Pallas kernels: 5.65 us -> 8.9 us
  local copies, waits for them, and re-layouts: 3.42 us -> 1.23 us
    ppermute x6, waiting for transfers between devices: 5.21 us -> 14.3 us  [on_device(): lax.ppermute(a, 'ex', [(e, (e + 2 * d) % N_EX) for e in range(N_EX)])]
    ppermute x6, starting transfers between devices: 11.5 us -> 7.57 us  [on_device(): lax.ppermute(a, 'ex', [(e, (e + 2 * d) % N_EX) for e in range(N_EX)])]
    ppermute x12, waiting for transfers between devices: 18.5 us -> 21.6 us  [along(): lax.ppermute(a, 'layer', [(n, y * SIDE + x) for n, (y, x) in enumerate(to)])]
    ppermute x12, starting transfers between devices: 23.8 us -> 20.8 us  [along(): lax.ppermute(a, 'layer', [(n, y * SIDE + x) for n, (y, x) in enumerate(to)])]
    pallas_call x2, Pallas kernels: 1.55 us -> 4.5 us  [laid_out(): pl.pallas_call(functools.partial(lay_out, half), in_specs=[pl.BlockSpec(m...]
    unnamed x6 -> x4, local copies, waits for them, and re-layouts: 3.1 us -> 0.91 us
    ppermute x8 -> x3, starting transfers between devices: 1.54 us -> 0.17 us  [on_device(): swap = lambda a: lax.ppermute(a, 'ex', [(e, e ^ 1) for e in range(N_EX)])]
  transfers between devices with their start and end apart: 26 -> 21, of which waited for: 11 -> 10; matrix products, arithmetic and copies ran while one was open for 0% -> 0% of each run, Pallas kernels for 3% -> 4%
where the time goes in v4:
time: 113 us
  waiting for transfers between devices  36.5 us (32%)
  blocking collectives  36.3 us (32%)
  starting transfers between devices  28.5 us (25%)
  Pallas kernels  8.9 us (8%)
  other arithmetic  1.39 us (1%)
  local copies, waits for them, and re-layouts  1.23 us (1%)
    all_to_all x2, blocking collectives, on_device(): across = lambda a: lax.all_to_all(a, 'layer', 0, 0, tiled=True)  36.3 us
    ppermute x12, waiting for transfers between devices, along(): lax.ppermute(a, 'layer', [(n, y * SIDE + x) for n, (y, x) in enumerate(to)])  21.6 us
    ppermute x12, starting transfers between devices, along(): lax.ppermute(a, 'layer', [(n, y * SIDE + x) for n, (y, x) in enumerate(to)])  20.8 us
    ppermute x6, waiting for transfers between devices, on_device(): lax.ppermute(a, 'ex', [(e, (e + 2 * d) % N_EX) for e in range(N_EX)])  14.3 us
    ppermute x6, starting transfers between devices, on_device(): lax.ppermute(a, 'ex', [(e, (e + 2 * d) % N_EX) for e in range(N_EX)])  7.57 us
    pallas_call x2, Pallas kernels, laid_out(): pl.pallas_call(functools.partial(lay_out, half), in_specs=[pl.BlockSpec(m...  4.5 us
  transfers between devices with their start and end apart: 21, of which 10 were waited for; matrix products, arithmetic and copies ran while one was open for 0% of the time, Pallas kernels for 4%

profile of v4, /device:TPU:0, one launch (start us, length us, event | category | flops | bytes accessed | tf_op | source)
XLA Modules:
  0.0 113.1 jit_solution(2779756099203811749)
XLA Ops:
  0.0 0.1 pad_add_fusion.place_ref
  0.1 0.0 copy-start
  0.1 0.9 copy-done
  1.0 2.2 %shard_map.37 = (bf16[1056,256]{1,0:T(8,128)(2,1)S(1)}, bf16[1056,256]{1,0:T(8,128)(2,1)S(1)}, bf16[1056,256]{1,0:T(8,128)(2,1)S(1)}, bf16[1056,256]{1,0:T(8,128)(2,1)S(1)}) custom-call(s32[2]{0:T(128)S(1)} %pad_add_fusion.place_ref, bf16[8192,256]{1,0:T(8,128)(2,1)} %bitcast.16, f32[128,256]{1,0:T(8,128)S(1)} %bitcast.14), custom_call_target="tpu_custom_call" | custom-call | bytes 4194304 | tf_op jit(solution)/shard_map/pallas_call | solution.py:64
  3.2 1.6 %collective-permute-start = (bf16[1056,256]{1,0:T(8,128)(2,1)S(1)}, bf16[1056,256]{1,0:T(8,128)(2,1)S(1)}, u32[]{:S(2)}, u32[]{:S(2)}) collective-permute-start(bf16[1056,256]{1,0:T(8,128)(2,1)S(1)} %get-tuple-element.28), channel_id=1, source_target_pairs={{0,8},{8,16},{16,24},{24,0},{32,40},{40,48},{48,56},{56,32},{64,72... | collective-permute-start | bytes 1622024 | tf_op jit(solution)/shard_map/ppermute | solution.py:316
  4.9 2.7 %collective-permute-start.1 = (bf16[1056,256]{1,0:T(8,128)(2,1)S(1)}, bf16[1056,256]{1,0:T(8,128)(2,1)S(1)}, u32[]{:S(2)}, u32[]{:S(2)}) collective-permute-start(bf16[1056,256]{1,0:T(8,128)(2,1)S(1)} %get-tuple-element.29), channel_id=1, source_target_pairs={{0,16},{8,24},{16,0},{24,8},{32,48},{40,56},{48,32},{56,40},{64,80... | collective-permute-start | bytes 1622024 | tf_op jit(solution)/shard_map/ppermute | solution.py:316
  7.6 1.4 %collective-permute-start.2 = (bf16[1056,256]{1,0:T(8,128)(2,1)S(1)}, bf16[1056,256]{1,0:T(8,128)(2,1)S(1)}, u32[]{:S(2)}, u32[]{:S(2)}) collective-permute-start(bf16[1056,256]{1,0:T(8,128)(2,1)S(1)} %get-tuple-element.30), channel_id=1, source_target_pairs={{0,24},{8,0},{16,8},{24,16},{32,56},{40,32},{48,40},{56,48},{64,88... | collective-permute-start | bytes 1622024 | tf_op jit(solution)/shard_map/ppermute | solution.py:316
  9.0 2.3 %shard_map.42 = (bf16[1056,256]{1,0:T(8,128)(2,1)S(1)}, bf16[1056,256]{1,0:T(8,128)(2,1)S(1)}, bf16[1056,256]{1,0:T(8,128)(2,1)S(1)}, bf16[1056,256]{1,0:T(8,128)(2,1)S(1)}) custom-call(s32[2]{0:T(128)S(1)} %pad_add_fusion.place_ref, bf16[8192,256]{1,0:T(8,128)(2,1)} %bitcast.17, f32[128,256]{1,0:T(8,128)S(1)} %bitcast.15), custom_call_target="tpu_custom_call" | custom-call | bytes 4194304 | tf_op jit(solution)/shard_map/pallas_call | solution.py:64
  11.3 1.6 %collective-permute-start.10 = (bf16[1056,256]{1,0:T(8,128)(2,1)S(1)}, bf16[1056,256]{1,0:T(8,128)(2,1)S(1)}, u32[]{:S(2)}, u32[]{:S(2)}) collective-permute-start(bf16[1056,256]{1,0:T(8,128)(2,1)S(1)} %get-tuple-element.40), channel_id=1, source_target_pairs={{0,32},{8,40},{16,48},{24,56},{32,64},{40,72},{48,80},{56,88},{64,... | collective-permute-start | bytes 1622024 | tf_op jit(solution)/shard_map/ppermute | solution.py:316
  12.9 2.9 %collective-permute-start.11 = (bf16[1056,256]{1,0:T(8,128)(2,1)S(1)}, bf16[1056,256]{1,0:T(8,128)(2,1)S(1)}, u32[]{:S(2)}, u32[]{:S(2)}) collective-permute-start(bf16[1056,256]{1,0:T(8,128)(2,1)S(1)} %get-tuple-element.41), channel_id=1, source_target_pairs={{0,64},{8,72},{16,80},{24,88},{32,96},{40,104},{48,112},{56,120},{... | collective-permute-start | bytes 1622024 | tf_op jit(solution)/shard_map/ppermute | solution.py:316
  15.8 2.6 %collective-permute-done.refs_1_ = bf16[1056,256]{1,0:T(8,128)(2,1)S(1)} collective-permute-done((bf16[1056,256]{1,0:T(8,128)(2,1)S(1)}, bf16[1056,256]{1,0:T(8,128)(2,1)S(1)}, u32[]{:S(2)}, u32[]{:S(2)}) %collective-permute-start) | collective-permute-done | bytes 540704 | tf_op jit(solution)/shard_map/ppermute | solution.py:316
  18.4 3.4 %collective-permute-start.12 = (bf16[1056,256]{1,0:T(8,128)(2,1)S(1)}, bf16[1056,256]{1,0:T(8,128)(2,1)S(1)}, u32[]{:S(2)}, u32[]{:S(2)}) collective-permute-start(bf16[1056,256]{1,0:T(8,128)(2,1)S(1)} %get-tuple-element.42), channel_id=1, source_target_pairs={{0,96},{8,104},{16,112},{24,120},{32,0},{40,8},{48,16},{56,24},{64... | collective-permute-start | bytes 1622024 | tf_op jit(solution)/shard_map/ppermute | solution.py:316
  21.8 9.4 %collective-permute-done.1.refs_2_ = bf16[1056,256]{1,0:T(8,128)(2,1)S(1)} collective-permute-done((bf16[1056,256]{1,0:T(8,128)(2,1)S(1)}, bf16[1056,256]{1,0:T(8,128)(2,1)S(1)}, u32[]{:S(2)}, u32[]{:S(2)}) %collective-permute-start.1) | collective-permute-done | bytes 540704 | tf_op jit(solution)/shard_map/ppermute | solution.py:316
  31.2 0.0 collective-permute-done.2.refs_3_
  31.2 0.9 shard_map.38
  32.1 0.0 copy-start.1
  32.1 1.6 %collective-permute-start.3 = (f32[256,256]{1,0:T(8,128)S(1)}, f32[256,256]{1,0:T(8,128)S(1)}, u32[]{:S(2)}, u32[]{:S(2)}) collective-permute-start(f32[256,256]{1,0:T(8,128)S(1)} %get-tuple-element.32), channel_id=1, source_target_pairs={{0,32},{8,40},{16,48},{24,56},{32,64},{40,72},{48,80},{56,88},{64,... | collective-permute-start | bytes 786440 | tf_op jit(solution)/shard_map/ppermute | solution.py:316
  33.8 2.9 %collective-permute-start.4 = (f32[256,256]{1,0:T(8,128)S(1)}, f32[256,256]{1,0:T(8,128)S(1)}, u32[]{:S(2)}, u32[]{:S(2)}) collective-permute-start(f32[256,256]{1,0:T(8,128)S(1)} %get-tuple-element.33), channel_id=1, source_target_pairs={{0,64},{8,72},{16,80},{24,88},{32,96},{40,104},{48,112},{56,120},{... | collective-permute-start | bytes 786440 | tf_op jit(solution)/shard_map/ppermute | solution.py:316
  36.7 0.0 collective-permute-done.10.refs_1_
  36.7 1.3 %collective-permute-start.5 = (f32[256,256]{1,0:T(8,128)S(1)}, f32[256,256]{1,0:T(8,128)S(1)}, u32[]{:S(2)}, u32[]{:S(2)}) collective-permute-start(f32[256,256]{1,0:T(8,128)S(1)} %get-tuple-element.34), channel_id=1, source_target_pairs={{0,96},{8,104},{16,112},{24,120},{32,0},{40,8},{48,16},{56,24},{64... | collective-permute-start | bytes 786440 | tf_op jit(solution)/shard_map/ppermute | solution.py:316
  38.0 2.6 %collective-permute-done.11.refs_2_ = bf16[1056,256]{1,0:T(8,128)(2,1)S(1)} collective-permute-done((bf16[1056,256]{1,0:T(8,128)(2,1)S(1)}, bf16[1056,256]{1,0:T(8,128)(2,1)S(1)}, u32[]{:S(2)}, u32[]{:S(2)}) %collective-permute-start.11) | collective-permute-done | bytes 540704 | tf_op jit(solution)/shard_map/ppermute | solution.py:316
  40.6 0.0 collective-permute-done.12.refs_3_
  40.6 0.9 shard_map.43
  41.6 0.1 collective-permute-start.13
  41.6 1.1 collective-permute-start.14
  42.8 3.5 %collective-permute-done.3.refs_1_ = f32[256,256]{1,0:T(8,128)S(1)} collective-permute-done((f32[256,256]{1,0:T(8,128)S(1)}, f32[256,256]{1,0:T(8,128)S(1)}, u32[]{:S(2)}, u32[]{:S(2)}) %collective-permute-start.3) | collective-permute-done | bytes 262176 | tf_op jit(solution)/shard_map/ppermute | solution.py:316
  46.2 0.0 collective-permute-start.15
  46.2 3.6 %collective-permute-done.4.refs_2_ = f32[256,256]{1,0:T(8,128)S(1)} collective-permute-done((f32[256,256]{1,0:T(8,128)S(1)}, f32[256,256]{1,0:T(8,128)S(1)}, u32[]{:S(2)}, u32[]{:S(2)}) %collective-permute-start.4) | collective-permute-done | bytes 262176 | tf_op jit(solution)/shard_map/ppermute | solution.py:316
  49.8 0.0 collective-permute-done.5.refs_3_
  49.8 0.1 shard_map.39
  49.9 2.0 %collective-permute-start.6 = (bf16[256,256]{1,0:T(8,128)(2,1)S(1)}, bf16[256,256]{1,0:T(8,128)(2,1)S(1)}, u32[]{:S(2)}, u32[]{:S(2)}) collective-permute-start(bf16[256,256]{1,0:T(8,128)(2,1)S(1)} %get-tuple-element.35.refs_0_), channel_id=1, source_target_pairs={{0,2},{1,3},{2,4},{3,5},{4,6},{5,7},{6,0},{7,1},{8,10},{9,11},{10,... | collective-permute-start | bytes 393224 | tf_op jit(solution)/shard_map/ppermute | solution.py:321
  51.9 2.2 %collective-permute-start.7 = (bf16[256,256]{1,0:T(8,128)(2,1)S(1)}, bf16[256,256]{1,0:T(8,128)(2,1)S(1)}, u32[]{:S(2)}, u32[]{:S(2)}) collective-permute-start(bf16[256,256]{1,0:T(8,128)(2,1)S(1)} %get-tuple-element.35.refs_0_), channel_id=1, source_target_pairs={{0,6},{1,7},{2,0},{3,1},{4,2},{5,3},{6,4},{7,5},{8,14},{9,15},{10,... | collective-permute-start | bytes 393224 | tf_op jit(solution)/shard_map/ppermute | solution.py:321
  54.1 2.9 %collective-permute-done.6.refs_1_.refs_2_ = bf16[256,256]{1,0:T(8,128)(2,1)S(1)} collective-permute-done((bf16[256,256]{1,0:T(8,128)(2,1)S(1)}, bf16[256,256]{1,0:T(8,128)(2,1)S(1)}, u32[]{:S(2)}, u32[]{:S(2)}) %collective-permute-start.6) | collective-permute-done | bytes 131104 | tf_op jit(solution)/shard_map/ppermute | solution.py:321
  57.0 0.0 collective-permute-start.8
  57.0 0.0 copy-done.1
  57.0 0.1 reshape.22
  57.1 0.0 collective-permute-done.13.refs_1_
  57.1 0.0 collective-permute-done.14.refs_2_
  57.1 0.0 collective-permute-done.15.refs_3_
  57.1 0.1 shard_map.44
  57.2 3.3 %collective-permute-start.17 = (bf16[256,256]{1,0:T(8,128)(2,1)S(1)}, bf16[256,256]{1,0:T(8,128)(2,1)S(1)}, u32[]{:S(2)}, u32[]{:S(2)}) collective-permute-start(bf16[256,256]{1,0:T(8,128)(2,1)S(1)} %get-tuple-element.47.refs_0_), channel_id=1, source_target_pairs={{0,6},{1,7},{2,0},{3,1},{4,2},{5,3},{6,4},{7,5},{8,14},{9,15},{10,... | collective-permute-start | bytes 393224 | tf_op jit(solution)/shard_map/ppermute | solution.py:321
  60.5 0.0 collective-permute-start.16
  60.5 0.0 collective-permute-done.7.refs_2_.refs_3_
  60.5 3.5 %collective-permute-done.8.refs_3_.refs_4_ = bf16[256,256]{1,0:T(8,128)(2,1)S(1)} collective-permute-done((bf16[256,256]{1,0:T(8,128)(2,1)S(1)}, bf16[256,256]{1,0:T(8,128)(2,1)S(1)}, u32[]{:S(2)}, u32[]{:S(2)}) %collective-permute-start.8) | collective-permute-done | bytes 131104 | tf_op jit(solution)/shard_map/ppermute | solution.py:321
  64.0 0.1 collective-permute-start.9
  64.1 0.0 collective-permute-done.17.refs_2_.refs_3_
  64.1 2.5 %collective-permute-done.16.refs_1_.refs_2_ = bf16[256,256]{1,0:T(8,128)(2,1)S(1)} collective-permute-done((bf16[256,256]{1,0:T(8,128)(2,1)S(1)}, bf16[256,256]{1,0:T(8,128)(2,1)S(1)}, u32[]{:S(2)}, u32[]{:S(2)}) %collective-permute-start.16) | collective-permute-done | bytes 131104 | tf_op jit(solution)/shard_map/ppermute | solution.py:321
  66.7 0.1 collective-permute-start.19
  66.8 0.1 collective-permute-start.18
  66.9 0.1 copy.10
  67.0 0.1 copy.11
  67.0 0.1 add_reduce_fusion
  67.1 0.1 reduce_sum.12
  67.2 5.5 %collective-permute-done.18.refs_4_ = bf16[256,256]{1,0:T(8,128)(2,1)S(1)} collective-permute-done((bf16[256,256]{1,0:T(8,128)(2,1)S(1)}, bf16[256,256]{1,0:T(8,128)(2,1)S(1)}, u32[]{:S(2)}, u32[]{:S(2)}) %collective-permute-start.18) | collective-permute-done | bytes 131104 | tf_op jit(solution)/shard_map/ppermute | solution.py:321
  72.7 0.0 collective-permute-start.20
  72.7 0.0 collective-permute-done.9.refs_5_
  72.7 0.8 shard_map.41
  73.5 0.5 collective-permute-done.20.refs_6_
  74.0 0.0 collective-permute-done.19.refs_5_
  74.0 1.4 %shard_map.46 = bf16[256,1536]{1,0:T(8,128)(2,1)S(1)} custom-call(s32[20]{0:T(128)S(1)} %fusion.where_ref, f32[16,256,128]{2,1,0:T(8,128)S(1)} %get-tuple-element.37.dots_ref, f32[16,256]{1,0:T(8,128)S(1)} %get-tuple-element.38.squares_ref, bf16[256,256]{1,0:T(8,128)(2,1)S(1)} %get-tuple-element.47.refs_0_, bf16[256,256]{1,0:T(8,128)(2,1)S(1)} %get-tuple-element.48.refs_1_, ...), custom_call_target="tpu_custom_call" | custom-call | flops 536870912 | bytes 3276800 | tf_op jit(solution)/shard_map/pallas_call | solution.py:235
  75.4 20.8 %all_to_all.10.sums_ref = bf16[16,16,1536]{2,1,0:T(8,128)(2,1)S(1)} all-to-all(bf16[16,16,1536]{2,1,0:T(8,128)(2,1)S(1)} %bitcast.13), channel_id=1, replica_groups=mesh['layer'=16,'ex'=8] {'layer'}, dimensions={0} | all-to-all | bytes 1572864 | tf_op jit(solution)/shard_map/all_to_all | solution.py:343
  96.2 0.2 shard_map.47
  96.4 15.5 %all_to_all.11 = bf16[16,16,1280]{2,1,0:T(8,128)(2,1)S(1)} all-to-all(bf16[16,16,1280]{2,1,0:T(8,128)(2,1)S(1)} %shard_map.47), channel_id=1, replica_groups=mesh['layer'=16,'ex'=8] {'layer'}, dimensions={0} | all-to-all | bytes 1310720 | tf_op jit(solution)/shard_map/all_to_all | solution.py:343
  111.9 1.2 %bitcast_convert_fusion = f32[256,1280]{1,0:T(8,128)} fusion(bf16[16,16,1280]{2,1,0:T(8,128)(2,1)S(1)} %all_to_all.11), kind=kLoop, calls=%fused_computation | loop fusion | flops 327680 | bytes 1966080 | tf_op jit(solution)/shard_map/convert_element_type | solution.py:346
  (5 shorter events, 0.1 us)
Async XLA Ops:
  0.1 0.9 copy-start
  3.2 15.2 %collective-permute-start = (bf16[1056,256]{1,0:T(8,128)(2,1)S(1)}, bf16[1056,256]{1,0:T(8,128)(2,1)S(1)}, u32[]{:S(2)}, u32[]{:S(2)}) collective-permute-start(bf16[1056,256]{1,0:T(8,128)(2,1)S(1)} %get-tuple-element.28), channel_id=1, source_target_pairs={{0,8},{8,16},{16,24},{24,0},{32,40},{40,48},{48,56},{56,32},{64,72... | collective-permute-start | bytes 1622024 | tf_op jit(solution)/shard_map/ppermute | solution.py:316
  4.9 26.3 %collective-permute-start.1 = (bf16[1056,256]{1,0:T(8,128)(2,1)S(1)}, bf16[1056,256]{1,0:T(8,128)(2,1)S(1)}, u32[]{:S(2)}, u32[]{:S(2)}) collective-permute-start(bf16[1056,256]{1,0:T(8,128)(2,1)S(1)} %get-tuple-element.29), channel_id=1, source_target_pairs={{0,16},{8,24},{16,0},{24,8},{32,48},{40,56},{48,32},{56,40},{64,80... | collective-permute-start | bytes 1622024 | tf_op jit(solution)/shard_map/ppermute | solution.py:316
  7.6 23.6 %collective-permute-start.2 = (bf16[1056,256]{1,0:T(8,128)(2,1)S(1)}, bf16[1056,256]{1,0:T(8,128)(2,1)S(1)}, u32[]{:S(2)}, u32[]{:S(2)}) collective-permute-start(bf16[1056,256]{1,0:T(8,128)(2,1)S(1)} %get-tuple-element.30), channel_id=1, source_target_pairs={{0,24},{8,0},{16,8},{24,16},{32,56},{40,32},{48,40},{56,48},{64,88... | collective-permute-start | bytes 1622024 | tf_op jit(solution)/shard_map/ppermute | solution.py:316
  11.3 25.4 %collective-permute-start.10 = (bf16[1056,256]{1,0:T(8,128)(2,1)S(1)}, bf16[1056,256]{1,0:T(8,128)(2,1)S(1)}, u32[]{:S(2)}, u32[]{:S(2)}) collective-permute-start(bf16[1056,256]{1,0:T(8,128)(2,1)S(1)} %get-tuple-element.40), channel_id=1, source_target_pairs={{0,32},{8,40},{16,48},{24,56},{32,64},{40,72},{48,80},{56,88},{64,... | collective-permute-start | bytes 1622024 | tf_op jit(solution)/shard_map/ppermute | solution.py:316
  12.9 27.7 %collective-permute-start.11 = (bf16[1056,256]{1,0:T(8,128)(2,1)S(1)}, bf16[1056,256]{1,0:T(8,128)(2,1)S(1)}, u32[]{:S(2)}, u32[]{:S(2)}) collective-permute-start(bf16[1056,256]{1,0:T(8,128)(2,1)S(1)} %get-tuple-element.41), channel_id=1, source_target_pairs={{0,64},{8,72},{16,80},{24,88},{32,96},{40,104},{48,112},{56,120},{... | collective-permute-start | bytes 1622024 | tf_op jit(solution)/shard_map/ppermute | solution.py:316
  18.4 22.2 %collective-permute-start.12 = (bf16[1056,256]{1,0:T(8,128)(2,1)S(1)}, bf16[1056,256]{1,0:T(8,128)(2,1)S(1)}, u32[]{:S(2)}, u32[]{:S(2)}) collective-permute-start(bf16[1056,256]{1,0:T(8,128)(2,1)S(1)} %get-tuple-element.42), channel_id=1, source_target_pairs={{0,96},{8,104},{16,112},{24,120},{32,0},{40,8},{48,16},{56,24},{64... | collective-permute-start | bytes 1622024 | tf_op jit(solution)/shard_map/ppermute | solution.py:316
  32.1 24.9 %copy-start.1 = (s32[80,3]{0,1:T(4,128)S(1)}, s32[80,3]{0,1:T(4,128)}, u32[]{:S(2)}) copy-start(s32[80,3]{0,1:T(4,128)} %param.5) | copy-start | bytes 2884
  32.1 14.1 %collective-permute-start.3 = (f32[256,256]{1,0:T(8,128)S(1)}, f32[256,256]{1,0:T(8,128)S(1)}, u32[]{:S(2)}, u32[]{:S(2)}) collective-permute-start(f32[256,256]{1,0:T(8,128)S(1)} %get-tuple-element.32), channel_id=1, source_target_pairs={{0,32},{8,40},{16,48},{24,56},{32,64},{40,72},{48,80},{56,88},{64,... | collective-permute-start | bytes 786440 | tf_op jit(solution)/shard_map/ppermute | solution.py:316
  33.8 16.0 %collective-permute-start.4 = (f32[256,256]{1,0:T(8,128)S(1)}, f32[256,256]{1,0:T(8,128)S(1)}, u32[]{:S(2)}, u32[]{:S(2)}) collective-permute-start(f32[256,256]{1,0:T(8,128)S(1)} %get-tuple-element.33), channel_id=1, source_target_pairs={{0,64},{8,72},{16,80},{24,88},{32,96},{40,104},{48,112},{56,120},{... | collective-permute-start | bytes 786440 | tf_op jit(solution)/shard_map/ppermute | solution.py:316
  36.7 13.1 %collective-permute-start.5 = (f32[256,256]{1,0:T(8,128)S(1)}, f32[256,256]{1,0:T(8,128)S(1)}, u32[]{:S(2)}, u32[]{:S(2)}) collective-permute-start(f32[256,256]{1,0:T(8,128)S(1)} %get-tuple-element.34), channel_id=1, source_target_pairs={{0,96},{8,104},{16,112},{24,120},{32,0},{40,8},{48,16},{56,24},{64... | collective-permute-start | bytes 786440 | tf_op jit(solution)/shard_map/ppermute | solution.py:316
  41.6 15.5 %collective-permute-start.13 = (f32[256,256]{1,0:T(8,128)S(1)}, f32[256,256]{1,0:T(8,128)S(1)}, u32[]{:S(2)}, u32[]{:S(2)}) collective-permute-start(f32[256,256]{1,0:T(8,128)S(1)} %get-tuple-element.44), channel_id=1, source_target_pairs={{0,8},{8,16},{16,24},{24,0},{32,40},{40,48},{48,56},{56,32},{64,72... | collective-permute-start | bytes 786440 | tf_op jit(solution)/shard_map/ppermute | solution.py:316
  41.6 15.4 %collective-permute-start.14 = (f32[256,256]{1,0:T(8,128)S(1)}, f32[256,256]{1,0:T(8,128)S(1)}, u32[]{:S(2)}, u32[]{:S(2)}) collective-permute-start(f32[256,256]{1,0:T(8,128)S(1)} %get-tuple-element.45), channel_id=1, source_target_pairs={{0,16},{8,24},{16,0},{24,8},{32,48},{40,56},{48,32},{56,40},{64,80... | collective-permute-start | bytes 786440 | tf_op jit(solution)/shard_map/ppermute | solution.py:316
  46.2 10.8 %collective-permute-start.15 = (f32[256,256]{1,0:T(8,128)S(1)}, f32[256,256]{1,0:T(8,128)S(1)}, u32[]{:S(2)}, u32[]{:S(2)}) collective-permute-start(f32[256,256]{1,0:T(8,128)S(1)} %get-tuple-element.46), channel_id=1, source_target_pairs={{0,24},{8,0},{16,8},{24,16},{32,56},{40,32},{48,40},{56,48},{64,88... | collective-permute-start | bytes 786440 | tf_op jit(solution)/shard_map/ppermute | solution.py:316
  49.9 7.1 %collective-permute-start.6 = (bf16[256,256]{1,0:T(8,128)(2,1)S(1)}, bf16[256,256]{1,0:T(8,128)(2,1)S(1)}, u32[]{:S(2)}, u32[]{:S(2)}) collective-permute-start(bf16[256,256]{1,0:T(8,128)(2,1)S(1)} %get-tuple-element.35.refs_0_), channel_id=1, source_target_pairs={{0,2},{1,3},{2,4},{3,5},{4,6},{5,7},{6,0},{7,1},{8,10},{9,11},{10,... | collective-permute-start | bytes 393224 | tf_op jit(solution)/shard_map/ppermute | solution.py:321
  51.9 8.6 %collective-permute-start.7 = (bf16[256,256]{1,0:T(8,128)(2,1)S(1)}, bf16[256,256]{1,0:T(8,128)(2,1)S(1)}, u32[]{:S(2)}, u32[]{:S(2)}) collective-permute-start(bf16[256,256]{1,0:T(8,128)(2,1)S(1)} %get-tuple-element.35.refs_0_), channel_id=1, source_target_pairs={{0,6},{1,7},{2,0},{3,1},{4,2},{5,3},{6,4},{7,5},{8,14},{9,15},{10,... | collective-permute-start | bytes 393224 | tf_op jit(solution)/shard_map/ppermute | solution.py:321
  57.0 7.0 %collective-permute-start.8 = (bf16[256,256]{1,0:T(8,128)(2,1)S(1)}, bf16[256,256]{1,0:T(8,128)(2,1)S(1)}, u32[]{:S(2)}, u32[]{:S(2)}) collective-permute-start(bf16[256,256]{1,0:T(8,128)(2,1)S(1)} %collective-permute-done.6.refs_1_.refs_2_), channel_id=1, source_target_pairs={{0,2},{1,3},{2,4},{3,5},{4,6},{5,7},{6,0},{7,1},{8,10},{9,11},{10,... | collective-permute-start | bytes 393224 | tf_op jit(solution)/shard_map/ppermute | solution.py:321
  57.2 7.0 %collective-permute-start.17 = (bf16[256,256]{1,0:T(8,128)(2,1)S(1)}, bf16[256,256]{1,0:T(8,128)(2,1)S(1)}, u32[]{:S(2)}, u32[]{:S(2)}) collective-permute-start(bf16[256,256]{1,0:T(8,128)(2,1)S(1)} %get-tuple-element.47.refs_0_), channel_id=1, source_target_pairs={{0,6},{1,7},{2,0},{3,1},{4,2},{5,3},{6,4},{7,5},{8,14},{9,15},{10,... | collective-permute-start | bytes 393224 | tf_op jit(solution)/shard_map/ppermute | solution.py:321
  60.5 6.2 %collective-permute-start.16 = (bf16[256,256]{1,0:T(8,128)(2,1)S(1)}, bf16[256,256]{1,0:T(8,128)(2,1)S(1)}, u32[]{:S(2)}, u32[]{:S(2)}) collective-permute-start(bf16[256,256]{1,0:T(8,128)(2,1)S(1)} %get-tuple-element.47.refs_0_), channel_id=1, source_target_pairs={{0,2},{1,3},{2,4},{3,5},{4,6},{5,7},{6,0},{7,1},{8,10},{9,11},{10,... | collective-permute-start | bytes 393224 | tf_op jit(solution)/shard_map/ppermute | solution.py:321
  64.0 8.7 %collective-permute-start.9 = (bf16[1024,256]{1,0:T(8,128)(2,1)S(1)}, bf16[1024,256]{1,0:T(8,128)(2,1)S(1)}, u32[]{:S(2)}, u32[]{:S(2)}) collective-permute-start(bf16[1024,256]{1,0:T(8,128)(2,1)S(1)} %shard_map.40), channel_id=1, source_target_pairs={{0,1},{1,0},{2,3},{3,2},{4,5},{5,4},{6,7},{7,6},{8,9},{9,8},{10,11... | collective-permute-start | bytes 1572872 | tf_op jit(solution)/shard_map/ppermute | solution.py:324
  66.7 7.4 %collective-permute-start.19 = (bf16[768,256]{1,0:T(8,128)(2,1)S(1)}, bf16[768,256]{1,0:T(8,128)(2,1)S(1)}, u32[]{:S(2)}, u32[]{:S(2)}) collective-permute-start(bf16[768,256]{1,0:T(8,128)(2,1)S(1)} %shard_map.45), channel_id=1, source_target_pairs={{0,1},{1,0},{2,3},{3,2},{4,5},{5,4},{6,7},{7,6},{8,9},{9,8},{10,11... | collective-permute-start | bytes 1179656 | tf_op jit(solution)/shard_map/ppermute | solution.py:324
  66.8 5.9 %collective-permute-start.18 = (bf16[256,256]{1,0:T(8,128)(2,1)S(1)}, bf16[256,256]{1,0:T(8,128)(2,1)S(1)}, u32[]{:S(2)}, u32[]{:S(2)}) collective-permute-start(bf16[256,256]{1,0:T(8,128)(2,1)S(1)} %collective-permute-done.17.refs_2_.refs_3_), channel_id=1, source_target_pairs={{0,6},{1,7},{2,0},{3,1},{4,2},{5,3},{6,4},{7,5},{8,14},{9,15},{10,... | collective-permute-start | bytes 393224 | tf_op jit(solution)/shard_map/ppermute | solution.py:321
  72.7 1.3 %collective-permute-start.20 = (bf16[256,256]{1,0:T(8,128)(2,1)S(1)}, bf16[256,256]{1,0:T(8,128)(2,1)S(1)}, u32[]{:S(2)}, u32[]{:S(2)}) collective-permute-start(bf16[256,256]{1,0:T(8,128)(2,1)S(1)} %collective-permute-done.18.refs_4_), channel_id=1, source_target_pairs={{0,1},{1,0},{2,3},{3,2},{4,5},{5,4},{6,7},{7,6},{8,9},{9,8},{10,11... | collective-permute-start | bytes 393224 | tf_op jit(solution)/shard_map/ppermute | solution.py:324

commit v5 on v3

--- a/solution.py
+++ b/solution.py
@@ -127,18 +127,43 @@
     )(*pieces)
 
 
+def stacked(parts):
+    rows = parts[0].shape[0]
+
+    def stack(*refs):
+        for n, ref in enumerate(refs[:-1]):
+            refs[-1][n * rows : (n + 1) * rows, :] = ref[...]
+
+    return pl.pallas_call(
+        stack,
+        in_specs=[pl.BlockSpec(memory_space=pltpu.VMEM)] * len(parts),
+        out_specs=pl.BlockSpec(memory_space=pltpu.VMEM),
+        out_shape=jax.ShapeDtypeStruct((len(parts) * rows, COLS), BF),
+        compiler_params=pltpu.CompilerParams(vmem_limit_bytes=32 * 2**20),
+        cost_estimate=pl.CostEstimate(
+            flops=0, bytes_accessed=4 * len(parts) * rows * COLS, transcendentals=0
+        ),
+    )(*parts)
+
+
 def tiles(where_ref, *refs):
     (out_ref, dots, squares), refs = refs[-3:], refs[:-3]
-    contract = (((0,), (0,)), ((), ()))
     highs, lows, parts = refs[:2], refs[2:4], refs[4:]
     high = [ref[...] for ref in highs]
     low = [ref[...] for ref in lows]
+    turned = [(high[half].T, low[half].T) for half in range(2)]
     for n in range(N_EX):
         dot, square = 0.0, 0.0
         for half in range(2):
-            part = high[half] if n == 0 else parts[half * (N_EX - 1) + n - 1][...]
-            for own in (high[half], low[half]):
-                dot += lax.dot_general(own, part, contract, preferred_element_type=F32)
+            *same, swapped = parts[half * SIDE : (half + 1) * SIDE]
+            if n == 0:
+                part = high[half]
+            elif n < SIDE:
+                part = same[n - 1][...]
+            else:
+                part = swapped[(n - SIDE) * QUARTER : (n - SIDE + 1) * QUARTER, :]
+            for own in turned[half]:
+                dot += jnp.dot(own, part, preferred_element_type=F32)
             wide = part.astype(F32)
             square += jnp.sum(wide * wide, axis=0, keepdims=True)
         for half in range(BLK_DEV):
@@ -265,7 +290,7 @@
         same = [around(high, d) for d in (1, 2, 3)]
         highs.append(high)
         lows.append(low)
-        others += [*same, *(swap(a) for a in (high, *same))]
+        others += [*same, swap(stacked([high, *same]))]
     sums = partial_tiles(where, highs, lows, others)
 
     across = lambda a: lax.all_to_all(a, "layer", 0, 0, tiled=True)

time: 108 us -> 107 us (level)
    ppermute x8 -> x2, starting transfers between devices: 1.54 us -> 0.17 us  [on_device(): swap = lambda a: lax.ppermute(a, 'ex', [(e, e ^ 1) for e in range(N_EX)])]
  transfers between devices with their start and end apart: 26 -> 20, of which waited for: 11 -> 9; matrix products, arithmetic and copies ran while one was open for 0% -> 0% of each run, Pallas kernels for 3% -> 3%
where the time goes in v5:
time: 107 us
  blocking collectives  36.4 us (34%)
  starting transfers between devices  35.9 us (34%)
  waiting for transfers between devices  24.3 us (23%)
  Pallas kernels  5.71 us (5%)
  local copies, waits for them, and re-layouts  3.42 us (3%)
  other arithmetic  1.38 us (1%)
    all_to_all x2, blocking collectives, on_device(): across = lambda a: lax.all_to_all(a, 'layer', 0, 0, tiled=True)  36.4 us
    ppermute x12, starting transfers between devices, along(): lax.ppermute(a, 'layer', [(n, y * SIDE + x) for n, (y, x) in enumerate(to)])  23.9 us
    ppermute x12, waiting for transfers between devices, along(): lax.ppermute(a, 'layer', [(n, y * SIDE + x) for n, (y, x) in enumerate(to)])  18.6 us
    ppermute x6, starting transfers between devices, on_device(): lax.ppermute(a, 'ex', [(e, (e + 2 * d) % N_EX) for e in range(N_EX)])  11.9 us
    ppermute x6, waiting for transfers between devices, on_device(): lax.ppermute(a, 'ex', [(e, (e + 2 * d) % N_EX) for e in range(N_EX)])  4.2 us
    unnamed x6, local copies, waits for them, and re-layouts  3.1 us
  transfers between devices with their start and end apart: 20, of which 9 were waited for; matrix products, arithmetic and copies ran while one was open for 0% of the time, Pallas kernels for 3%

profile of v5, /device:TPU:0, one launch (start us, length us, event | category | flops | bytes accessed | tf_op | source)
XLA Modules:
  0.0 107.2 jit_solution(4967810937644778123)
XLA Ops:
  0.0 0.1 pad_add_fusion.place_ref
  0.1 0.0 copy-start
  0.1 2.2 %copy-done = bf16[1,8192,256]{2,1,0:T(8,128)(2,1)S(1)} copy-done((bf16[1,8192,256]{2,1,0:T(8,128)(2,1)S(1)}, bf16[1,8192,256]{2,1,0:T(8,128)(2,1)}, u32[]{:S(2)}) %copy-start) | copy-done | bytes 4194328
  2.3 0.0 copy-start.1
  2.3 0.9 copy-done.1
  3.2 0.8 shard_map.37
  3.9 1.6 %collective-permute-start = (bf16[1056,256]{1,0:T(8,128)(2,1)S(1)}, bf16[1056,256]{1,0:T(8,128)(2,1)S(1)}, u32[]{:S(2)}, u32[]{:S(2)}) collective-permute-start(bf16[1056,256]{1,0:T(8,128)(2,1)S(1)} %get-tuple-element.26), channel_id=1, source_target_pairs={{0,8},{8,16},{16,24},{24,0},{32,40},{40,48},{48,56},{56,32},{64,72... | collective-permute-start | bytes 1622024 | tf_op jit(solution)/shard_map/ppermute | solution.py:275
  5.6 2.7 %collective-permute-start.1 = (bf16[1056,256]{1,0:T(8,128)(2,1)S(1)}, bf16[1056,256]{1,0:T(8,128)(2,1)S(1)}, u32[]{:S(2)}, u32[]{:S(2)}) collective-permute-start(bf16[1056,256]{1,0:T(8,128)(2,1)S(1)} %get-tuple-element.27), channel_id=1, source_target_pairs={{0,16},{8,24},{16,0},{24,8},{32,48},{40,56},{48,32},{56,40},{64,80... | collective-permute-start | bytes 1622024 | tf_op jit(solution)/shard_map/ppermute | solution.py:275
  8.3 1.4 %collective-permute-start.2 = (bf16[1056,256]{1,0:T(8,128)(2,1)S(1)}, bf16[1056,256]{1,0:T(8,128)(2,1)S(1)}, u32[]{:S(2)}, u32[]{:S(2)}) collective-permute-start(bf16[1056,256]{1,0:T(8,128)(2,1)S(1)} %get-tuple-element.28), channel_id=1, source_target_pairs={{0,24},{8,0},{16,8},{24,16},{32,56},{40,32},{48,40},{56,48},{64,88... | collective-permute-start | bytes 1622024 | tf_op jit(solution)/shard_map/ppermute | solution.py:275
  9.8 0.8 shard_map.40
  10.5 1.6 %collective-permute-start.6 = (bf16[1056,256]{1,0:T(8,128)(2,1)S(1)}, bf16[1056,256]{1,0:T(8,128)(2,1)S(1)}, u32[]{:S(2)}, u32[]{:S(2)}) collective-permute-start(bf16[1056,256]{1,0:T(8,128)(2,1)S(1)} %get-tuple-element.35), channel_id=1, source_target_pairs={{0,32},{8,40},{16,48},{24,56},{32,64},{40,72},{48,80},{56,88},{64,... | collective-permute-start | bytes 1622024 | tf_op jit(solution)/shard_map/ppermute | solution.py:275
  12.2 2.9 %collective-permute-start.7 = (bf16[1056,256]{1,0:T(8,128)(2,1)S(1)}, bf16[1056,256]{1,0:T(8,128)(2,1)S(1)}, u32[]{:S(2)}, u32[]{:S(2)}) collective-permute-start(bf16[1056,256]{1,0:T(8,128)(2,1)S(1)} %get-tuple-element.36), channel_id=1, source_target_pairs={{0,64},{8,72},{16,80},{24,88},{32,96},{40,104},{48,112},{56,120},{... | collective-permute-start | bytes 1622024 | tf_op jit(solution)/shard_map/ppermute | solution.py:275
  15.1 4.0 %collective-permute-done.refs_1_ = bf16[1056,256]{1,0:T(8,128)(2,1)S(1)} collective-permute-done((bf16[1056,256]{1,0:T(8,128)(2,1)S(1)}, bf16[1056,256]{1,0:T(8,128)(2,1)S(1)}, u32[]{:S(2)}, u32[]{:S(2)}) %collective-permute-start) | collective-permute-done | bytes 540704 | tf_op jit(solution)/shard_map/ppermute | solution.py:275
  19.1 3.4 %collective-permute-start.8 = (bf16[1056,256]{1,0:T(8,128)(2,1)S(1)}, bf16[1056,256]{1,0:T(8,128)(2,1)S(1)}, u32[]{:S(2)}, u32[]{:S(2)}) collective-permute-start(bf16[1056,256]{1,0:T(8,128)(2,1)S(1)} %get-tuple-element.37), channel_id=1, source_target_pairs={{0,96},{8,104},{16,112},{24,120},{32,0},{40,8},{48,16},{56,24},{64... | collective-permute-start | bytes 1622024 | tf_op jit(solution)/shard_map/ppermute | solution.py:275
  22.5 9.4 %collective-permute-done.1.refs_2_ = bf16[1056,256]{1,0:T(8,128)(2,1)S(1)} collective-permute-done((bf16[1056,256]{1,0:T(8,128)(2,1)S(1)}, bf16[1056,256]{1,0:T(8,128)(2,1)S(1)}, u32[]{:S(2)}, u32[]{:S(2)}) %collective-permute-start.1) | collective-permute-done | bytes 540704 | tf_op jit(solution)/shard_map/ppermute | solution.py:275
  31.9 0.0 collective-permute-done.2.refs_3_
  31.9 0.9 shard_map.38
  32.8 1.6 %collective-permute-start.3 = (f32[256,256]{1,0:T(8,128)S(1)}, f32[256,256]{1,0:T(8,128)S(1)}, u32[]{:S(2)}, u32[]{:S(2)}) collective-permute-start(f32[256,256]{1,0:T(8,128)S(1)} %get-tuple-element.30), channel_id=1, source_target_pairs={{0,32},{8,40},{16,48},{24,56},{32,64},{40,72},{48,80},{56,88},{64,... | collective-permute-start | bytes 786440 | tf_op jit(solution)/shard_map/ppermute | solution.py:275
  34.5 2.9 %collective-permute-start.4 = (f32[256,256]{1,0:T(8,128)S(1)}, f32[256,256]{1,0:T(8,128)S(1)}, u32[]{:S(2)}, u32[]{:S(2)}) collective-permute-start(f32[256,256]{1,0:T(8,128)S(1)} %get-tuple-element.31), channel_id=1, source_target_pairs={{0,64},{8,72},{16,80},{24,88},{32,96},{40,104},{48,112},{56,120},{... | collective-permute-start | bytes 786440 | tf_op jit(solution)/shard_map/ppermute | solution.py:275
  37.4 0.0 collective-permute-done.6.refs_1_
  37.4 1.3 %collective-permute-start.5 = (f32[256,256]{1,0:T(8,128)S(1)}, f32[256,256]{1,0:T(8,128)S(1)}, u32[]{:S(2)}, u32[]{:S(2)}) collective-permute-start(f32[256,256]{1,0:T(8,128)S(1)} %get-tuple-element.32), channel_id=1, source_target_pairs={{0,96},{8,104},{16,112},{24,120},{32,0},{40,8},{48,16},{56,24},{64... | collective-permute-start | bytes 786440 | tf_op jit(solution)/shard_map/ppermute | solution.py:275
  38.7 0.0 collective-permute-done.7.refs_2_
  38.7 0.0 collective-permute-done.8.refs_3_
  38.7 0.9 shard_map.41
  39.7 0.0 copy-start.2
  39.7 1.4 %collective-permute-start.9 = (f32[256,256]{1,0:T(8,128)S(1)}, f32[256,256]{1,0:T(8,128)S(1)}, u32[]{:S(2)}, u32[]{:S(2)}) collective-permute-start(f32[256,256]{1,0:T(8,128)S(1)} %get-tuple-element.39), channel_id=1, source_target_pairs={{0,8},{8,16},{16,24},{24,0},{32,40},{40,48},{48,56},{56,32},{64,72... | collective-permute-start | bytes 786440 | tf_op jit(solution)/shard_map/ppermute | solution.py:275
  41.1 2.4 %collective-permute-start.10 = (f32[256,256]{1,0:T(8,128)S(1)}, f32[256,256]{1,0:T(8,128)S(1)}, u32[]{:S(2)}, u32[]{:S(2)}) collective-permute-start(f32[256,256]{1,0:T(8,128)S(1)} %get-tuple-element.40), channel_id=1, source_target_pairs={{0,16},{8,24},{16,0},{24,8},{32,48},{40,56},{48,32},{56,40},{64,80... | collective-permute-start | bytes 786440 | tf_op jit(solution)/shard_map/ppermute | solution.py:275
  43.5 1.1 %collective-permute-done.3.refs_1_ = f32[256,256]{1,0:T(8,128)S(1)} collective-permute-done((f32[256,256]{1,0:T(8,128)S(1)}, f32[256,256]{1,0:T(8,128)S(1)}, u32[]{:S(2)}, u32[]{:S(2)}) %collective-permute-start.3) | collective-permute-done | bytes 262176 | tf_op jit(solution)/shard_map/ppermute | solution.py:275
  44.6 0.4 collective-permute-start.11
  45.0 4.0 %collective-permute-done.4.refs_2_ = f32[256,256]{1,0:T(8,128)S(1)} collective-permute-done((f32[256,256]{1,0:T(8,128)S(1)}, f32[256,256]{1,0:T(8,128)S(1)}, u32[]{:S(2)}, u32[]{:S(2)}) %collective-permute-start.4) | collective-permute-done | bytes 262176 | tf_op jit(solution)/shard_map/ppermute | solution.py:275
  49.1 0.0 collective-permute-done.5.refs_3_
  49.1 0.1 shard_map.39
  49.1 2.0 %collective-permute-start.12 = (bf16[256,256]{1,0:T(8,128)(2,1)S(1)}, bf16[256,256]{1,0:T(8,128)(2,1)S(1)}, u32[]{:S(2)}, u32[]{:S(2)}) collective-permute-start(bf16[256,256]{1,0:T(8,128)(2,1)S(1)} %get-tuple-element.33.refs_0_), channel_id=1, source_target_pairs={{0,2},{1,3},{2,4},{3,5},{4,6},{5,7},{6,0},{7,1},{8,10},{9,11},{10,... | collective-permute-start | bytes 393224 | tf_op jit(solution)/shard_map/ppermute | solution.py:280
  51.1 3.6 %collective-permute-start.13 = (bf16[256,256]{1,0:T(8,128)(2,1)S(1)}, bf16[256,256]{1,0:T(8,128)(2,1)S(1)}, u32[]{:S(2)}, u32[]{:S(2)}) collective-permute-start(bf16[256,256]{1,0:T(8,128)(2,1)S(1)} %get-tuple-element.33.refs_0_), channel_id=1, source_target_pairs={{0,4},{1,5},{2,6},{3,7},{4,0},{5,1},{6,2},{7,3},{8,12},{9,13},{10,... | collective-permute-start | bytes 393224 | tf_op jit(solution)/shard_map/ppermute | solution.py:280
  54.7 0.0 collective-permute-done.9.refs_1_
  54.7 1.0 collective-permute-start.14
  55.7 0.0 collective-permute-done.10.refs_2_
  55.7 0.0 collective-permute-done.11.refs_3_
  55.7 0.1 shard_map.42
  55.8 1.1 %collective-permute-start.16 = (bf16[256,256]{1,0:T(8,128)(2,1)S(1)}, bf16[256,256]{1,0:T(8,128)(2,1)S(1)}, u32[]{:S(2)}, u32[]{:S(2)}) collective-permute-start(bf16[256,256]{1,0:T(8,128)(2,1)S(1)} %get-tuple-element.42.refs_0_.refs_1_), channel_id=1, source_target_pairs={{0,2},{1,3},{2,4},{3,5},{4,6},{5,7},{6,0},{7,1},{8,10},{9,11},{10,... | collective-permute-start | bytes 393224 | tf_op jit(solution)/shard_map/ppermute | solution.py:280
  56.9 3.2 %collective-permute-start.17 = (bf16[256,256]{1,0:T(8,128)(2,1)S(1)}, bf16[256,256]{1,0:T(8,128)(2,1)S(1)}, u32[]{:S(2)}, u32[]{:S(2)}) collective-permute-start(bf16[256,256]{1,0:T(8,128)(2,1)S(1)} %get-tuple-element.42.refs_0_.refs_1_), channel_id=1, source_target_pairs={{0,4},{1,5},{2,6},{3,7},{4,0},{5,1},{6,2},{7,3},{8,12},{9,13},{10,... | collective-permute-start | bytes 393224 | tf_op jit(solution)/shard_map/ppermute | solution.py:280
  60.1 0.0 collective-permute-done.12.refs_1_.refs_4_
  60.1 1.0 collective-permute-start.18
  61.1 0.0 copy-done.2
  61.1 0.1 reshape.22
  61.2 0.0 collective-permute-done.13.refs_2_.refs_5_
  61.2 0.1 collective-permute-done.14.refs_3_.refs_6_
  61.4 0.1 collective-permute-start.15
  61.5 1.9 %collective-permute-done.16.refs_1_.refs_8_ = bf16[256,256]{1,0:T(8,128)(2,1)S(1)} collective-permute-done((bf16[256,256]{1,0:T(8,128)(2,1)S(1)}, bf16[256,256]{1,0:T(8,128)(2,1)S(1)}, u32[]{:S(2)}, u32[]{:S(2)}) %collective-permute-start.16) | collective-permute-done | bytes 131104 | tf_op jit(solution)/shard_map/ppermute | solution.py:280
  63.3 2.1 %collective-permute-done.17.refs_2_.refs_9_ = bf16[256,256]{1,0:T(8,128)(2,1)S(1)} collective-permute-done((bf16[256,256]{1,0:T(8,128)(2,1)S(1)}, bf16[256,256]{1,0:T(8,128)(2,1)S(1)}, u32[]{:S(2)}, u32[]{:S(2)}) %collective-permute-start.17) | collective-permute-done | bytes 131104 | tf_op jit(solution)/shard_map/ppermute | solution.py:280
  65.5 0.1 collective-permute-done.18.refs_3_.refs_10_
  65.6 0.1 collective-permute-start.19
  65.7 0.1 copy.11
  65.8 0.1 copy.10
  65.8 0.1 add_reduce_fusion
  65.9 0.1 reduce_sum.12
  66.0 0.0 collective-permute-done.15.refs_7_
  66.1 1.5 %collective-permute-done.19.refs_11_ = bf16[1024,256]{1,0:T(8,128)(2,1)S(1)} collective-permute-done((bf16[1024,256]{1,0:T(8,128)(2,1)S(1)}, bf16[1024,256]{1,0:T(8,128)(2,1)S(1)}, u32[]{:S(2)}, u32[]{:S(2)}) %collective-permute-start.19) | collective-permute-done | bytes 524320 | tf_op jit(solution)/shard_map/ppermute | solution.py:283
  67.6 1.9 %shard_map.45 = bf16[256,1536]{1,0:T(8,128)(2,1)S(1)} custom-call(s32[20]{0:T(128)S(1)} %fusion.1.where_ref, bf16[256,256]{1,0:T(8,128)(2,1)S(1)} %get-tuple-element.33.refs_0_, bf16[256,256]{1,0:T(8,128)(2,1)S(1)} %get-tuple-element.42.refs_0_.refs_1_, bf16[256,256]{1,0:T(8,128)(2,1)S(1)} %get-tuple-element.43.refs_2_, ...), custom_call_target="tpu_custom_call" | custom-call | flops 1073741824 | bytes 3145728 | tf_op jit(solution)/shard_map/pallas_call | solution.py:195
  69.5 20.8 %all_to_all.10.sums_ref = bf16[16,16,1536]{2,1,0:T(8,128)(2,1)S(1)} all-to-all(bf16[16,16,1536]{2,1,0:T(8,128)(2,1)S(1)} %bitcast.15), channel_id=1, replica_groups=mesh['layer'=16,'ex'=8] {'layer'}, dimensions={0} | all-to-all | bytes 1572864 | tf_op jit(solution)/shard_map/all_to_all | solution.py:296
  90.3 0.2 shard_map.46
  90.5 15.5 %all_to_all.11 = bf16[16,16,1280]{2,1,0:T(8,128)(2,1)S(1)} all-to-all(bf16[16,16,1280]{2,1,0:T(8,128)(2,1)S(1)} %shard_map.46), channel_id=1, replica_groups=mesh['layer'=16,'ex'=8] {'layer'}, dimensions={0} | all-to-all | bytes 1310720 | tf_op jit(solution)/shard_map/all_to_all | solution.py:296
  106.0 1.2 %bitcast_convert_fusion = f32[256,1280]{1,0:T(8,128)} fusion(bf16[16,16,1280]{2,1,0:T(8,128)(2,1)S(1)} %all_to_all.11), kind=kLoop, calls=%fused_computation | loop fusion | flops 327680 | bytes 1966080 | tf_op jit(solution)/shard_map/convert_element_type | solution.py:299
  (5 shorter events, 0.1 us)
Async XLA Ops:
  0.1 2.2 %copy-start = (bf16[1,8192,256]{2,1,0:T(8,128)(2,1)S(1)}, bf16[1,8192,256]{2,1,0:T(8,128)(2,1)}, u32[]{:S(2)}) copy-start(bf16[1,8192,256]{2,1,0:T(8,128)(2,1)} %param.3) | copy-start | bytes 12582916
  2.3 0.9 copy-start.1
  3.9 15.2 %collective-permute-start = (bf16[1056,256]{1,0:T(8,128)(2,1)S(1)}, bf16[1056,256]{1,0:T(8,128)(2,1)S(1)}, u32[]{:S(2)}, u32[]{:S(2)}) collective-permute-start(bf16[1056,256]{1,0:T(8,128)(2,1)S(1)} %get-tuple-element.26), channel_id=1, source_target_pairs={{0,8},{8,16},{16,24},{24,0},{32,40},{40,48},{48,56},{56,32},{64,72... | collective-permute-start | bytes 1622024 | tf_op jit(solution)/shard_map/ppermute | solution.py:275
  5.6 26.3 %collective-permute-start.1 = (bf16[1056,256]{1,0:T(8,128)(2,1)S(1)}, bf16[1056,256]{1,0:T(8,128)(2,1)S(1)}, u32[]{:S(2)}, u32[]{:S(2)}) collective-permute-start(bf16[1056,256]{1,0:T(8,128)(2,1)S(1)} %get-tuple-element.27), channel_id=1, source_target_pairs={{0,16},{8,24},{16,0},{24,8},{32,48},{40,56},{48,32},{56,40},{64,80... | collective-permute-start | bytes 1622024 | tf_op jit(solution)/shard_map/ppermute | solution.py:275
  8.3 23.6 %collective-permute-start.2 = (bf16[1056,256]{1,0:T(8,128)(2,1)S(1)}, bf16[1056,256]{1,0:T(8,128)(2,1)S(1)}, u32[]{:S(2)}, u32[]{:S(2)}) collective-permute-start(bf16[1056,256]{1,0:T(8,128)(2,1)S(1)} %get-tuple-element.28), channel_id=1, source_target_pairs={{0,24},{8,0},{16,8},{24,16},{32,56},{40,32},{48,40},{56,48},{64,88... | collective-permute-start | bytes 1622024 | tf_op jit(solution)/shard_map/ppermute | solution.py:275
  10.5 26.8 %collective-permute-start.6 = (bf16[1056,256]{1,0:T(8,128)(2,1)S(1)}, bf16[1056,256]{1,0:T(8,128)(2,1)S(1)}, u32[]{:S(2)}, u32[]{:S(2)}) collective-permute-start(bf16[1056,256]{1,0:T(8,128)(2,1)S(1)} %get-tuple-element.35), channel_id=1, source_target_pairs={{0,32},{8,40},{16,48},{24,56},{32,64},{40,72},{48,80},{56,88},{64,... | collective-permute-start | bytes 1622024 | tf_op jit(solution)/shard_map/ppermute | solution.py:275
  12.2 26.5 %collective-permute-start.7 = (bf16[1056,256]{1,0:T(8,128)(2,1)S(1)}, bf16[1056,256]{1,0:T(8,128)(2,1)S(1)}, u32[]{:S(2)}, u32[]{:S(2)}) collective-permute-start(bf16[1056,256]{1,0:T(8,128)(2,1)S(1)} %get-tuple-element.36), channel_id=1, source_target_pairs={{0,64},{8,72},{16,80},{24,88},{32,96},{40,104},{48,112},{56,120},{... | collective-permute-start | bytes 1622024 | tf_op jit(solution)/shard_map/ppermute | solution.py:275
  19.1 19.6 %collective-permute-start.8 = (bf16[1056,256]{1,0:T(8,128)(2,1)S(1)}, bf16[1056,256]{1,0:T(8,128)(2,1)S(1)}, u32[]{:S(2)}, u32[]{:S(2)}) collective-permute-start(bf16[1056,256]{1,0:T(8,128)(2,1)S(1)} %get-tuple-element.37), channel_id=1, source_target_pairs={{0,96},{8,104},{16,112},{24,120},{32,0},{40,8},{48,16},{56,24},{64... | collective-permute-start | bytes 1622024 | tf_op jit(solution)/shard_map/ppermute | solution.py:275
  32.8 11.8 %collective-permute-start.3 = (f32[256,256]{1,0:T(8,128)S(1)}, f32[256,256]{1,0:T(8,128)S(1)}, u32[]{:S(2)}, u32[]{:S(2)}) collective-permute-start(f32[256,256]{1,0:T(8,128)S(1)} %get-tuple-element.30), channel_id=1, source_target_pairs={{0,32},{8,40},{16,48},{24,56},{32,64},{40,72},{48,80},{56,88},{64,... | collective-permute-start | bytes 786440 | tf_op jit(solution)/shard_map/ppermute | solution.py:275
  34.5 14.6 %collective-permute-start.4 = (f32[256,256]{1,0:T(8,128)S(1)}, f32[256,256]{1,0:T(8,128)S(1)}, u32[]{:S(2)}, u32[]{:S(2)}) collective-permute-start(f32[256,256]{1,0:T(8,128)S(1)} %get-tuple-element.31), channel_id=1, source_target_pairs={{0,64},{8,72},{16,80},{24,88},{32,96},{40,104},{48,112},{56,120},{... | collective-permute-start | bytes 786440 | tf_op jit(solution)/shard_map/ppermute | solution.py:275
  37.4 11.7 %collective-permute-start.5 = (f32[256,256]{1,0:T(8,128)S(1)}, f32[256,256]{1,0:T(8,128)S(1)}, u32[]{:S(2)}, u32[]{:S(2)}) collective-permute-start(f32[256,256]{1,0:T(8,128)S(1)} %get-tuple-element.32), channel_id=1, source_target_pairs={{0,96},{8,104},{16,112},{24,120},{32,0},{40,8},{48,16},{56,24},{64... | collective-permute-start | bytes 786440 | tf_op jit(solution)/shard_map/ppermute | solution.py:275
  39.7 21.4 %copy-start.2 = (s32[80,3]{0,1:T(4,128)S(1)}, s32[80,3]{0,1:T(4,128)}, u32[]{:S(2)}) copy-start(s32[80,3]{0,1:T(4,128)} %param.5) | copy-start | bytes 2884
  39.7 15.0 %collective-permute-start.9 = (f32[256,256]{1,0:T(8,128)S(1)}, f32[256,256]{1,0:T(8,128)S(1)}, u32[]{:S(2)}, u32[]{:S(2)}) collective-permute-start(f32[256,256]{1,0:T(8,128)S(1)} %get-tuple-element.39), channel_id=1, source_target_pairs={{0,8},{8,16},{16,24},{24,0},{32,40},{40,48},{48,56},{56,32},{64,72... | collective-permute-start | bytes 786440 | tf_op jit(solution)/shard_map/ppermute | solution.py:275
  41.1 14.6 %collective-permute-start.10 = (f32[256,256]{1,0:T(8,128)S(1)}, f32[256,256]{1,0:T(8,128)S(1)}, u32[]{:S(2)}, u32[]{:S(2)}) collective-permute-start(f32[256,256]{1,0:T(8,128)S(1)} %get-tuple-element.40), channel_id=1, source_target_pairs={{0,16},{8,24},{16,0},{24,8},{32,48},{40,56},{48,32},{56,40},{64,80... | collective-permute-start | bytes 786440 | tf_op jit(solution)/shard_map/ppermute | solution.py:275
  44.6 11.1 %collective-permute-start.11 = (f32[256,256]{1,0:T(8,128)S(1)}, f32[256,256]{1,0:T(8,128)S(1)}, u32[]{:S(2)}, u32[]{:S(2)}) collective-permute-start(f32[256,256]{1,0:T(8,128)S(1)} %get-tuple-element.41), channel_id=1, source_target_pairs={{0,24},{8,0},{16,8},{24,16},{32,56},{40,32},{48,40},{56,48},{64,88... | collective-permute-start | bytes 786440 | tf_op jit(solution)/shard_map/ppermute | solution.py:275
  49.1 11.0 %collective-permute-start.12 = (bf16[256,256]{1,0:T(8,128)(2,1)S(1)}, bf16[256,256]{1,0:T(8,128)(2,1)S(1)}, u32[]{:S(2)}, u32[]{:S(2)}) collective-permute-start(bf16[256,256]{1,0:T(8,128)(2,1)S(1)} %get-tuple-element.33.refs_0_), channel_id=1, source_target_pairs={{0,2},{1,3},{2,4},{3,5},{4,6},{5,7},{6,0},{7,1},{8,10},{9,11},{10,... | collective-permute-start | bytes 393224 | tf_op jit(solution)/shard_map/ppermute | solution.py:280
  51.1 10.1 %collective-permute-start.13 = (bf16[256,256]{1,0:T(8,128)(2,1)S(1)}, bf16[256,256]{1,0:T(8,128)(2,1)S(1)}, u32[]{:S(2)}, u32[]{:S(2)}) collective-permute-start(bf16[256,256]{1,0:T(8,128)(2,1)S(1)} %get-tuple-element.33.refs_0_), channel_id=1, source_target_pairs={{0,4},{1,5},{2,6},{3,7},{4,0},{5,1},{6,2},{7,3},{8,12},{9,13},{10,... | collective-permute-start | bytes 393224 | tf_op jit(solution)/shard_map/ppermute | solution.py:280
  54.7 6.6 %collective-permute-start.14 = (bf16[256,256]{1,0:T(8,128)(2,1)S(1)}, bf16[256,256]{1,0:T(8,128)(2,1)S(1)}, u32[]{:S(2)}, u32[]{:S(2)}) collective-permute-start(bf16[256,256]{1,0:T(8,128)(2,1)S(1)} %get-tuple-element.33.refs_0_), channel_id=1, source_target_pairs={{0,6},{1,7},{2,0},{3,1},{4,2},{5,3},{6,4},{7,5},{8,14},{9,15},{10,... | collective-permute-start | bytes 393224 | tf_op jit(solution)/shard_map/ppermute | solution.py:280
  55.8 7.6 %collective-permute-start.16 = (bf16[256,256]{1,0:T(8,128)(2,1)S(1)}, bf16[256,256]{1,0:T(8,128)(2,1)S(1)}, u32[]{:S(2)}, u32[]{:S(2)}) collective-permute-start(bf16[256,256]{1,0:T(8,128)(2,1)S(1)} %get-tuple-element.42.refs_0_.refs_1_), channel_id=1, source_target_pairs={{0,2},{1,3},{2,4},{3,5},{4,6},{5,7},{6,0},{7,1},{8,10},{9,11},{10,... | collective-permute-start | bytes 393224 | tf_op jit(solution)/shard_map/ppermute | solution.py:280
  56.9 8.6 %collective-permute-start.17 = (bf16[256,256]{1,0:T(8,128)(2,1)S(1)}, bf16[256,256]{1,0:T(8,128)(2,1)S(1)}, u32[]{:S(2)}, u32[]{:S(2)}) collective-permute-start(bf16[256,256]{1,0:T(8,128)(2,1)S(1)} %get-tuple-element.42.refs_0_.refs_1_), channel_id=1, source_target_pairs={{0,4},{1,5},{2,6},{3,7},{4,0},{5,1},{6,2},{7,3},{8,12},{9,13},{10,... | collective-permute-start | bytes 393224 | tf_op jit(solution)/shard_map/ppermute | solution.py:280
  60.1 5.4 %collective-permute-start.18 = (bf16[256,256]{1,0:T(8,128)(2,1)S(1)}, bf16[256,256]{1,0:T(8,128)(2,1)S(1)}, u32[]{:S(2)}, u32[]{:S(2)}) collective-permute-start(bf16[256,256]{1,0:T(8,128)(2,1)S(1)} %get-tuple-element.42.refs_0_.refs_1_), channel_id=1, source_target_pairs={{0,6},{1,7},{2,0},{3,1},{4,2},{5,3},{6,4},{7,5},{8,14},{9,15},{10,... | collective-permute-start | bytes 393224 | tf_op jit(solution)/shard_map/ppermute | solution.py:280
  61.4 4.7 %collective-permute-start.15 = (bf16[1024,256]{1,0:T(8,128)(2,1)S(1)}, bf16[1024,256]{1,0:T(8,128)(2,1)S(1)}, u32[]{:S(2)}, u32[]{:S(2)}) collective-permute-start(bf16[1024,256]{1,0:T(8,128)(2,1)S(1)} %shard_map.43), channel_id=1, source_target_pairs={{0,1},{1,0},{2,3},{3,2},{4,5},{5,4},{6,7},{7,6},{8,9},{9,8},{10,11... | collective-permute-start | bytes 1572872 | tf_op jit(solution)/shard_map/ppermute | solution.py:283
  65.6 2.0 %collective-permute-start.19 = (bf16[1024,256]{1,0:T(8,128)(2,1)S(1)}, bf16[1024,256]{1,0:T(8,128)(2,1)S(1)}, u32[]{:S(2)}, u32[]{:S(2)}) collective-permute-start(bf16[1024,256]{1,0:T(8,128)(2,1)S(1)} %shard_map.44), channel_id=1, source_target_pairs={{0,1},{1,0},{2,3},{3,2},{4,5},{5,4},{6,7},{7,6},{8,9},{9,8},{10,11... | collective-permute-start | bytes 1572872 | tf_op jit(solution)/shard_map/ppermute | solution.py:283
